TPU v7x, 32 devices: a whole 2x2x4 slice. The times are simulated.
32 devices in a mesh: dp: 8 (over y, x, core), tensor: 4 (over z).
Axes of the slice: x: 2, y: 2, z: 4, core: 2. Of those that a mesh axis runs over, the one named last changes fastest.
Arguments:
- tokens: bfloat16 [8192, 2560], P(('dp', 'tensor')), may hold values from -6 to 6
- cotangent: bfloat16 [8192, 2560], P(('dp', 'tensor')), may hold values from -6 to 6
- lengths: int32 [8, 3], P('dp'), may hold values from 1 to 576, 1024 in all within a row
- seq_deal: int32 [256], replicated, may hold values from 0 to 255, as said below
- mixer_gain: bfloat16 [2560], P('dp'), may hold values from 0.25 to 1.75
- recur_weight: bfloat16 [2560, 2560], P('dp', 'tensor'), may hold values from -0.125 to 0.125
- gelu_weight: bfloat16 [2560, 2560], P('dp', 'tensor'), may hold values from -0.125 to 0.125
- kernel_taps: bfloat16 [4, 2560], P(None, ('tensor', 'dp')), may hold values from -3 to 3
- kernel_bias: bfloat16 [2560], P(('tensor', 'dp')), may hold values from -3 to 3
- decay_param: bfloat16 [2560], P(('tensor', 'dp')), may hold values from 0.5 to 6
- rate_bias: bfloat16 [2560], P(('tensor', 'dp')), may hold values from -4 to 4
- input_bias: bfloat16 [2560], P(('tensor', 'dp')), may hold values from -4 to 4
- rate_blocks: bfloat16 [10, 256, 256], P(None, None, 'dp'), may hold values from -0.375 to 0.375
- input_blocks: bfloat16 [10, 256, 256], P(None, None, 'dp'), may hold values from -0.375 to 0.375
- mixer_out: bfloat16 [2560, 2560], P('tensor', 'dp'), may hold values from -0.3125 to 0.3125
- feed_gain: bfloat16 [2560], P('dp'), may hold values from 0.25 to 1.75
- feed_gate: bfloat16 [2560, 7680], P('dp', 'tensor'), may hold values from -0.125 to 0.125
- feed_up: bfloat16 [2560, 7680], P('dp', 'tensor'), may hold values from -0.125 to 0.125
- feed_down: bfloat16 [7680, 2560], P('tensor', 'dp'), may hold values from -0.09375 to 0.09375
Outputs:
- block_out: bfloat16 [8192, 2560], P(('dp', 'tensor'))
- tokens_grad: bfloat16 [8192, 2560], P(('dp', 'tensor'))
- grad_mixer_gain: float32 [2560], P('dp')
- grad_recur_weight: float32 [2560, 2560], P('dp', 'tensor')
- grad_gelu_weight: float32 [2560, 2560], P('dp', 'tensor')
- grad_kernel_taps: float32 [4, 2560], P(None, ('tensor', 'dp'))
- grad_kernel_bias: float32 [2560], P(('tensor', 'dp'))
- grad_decay_param: float32 [2560], P(('tensor', 'dp'))
- grad_rate_bias: float32 [2560], P(('tensor', 'dp'))
- grad_input_bias: float32 [2560], P(('tensor', 'dp'))
- grad_rate_blocks: float32 [10, 256, 256], P(None, None, 'dp')
- grad_input_blocks: float32 [10, 256, 256], P(None, None, 'dp')
- grad_mixer_out: float32 [2560, 2560], P('tensor', 'dp')
- grad_feed_gain: float32 [2560], P('dp')
- grad_feed_gate: float32 [2560, 7680], P('dp', 'tensor')
- grad_feed_up: float32 [2560, 7680], P('dp', 'tensor')
- grad_feed_down: float32 [7680, 2560], P('tensor', 'dp')
Inputs may be any that keep to these rules, and one draw needn't show every extreme that they name: `seq_deal`: the pieces dealt to one device come one from each index of dp, from devices with the same index of tensor; the pieces that one device holds go to different indices of dp. `lengths`: each row sums to 1024 and its largest entry is 576.
All inputs are finite; a program needn't handle non-finite values.
Results may differ from a plain program's by a relative error of at most 0.02.
Values may be sent and summed in bfloat16 or wider, within the bound.
No kernel may reach another device: no remote copies, remote signals or barrier semaphores. Data moves between devices by JAX's collectives and lax.ppermute only.
A program may use at most 256 MiB of HBM per device.

v0:
```python
import jax
import jax.numpy as jnp
from jax import lax
from jax.sharding import PartitionSpec as P

norm_eps = 1e-06
scale_floor = 0.001


def smooth_gelu(values):
    return jax.nn.gelu(values, approximate=True)


def gated_gelu(gate_pre, up_pre):
    return smooth_gelu(gate_pre) * up_pre


def rms_norm(values, gain_vec):
    return (
        values * lax.rsqrt(jnp.mean(values * values, axis=-1, keepdims=True) + norm_eps) * gain_vec
    )


def positions(seq_lengths, row_total):
    ends = jnp.cumsum(seq_lengths)
    starts = ends - seq_lengths
    places = jnp.arange(row_total, dtype=jnp.int32)
    begins = jnp.max(jnp.where(starts[None, :] <= places[:, None], starts[None, :], 0), axis=1)
    return places - begins


def causal_conv(values, taps, tap_bias, offset):
    tap_count = taps.shape[0]
    padded = jnp.pad(values, ((tap_count - 1, 0), (0, 0)))
    running = tap_bias[None, :] + jnp.zeros_like(values)
    for shift_lag in range(tap_count):
        shifted = padded[tap_count - 1 - shift_lag : tap_count - 1 - shift_lag + values.shape[0]]
        running = (
            running
            + jnp.where((offset >= shift_lag)[:, None], shifted, 0.0) * taps[shift_lag][None, :]
        )
    return running


def decay_input(pre_rate, pre_input, conv_out, decay_param, offset):
    rate_gate = jax.nn.sigmoid(pre_rate)
    input_gate = jax.nn.sigmoid(pre_input)
    log_decay = -8.0 * rate_gate * jax.nn.softplus(-decay_param)[None, :]
    decay_rate = jnp.where((offset == 0)[:, None], 0.0, jnp.exp(log_decay))
    input_scale = jnp.sqrt(jnp.maximum(1.0 - decay_rate * decay_rate, scale_floor))
    return (decay_rate, input_scale * input_gate * conv_out)


def combine(earlier, latter):
    return (earlier[0] * latter[0], latter[0] * earlier[1] + latter[1])


def contract_rows(left, right):
    return lax.dot_general(
        left, right, (((0,), (0,)), ((), ())), preferred_element_type=jnp.float32
    )


def contract_cols(left, right):
    return lax.dot_general(
        left, right, (((1,), (1,)), ((), ())), preferred_element_type=jnp.float32
    )


def per_device(
    tokens,
    cotangent,
    lengths,
    seq_deal,
    mixer_gain,
    recur_weight,
    gelu_weight,
    kernel_taps,
    kernel_bias,
    decay_param,
    rate_bias,
    input_bias,
    rate_blocks,
    input_blocks,
    mixer_out,
    feed_gain,
    feed_gate,
    feed_up,
    feed_down,
):
    groups = lax.axis_size("dp")
    lanes = lax.axis_size("tensor")
    group_index = lax.axis_index("dp")
    tensor_index = lax.axis_index("tensor")
    device = group_index * lanes + tensor_index
    row_count = tokens.shape[0]
    piece_rows = row_count // groups
    model_width = tokens.shape[1]
    slot_ids = jnp.arange(groups, dtype=jnp.int32)
    own_ids = device * groups + slot_ids
    inverse = (
        jnp.zeros_like(seq_deal).at[seq_deal].set(jnp.arange(seq_deal.shape[0], dtype=jnp.int32))
    )
    target_group = inverse[own_ids] // groups // lanes
    source_group = seq_deal[own_ids] // groups // lanes
    send_order = jnp.sum(
        jnp.where(target_group[None, :] == slot_ids[:, None], slot_ids[None, :], 0), axis=1
    )
    back_order = jnp.sum(
        jnp.where(source_group[None, :] == slot_ids[:, None], slot_ids[None, :], 0), axis=1
    )

    def ordered_pieces(values_in, order_ids):
        return jnp.take(values_in.reshape(groups, piece_rows, model_width), order_ids, axis=0)

    moved_tokens, moved_cot = (
        lax.all_to_all(
            ordered_pieces(tokens, send_order), "dp", split_axis=0, concat_axis=0, tiled=True
        ),
        lax.all_to_all(
            ordered_pieces(cotangent, send_order), "dp", split_axis=0, concat_axis=0, tiled=True
        ),
    )
    x_rows = (
        jnp.take(moved_tokens, source_group, axis=0)
        .reshape(row_count, model_width)
        .astype(jnp.float32)
    )
    cot_rows = (
        jnp.take(moved_cot, source_group, axis=0)
        .reshape(row_count, model_width)
        .astype(jnp.float32)
    )
    (
        gain_first,
        weight_x,
        weight_y,
        taps_all,
        taps_bias,
        decay_vec,
        rate_vec,
        input_vec,
        blocks_rate,
        blocks_input,
        weight_out,
        gain_second,
        weight_gate,
        weight_up,
        weight_down,
    ) = (
        lax.all_gather(mixer_gain, "dp", axis=0, tiled=True),
        lax.all_gather(recur_weight, "dp", axis=0, tiled=True),
        lax.all_gather(gelu_weight, "dp", axis=0, tiled=True),
        lax.all_gather(kernel_taps, "dp", axis=1, tiled=True),
        lax.all_gather(kernel_bias, "dp", axis=0, tiled=True),
        lax.all_gather(decay_param, "dp", axis=0, tiled=True),
        lax.all_gather(rate_bias, "dp", axis=0, tiled=True),
        lax.all_gather(input_bias, "dp", axis=0, tiled=True),
        lax.all_gather(rate_blocks, "dp", axis=2, tiled=True),
        lax.all_gather(input_blocks, "dp", axis=2, tiled=True),
        lax.all_gather(mixer_out, "dp", axis=1, tiled=True),
        lax.all_gather(feed_gain, "dp", axis=0, tiled=True),
        lax.all_gather(feed_gate, "dp", axis=0, tiled=True),
        lax.all_gather(feed_up, "dp", axis=0, tiled=True),
        lax.all_gather(feed_down, "dp", axis=1, tiled=True),
    )
    group_rows = row_count * lanes
    offset = positions(lengths[0], group_rows)
    channels = weight_x.shape[1]
    head_count = blocks_rate.shape[0]
    block_width = blocks_rate.shape[1]
    lru_total = channels * lanes

    def gather_rows(values_in):
        return lax.all_gather(values_in, "tensor", axis=0, tiled=True)

    def sum_branch(term_fn):
        return lax.psum_scatter(
            term_fn(jnp.int32(0), lax.axis_size("tensor") * row_count),
            "tensor",
            scatter_dimension=0,
            tiled=True,
        )

    def sum_input(term_fn):
        return lax.psum_scatter(
            term_fn(jnp.int32(0), lax.axis_size("tensor") * row_count),
            "tensor",
            scatter_dimension=0,
            tiled=True,
        )

    gain_first_f = gain_first.astype(jnp.float32)
    normed_first_f, norm_first_pull = jax.vjp(rms_norm, x_rows, gain_first_f)
    normed_first_all = gather_rows(normed_first_f.astype(jnp.bfloat16))
    branch_y = jnp.dot(normed_first_all, weight_y, preferred_element_type=jnp.float32)
    branch_x = jnp.dot(normed_first_all, weight_x, preferred_element_type=jnp.float32)

    def conv_local(values, taps, tap_bias):
        return causal_conv(values, taps, tap_bias, offset)

    conv_value, conv_pull = jax.vjp(
        conv_local, branch_x, taps_all.astype(jnp.float32), taps_bias.astype(jnp.float32)
    )
    conv_low = conv_value.astype(jnp.bfloat16)
    full_conv = lax.all_to_all(
        conv_low.reshape(lanes, row_count, channels),
        "tensor",
        split_axis=0,
        concat_axis=2,
        tiled=True,
    )
    item_rows = full_conv.shape[1]
    heads_view = full_conv[0].reshape(item_rows, head_count, block_width)
    rate_part = jnp.einsum(
        "thi,hij->thj", heads_view, blocks_rate, preferred_element_type=jnp.float32
    ).reshape(1, item_rows, lru_total)
    input_part = jnp.einsum(
        "thi,hij->thj", heads_view, blocks_input, preferred_element_type=jnp.float32
    ).reshape(1, item_rows, lru_total)
    rate_back = lax.all_to_all(rate_part, "tensor", split_axis=2, concat_axis=0, tiled=True)
    input_back = lax.all_to_all(input_part, "tensor", split_axis=2, concat_axis=0, tiled=True)
    pre_rate = rate_back.reshape(group_rows, channels) + rate_vec.astype(jnp.float32)[None, :]
    pre_input = input_back.reshape(group_rows, channels) + input_vec.astype(jnp.float32)[None, :]

    def gates_local(rate_pre, input_pre, conv_in, decay_in):
        return decay_input(rate_pre, input_pre, conv_in, decay_in, offset)

    (decay_rate, driven), gates_pull = jax.vjp(
        gates_local,
        pre_rate,
        pre_input,
        conv_low.astype(jnp.float32),
        decay_vec.astype(jnp.float32),
    )
    _, lru_state = lax.associative_scan(combine, (decay_rate, driven))
    act_y, gelu_pull = jax.vjp(smooth_gelu, branch_y)
    mixed_out = (lru_state * act_y).astype(jnp.bfloat16)

    def mixer_term(row_start, row_span):
        return jnp.dot(mixed_out, weight_out, preferred_element_type=jnp.float32)

    middle = x_rows + sum_branch(mixer_term)
    gain_second_f = gain_second.astype(jnp.float32)
    normed_second_f, norm_second_pull = jax.vjp(rms_norm, middle, gain_second_f)
    normed_second_all = gather_rows(normed_second_f.astype(jnp.bfloat16))
    gate_pre = jnp.dot(normed_second_all, weight_gate, preferred_element_type=jnp.float32)
    up_pre = jnp.dot(normed_second_all, weight_up, preferred_element_type=jnp.float32)
    hidden_f, hidden_pull = jax.vjp(gated_gelu, gate_pre, up_pre)
    hidden = hidden_f.astype(jnp.bfloat16)

    def feed_term(row_start, row_span):
        return jnp.dot(hidden, weight_down, preferred_element_type=jnp.float32)

    block_rows = (middle + sum_branch(feed_term)).astype(jnp.bfloat16)
    grad_second_all = gather_rows(cot_rows.astype(jnp.bfloat16))
    grad_down = contract_rows(hidden, grad_second_all)
    grad_hidden = contract_cols(grad_second_all, weight_down)
    grad_gate_f, grad_up_f = hidden_pull(grad_hidden)
    grad_gate_low = grad_gate_f.astype(jnp.bfloat16)
    grad_up_low = grad_up_f.astype(jnp.bfloat16)
    grad_w_gate = contract_rows(normed_second_all, grad_gate_low)
    grad_w_up = contract_rows(normed_second_all, grad_up_low)

    def feed_input(row_start, row_span):
        return contract_cols(grad_gate_low, weight_gate) + contract_cols(grad_up_low, weight_up)

    grad_norm_second = sum_input(feed_input)
    grad_middle_part, grad_gain_second = norm_second_pull(grad_norm_second)
    grad_middle = cot_rows + grad_middle_part
    grad_first_all = gather_rows(grad_middle.astype(jnp.bfloat16))
    grad_w_out = contract_rows(mixed_out, grad_first_all)
    grad_mixed = contract_cols(grad_first_all, weight_out)
    grad_state = grad_mixed * act_y
    grad_y_low = gelu_pull(grad_mixed * lru_state)[0].astype(jnp.bfloat16)
    decay_next = jnp.concatenate([decay_rate[1:], jnp.zeros_like(decay_rate[:1])], axis=0)
    _, adjoint = lax.associative_scan(combine, (decay_next, grad_state), reverse=True)
    state_prev = jnp.concatenate([jnp.zeros_like(lru_state[:1]), lru_state[:-1]], axis=0)
    grad_rate_f, grad_input_f, grad_conv_direct, grad_decay = gates_pull(
        (adjoint * state_prev, adjoint)
    )
    grad_rate_low = grad_rate_f.astype(jnp.bfloat16)
    grad_input_low = grad_input_f.astype(jnp.bfloat16)
    pieces = (
        lax.all_to_all(
            grad_rate_low.reshape(lanes, row_count, channels),
            "tensor",
            split_axis=0,
            concat_axis=2,
            tiled=True,
        ),
        lax.all_to_all(
            grad_input_low.reshape(lanes, row_count, channels),
            "tensor",
            split_axis=0,
            concat_axis=2,
            tiled=True,
        ),
    )
    item_rows = pieces[0].shape[1]
    rate_view = pieces[0][0].reshape(item_rows, head_count, block_width)
    input_view = pieces[1][0].reshape(item_rows, head_count, block_width)
    through = jnp.einsum(
        "thj,hij->thi", rate_view, blocks_rate, preferred_element_type=jnp.float32
    ) + jnp.einsum("thj,hij->thi", input_view, blocks_input, preferred_element_type=jnp.float32)
    through_back = lax.all_to_all(
        through.reshape(1, item_rows, lru_total).astype(jnp.bfloat16),
        "tensor",
        split_axis=2,
        concat_axis=0,
        tiled=True,
    ).astype(jnp.float32)
    rate_full = pieces[0]
    input_full = pieces[1]
    grad_conv = grad_conv_direct + through_back.reshape(group_rows, channels)
    conv_heads = full_conv[0].reshape(row_count, head_count, block_width)
    grad_blocks_rate = jnp.einsum(
        "thi,thj->hij",
        conv_heads,
        rate_full[0].reshape(row_count, head_count, block_width),
        preferred_element_type=jnp.float32,
    )
    grad_blocks_input = jnp.einsum(
        "thi,thj->hij",
        conv_heads,
        input_full[0].reshape(row_count, head_count, block_width),
        preferred_element_type=jnp.float32,
    )
    grad_rate_vec = jnp.sum(grad_rate_low.astype(jnp.float32), axis=0)
    grad_input_vec = jnp.sum(grad_input_low.astype(jnp.float32), axis=0)
    grad_branch_x, grad_taps, grad_taps_bias = conv_pull(grad_conv)
    grad_x_low = grad_branch_x.astype(jnp.bfloat16)
    grad_w_x = contract_rows(normed_first_all, grad_x_low)
    grad_w_y = contract_rows(normed_first_all, grad_y_low)

    def first_input(row_start, row_span):
        return contract_cols(grad_x_low, weight_x) + contract_cols(grad_y_low, weight_y)

    grad_norm_first = sum_input(first_input)
    grad_tokens_part, grad_gain_first = norm_first_pull(grad_norm_first)
    grad_token_rows = (grad_middle + grad_tokens_part).astype(jnp.bfloat16)
    returned_out, returned_grad = (
        lax.all_to_all(
            ordered_pieces(block_rows, back_order), "dp", split_axis=0, concat_axis=0, tiled=True
        ),
        lax.all_to_all(
            ordered_pieces(grad_token_rows, back_order),
            "dp",
            split_axis=0,
            concat_axis=0,
            tiled=True,
        ),
    )
    block_out = jnp.take(returned_out, target_group, axis=0).reshape(row_count, model_width)
    tokens_grad = jnp.take(returned_grad, target_group, axis=0).reshape(row_count, model_width)
    shared = (grad_gain_first, grad_gain_second, grad_blocks_rate, grad_blocks_input)
    shared = (
        lax.psum(grad_gain_first.astype(jnp.bfloat16), "tensor").astype(jnp.float32),
        lax.psum(grad_gain_second.astype(jnp.bfloat16), "tensor").astype(jnp.float32),
        lax.psum(grad_blocks_rate.astype(jnp.bfloat16), "tensor").astype(jnp.float32),
        lax.psum(grad_blocks_input.astype(jnp.bfloat16), "tensor").astype(jnp.float32),
    )
    summed = (
        lax.psum_scatter(
            shared[0].astype(jnp.bfloat16), "dp", scatter_dimension=0, tiled=True
        ).astype(jnp.float32),
        lax.psum_scatter(
            shared[1].astype(jnp.bfloat16), "dp", scatter_dimension=0, tiled=True
        ).astype(jnp.float32),
        lax.psum_scatter(
            shared[2].astype(jnp.bfloat16), "dp", scatter_dimension=2, tiled=True
        ).astype(jnp.float32),
        lax.psum_scatter(
            shared[3].astype(jnp.bfloat16), "dp", scatter_dimension=2, tiled=True
        ).astype(jnp.float32),
        lax.psum_scatter(
            grad_w_x.astype(jnp.bfloat16), "dp", scatter_dimension=0, tiled=True
        ).astype(jnp.float32),
        lax.psum_scatter(
            grad_w_y.astype(jnp.bfloat16), "dp", scatter_dimension=0, tiled=True
        ).astype(jnp.float32),
        lax.psum_scatter(
            grad_taps.astype(jnp.bfloat16), "dp", scatter_dimension=1, tiled=True
        ).astype(jnp.float32),
        lax.psum_scatter(
            grad_taps_bias.astype(jnp.bfloat16), "dp", scatter_dimension=0, tiled=True
        ).astype(jnp.float32),
        lax.psum_scatter(
            grad_decay.astype(jnp.bfloat16), "dp", scatter_dimension=0, tiled=True
        ).astype(jnp.float32),
        lax.psum_scatter(
            grad_rate_vec.astype(jnp.bfloat16), "dp", scatter_dimension=0, tiled=True
        ).astype(jnp.float32),
        lax.psum_scatter(
            grad_input_vec.astype(jnp.bfloat16), "dp", scatter_dimension=0, tiled=True
        ).astype(jnp.float32),
        lax.psum_scatter(
            grad_w_out.astype(jnp.bfloat16), "dp", scatter_dimension=1, tiled=True
        ).astype(jnp.float32),
        lax.psum_scatter(
            grad_w_gate.astype(jnp.bfloat16), "dp", scatter_dimension=0, tiled=True
        ).astype(jnp.float32),
        lax.psum_scatter(
            grad_w_up.astype(jnp.bfloat16), "dp", scatter_dimension=0, tiled=True
        ).astype(jnp.float32),
        lax.psum_scatter(
            grad_down.astype(jnp.bfloat16), "dp", scatter_dimension=1, tiled=True
        ).astype(jnp.float32),
    )
    feed_parts = (summed[12], summed[13], summed[14])
    shared_parts = (summed[0], summed[1], summed[2], summed[3])
    return (
        block_out,
        tokens_grad,
        shared_parts[0],
        summed[4],
        summed[5],
        summed[6],
        summed[7],
        summed[8],
        summed[9],
        summed[10],
        shared_parts[2],
        shared_parts[3],
        summed[11],
        shared_parts[1],
        feed_parts[0],
        feed_parts[1],
        feed_parts[2],
    )


def solution(mesh):
    in_specs = (
        P(("dp", "tensor"), None),
        P(("dp", "tensor"), None),
        P("dp", None),
        P(),
        P("dp"),
        P("dp", "tensor"),
        P("dp", "tensor"),
        P(None, ("tensor", "dp")),
        P(("tensor", "dp")),
        P(("tensor", "dp")),
        P(("tensor", "dp")),
        P(("tensor", "dp")),
        P(None, None, "dp"),
        P(None, None, "dp"),
        P("tensor", "dp"),
        P("dp"),
        P("dp", "tensor"),
        P("dp", "tensor"),
        P("tensor", "dp"),
    )
    out_specs = (
        P(("dp", "tensor"), None),
        P(("dp", "tensor"), None),
        P("dp"),
        P("dp", "tensor"),
        P("dp", "tensor"),
        P(None, ("tensor", "dp")),
        P(("tensor", "dp")),
        P(("tensor", "dp")),
        P(("tensor", "dp")),
        P(("tensor", "dp")),
        P(None, None, "dp"),
        P(None, None, "dp"),
        P("tensor", "dp"),
        P("dp"),
        P("dp", "tensor"),
        P("dp", "tensor"),
        P("tensor", "dp"),
    )
    return jax.shard_map(
        per_device, mesh=mesh, in_specs=in_specs, out_specs=out_specs, check_vma=False
    )
```

profile of v0, /device:TPU:0, one launch (start us, length us, event | category | flops | bytes accessed | tf_op | source)
XLA Modules:
  0.0 2596.8 jit_solution(8369502734765483385)
XLA Ops:
  25.8 33.8 %all-reduce.64 = (bf16[2560]{0:T(1024)(128)(2,1)S(1)}, bf16[640]{0:T(1024)(128)(2,1)S(1)}, bf16[640]{0:T(1024)(128)(2,1)S(1)}, bf16[640]{0:T(1024)(128)(2,1)S(1)...) all-reduce(bf16[2560]{0:T(1024)(128)(2,1)S(1)} %dynamic-update-slic, ...), channel_id=1, replica_groups=mesh['dp'=8,'tensor'=4] {'dp'}, use_global_device_ids=true, to_apply=%add.52 | all-reduce | flops 7680 | bytes 30720
  73.1 88.0 %all-gather.14.cloned.1.call-done = bf16[1024,2560]{1,0:T(8,128)(2,1)} async-done(((bf16[256,2560]{1,0:T(8,128)(2,1)}), bf16[1024,2560]{1,0:T(8,128)(2,1)}) %all-gather.14.cloned.1.call-update) | async-done | bytes 5242896 | tf_op jit(solution)/shard_map/all_gather | solution.py:175
  186.1 22.9 all-to-all-done.1
  242.9 44.3 %all-to-all-done.2 = f32[1,256,2560]{1,0,2:T(1,128)} async-done(((f32[1,256,2560]{1,0,2:T(1,128)}), f32[1,256,2560]{1,0,2:T(1,128)}, u32[]{:S(2)}, u32[]{:S(2)}) %all-to-all-start.2) | async-done | bytes 2621472 | tf_op jit(solution)/shard_map/all_to_all | solution.py:221
  299.0 50.8 %all-to-all-done.3 = f32[1,256,2560]{1,0,2:T(1,128)S(1)} async-done(((f32[1,256,2560]{1,0,2:T(1,128)}), f32[1,256,2560]{1,0,2:T(1,128)S(1)}, u32[]{:S(2)}, u32[]{:S(2)}) %all-to-all-start.3) | async-done | bytes 2621472 | tf_op jit(solution)/shard_map/all_to_all | solution.py:222
  462.1 176.4 %reduce-scatter.16.cloned.1.call-done = f32[256,2560]{1,0:T(8,128)} async-done(((f32[1024,2560]{1,0:T(8,128)}), f32[256,2560]{1,0:T(8,128)}) %reduce-scatter.16.cloned.1.call-update) | async-done | bytes 2621456 | tf_op jit(solution)/shard_map/reduce_scatter | solution.py:178
  643.4 35.6 %all_to_all.104 = bf16[8,32,2560]{2,1,0:T(8,128)(2,1)} all-to-all(bf16[8,32,2560]{2,1,0:T(8,128)(2,1)} %get-tuple-element.131), channel_id=1, replica_groups=mesh['dp'=8,'tensor'=4] {'dp'}, dimensions={0} | all-to-all | bytes 2621440 | tf_op jit(solution)/shard_map/all_to_all | solution.py:120
  685.2 29.0 %all-gather.30.cloned.1.call-done = bf16[2560,1920]{1,0:T(8,128)(2,1)} async-done(((bf16[320,1920]{1,0:T(8,128)(2,1)}), bf16[2560,1920]{1,0:T(8,128)(2,1)}) %all-gather.30.cloned.1.call-update) | async-done | bytes 9830416 | tf_op jit(solution)/shard_map/all_gather | solution.py:164
  714.2 100.2 %all-gather.26.cloned.1.call-done = bf16[1024,2560]{1,0:T(8,128)(2,1)} async-done(((bf16[256,2560]{1,0:T(8,128)(2,1)}), bf16[1024,2560]{1,0:T(8,128)(2,1)}) %all-gather.26.cloned.1.call-update) | async-done | bytes 5242896 | tf_op jit(solution)/shard_map/all_gather | solution.py:175
  831.6 43.5 %all-gather.28.cloned.1.call-done = bf16[2560,1920]{1,0:T(8,128)(2,1)} async-done(((bf16[320,1920]{1,0:T(8,128)(2,1)}), bf16[2560,1920]{1,0:T(8,128)(2,1)}) %all-gather.28.cloned.1.call-update) | async-done | bytes 9830416 | tf_op jit(solution)/shard_map/all_gather | solution.py:163
  892.2 83.1 %all-gather.34.cloned.1.call-done = bf16[1024,2560]{1,0:T(8,128)(2,1)} async-done(((bf16[256,2560]{1,0:T(8,128)(2,1)}), bf16[1024,2560]{1,0:T(8,128)(2,1)}) %all-gather.34.cloned.1.call-update) | async-done | bytes 5242896 | tf_op jit(solution)/shard_map/all_gather | solution.py:175
  975.4 60.6 %all-gather.32.cloned.1.call-done = bf16[1920,2560]{0,1:T(8,128)(2,1)} async-done(((bf16[1920,320]{0,1:T(8,128)(2,1)}), bf16[1920,2560]{0,1:T(8,128)(2,1)}) %all-gather.32.cloned.1.call-update) | async-done | bytes 9830416 | tf_op jit(solution)/shard_map/all_gather | solution.py:165
  1036.0 27.0 %multiply_convert_fusion = (bf16[1024,1920]{1,0:T(8,128)(2,1)}, bf16[1024,1920]{1,0:T(8,128)(2,1)}, bf16[1024,1920]{1,0:T(8,128)(2,1)}) fusion(f32[1024,1920]{1,0:T(8,128)} %fusion.106, f32[1024,1920]{1,0:T(8,128)} %fusion.107, bf16[1024,2560]{1,0:T(8,128)(2,1)} %all-gather.34.cloned.1.call-done, bf16[1920,2560]{0,1:T(8,128)(2,1)} %all-gather.32.cloned.1.call-done), kind=kOutput, calls=%fused_computation.23 | convolution fusion | flops 10117447680 | bytes 42598400 | tf_op jit(solution)/shard_map/dot_general | solution.py:65
  1080.3 17.9 convolution_add_fusion
  1098.3 178.1 %reduce-scatter.20.cloned.1.call-done = f32[256,2560]{1,0:T(8,128)} async-done(((f32[1024,2560]{1,0:T(8,128)}), f32[256,2560]{1,0:T(8,128)}) %reduce-scatter.20.cloned.1.call-update) | async-done | bytes 2621456 | tf_op jit(solution)/shard_map/reduce_scatter | solution.py:186
  1333.1 48.3 %all-gather.36.cloned.1.call-done = bf16[1024,2560]{1,0:T(8,128)(2,1)} async-done(((bf16[256,2560]{1,0:T(8,128)(2,1)}), bf16[1024,2560]{1,0:T(8,128)(2,1)}) %all-gather.36.cloned.1.call-update) | async-done | bytes 5242896 | tf_op jit(solution)/shard_map/all_gather | solution.py:175
  1481.9 21.0 rev.2
  1524.1 29.4 %all-to-all-done.7 = bf16[4,256,640]{1,2,0:T(8,128)(2,1)} async-done(((bf16[4,256,640]{1,2,0:T(8,128)(2,1)}), bf16[4,256,640]{1,2,0:T(8,128)(2,1)}, u32[]{:S(2)}, u32[]{:S(2)}) %all-to-all-start.7) | async-done | bytes 1310752 | tf_op jit(solution)/shard_map/all_to_all | solution.py:292
  1561.2 27.6 %all-to-all-done.6 = bf16[4,256,640]{1,2,0:T(8,128)(2,1)} async-done(((bf16[4,256,640]{1,2,0:T(8,128)(2,1)}), bf16[4,256,640]{1,2,0:T(8,128)(2,1)}, u32[]{:S(2)}, u32[]{:S(2)}) %all-to-all-start.6) | async-done | bytes 1310752 | tf_op jit(solution)/shard_map/all_to_all | solution.py:285
  1636.2 27.4 %all-to-all-done.8 = bf16[4,2,81920]{2,1,0:T(2,128)(2,1)} async-done(((bf16[4,2,81920]{2,1,0:T(2,128)(2,1)}), bf16[4,2,81920]{2,1,0:T(2,128)(2,1)}, u32[]{:S(2)}, u32[]{:S(2)}) %all-to-all-start.8) | async-done | bytes 1310752 | tf_op jit(solution)/shard_map/all_to_all | solution.py:306
  1794.8 80.8 %reduce-scatter.22.cloned.1.call-done = f32[256,2560]{1,0:T(8,128)} async-done(((f32[1024,2560]{1,0:T(8,128)}), f32[256,2560]{1,0:T(8,128)}) %reduce-scatter.22.cloned.1.call-update) | async-done | bytes 2621456 | tf_op jit(solution)/shard_map/reduce_scatter | solution.py:186
  1878.6 178.2 %reduce-scatter.18.cloned.1.call-done = f32[256,2560]{1,0:T(8,128)} async-done(((f32[1024,2560]{1,0:T(8,128)}), f32[256,2560]{1,0:T(8,128)}) %reduce-scatter.18.cloned.1.call-update) | async-done | bytes 2621456 | tf_op jit(solution)/shard_map/reduce_scatter | solution.py:178
  2069.6 23.2 all_to_all.105
  2097.7 56.9 %reduce-scatter.34.cloned.1.call-done = bf16[1920,320]{0,1:T(8,128)(2,1)} async-done(((bf16[1920,2560]{0,1:T(8,128)(2,1)}), bf16[1920,320]{0,1:T(8,128)(2,1)}) %reduce-scatter.34.cloned.1.call-update) | async-done | bytes 1228816 | tf_op jit(solution)/shard_map/reduce_scatter | solution.py:406
  2157.6 78.9 %reduce-scatter.30.cloned.1.call-done = bf16[320,1920]{1,0:T(8,128)(2,1)} async-done(((bf16[2560,1920]{1,0:T(8,128)(2,1)}), bf16[320,1920]{1,0:T(8,128)(2,1)}) %reduce-scatter.30.cloned.1.call-update) | async-done | bytes 1228816 | tf_op jit(solution)/shard_map/reduce_scatter | solution.py:400
  2239.3 79.0 %reduce-scatter.32.cloned.1.call-done = bf16[320,1920]{1,0:T(8,128)(2,1)} async-done(((bf16[2560,1920]{1,0:T(8,128)(2,1)}), bf16[320,1920]{1,0:T(8,128)(2,1)}) %reduce-scatter.32.cloned.1.call-update) | async-done | bytes 1228816 | tf_op jit(solution)/shard_map/reduce_scatter | solution.py:403
  2321.2 32.5 %reduce-scatter.40.cloned.1.call-done = bf16[80,4]{1,0:T(8,128)(2,1)} async-done(((bf16[640,4]{1,0:T(8,128)(2,1)}), bf16[80,4]{1,0:T(8,128)(2,1)}) %reduce-scatter.40.cloned.1.call-update) | async-done | bytes 656
  2355.1 37.5 %all-reduce.69.cloned.1.call-done = (bf16[10,256,32]{1,2,0:T(8,128)(2,1)}, bf16[10,256,32]{1,2,0:T(8,128)(2,1)}) async-done(((bf16[10,256,32]{1,2,0:T(8,128)(2,1)}, bf16[10,256,32]{1,2,0:T(8,128)(2,1)}), (bf16[10,256,32]{1,2,0:T(8,128)(2,1)}, bf16[10,256,32]{1,2,0:T(8,128)(2,1)})) %all-reduce.69.cloned.1.call-update) | async-done | bytes 327696 | tf_op jit(solution)/shard_map/psum | solution.py:360
  2396.0 47.0 %reduce-scatter.28.cloned.1.call-done = bf16[640,320]{0,1:T(8,128)(2,1)} async-done(((bf16[640,2560]{0,1:T(8,128)(2,1)}), bf16[640,320]{0,1:T(8,128)(2,1)}) %reduce-scatter.28.cloned.1.call-update) | async-done | bytes 409616 | tf_op jit(solution)/shard_map/reduce_scatter | solution.py:397
  2444.9 48.8 %reduce-scatter.26.cloned.1.call-done = bf16[320,640]{1,0:T(8,128)(2,1)} async-done(((bf16[2560,640]{1,0:T(8,128)(2,1)}), bf16[320,640]{1,0:T(8,128)(2,1)}) %reduce-scatter.26.cloned.1.call-update) | async-done | bytes 409616 | tf_op jit(solution)/shard_map/reduce_scatter | solution.py:379
  2495.6 48.6 %reduce-scatter.24.cloned.1.call-done = bf16[320,640]{1,0:T(8,128)(2,1)} async-done(((bf16[2560,640]{1,0:T(8,128)(2,1)}), bf16[320,640]{1,0:T(8,128)(2,1)}) %reduce-scatter.24.cloned.1.call-update) | async-done | bytes 409616 | tf_op jit(solution)/shard_map/reduce_scatter | solution.py:376
  2546.3 23.1 all-reduce.63
  (648 shorter events, 698.0 us)
Async XLA Ops:
  7.2 65.9 %all-gather.16.cloned.1.call-start = ((), (), s32[]{:S(2)}) async-start(), calls=%async_computation.24 | async-start | bytes 3686400 | tf_op jit(solution)/shard_map/all_gather | solution.py:152
  16.4 43.3 %all-to-all-start = ((bf16[8,32,2560]{2,1,0:T(8,128)(2,1)}), bf16[8,32,2560]{2,1,0:T(8,128)(2,1)S(1)}, u32[]{:S(2)}, u32[]{:S(2)}) async-start(bf16[8,32,2560]{2,1,0:T(8,128)(2,1)} %get-tuple-element.132), calls=%async_computation | async-start | bytes 2621440 | tf_op jit(solution)/shard_map/all_to_all | solution.py:117
  21.8 139.4 %all-gather.14.cloned.1.call-start = ((), (), s32[]{:S(2)}) async-start(), calls=%async_computation.23 | async-start | bytes 6553600 | tf_op jit(solution)/shard_map/all_gather | solution.py:175
  62.5 123.6 %all-gather.18.cloned.1.call-start = ((), (), s32[]{:S(2)}) async-start(), calls=%async_computation.25 | async-start | bytes 1474560 | tf_op jit(solution)/shard_map/all_gather | solution.py:159
  177.2 51.5 %all-gather.20.cloned.1.call-start = ((), (), s32[]{:S(2)}) async-start(), calls=%async_computation.26 | async-start | bytes 1474560 | tf_op jit(solution)/shard_map/all_gather | solution.py:160
  223.6 63.6 %all-to-all-start.2 = ((f32[1,256,2560]{1,0,2:T(1,128)}), f32[1,256,2560]{1,0,2:T(1,128)}, u32[]{:S(2)}, u32[]{:S(2)}) async-start(f32[1,256,2560]{1,0,2:T(1,128)} %copy.88), calls=%async_computation.2 | async-start | bytes 5242880 | tf_op jit(solution)/shard_map/all_to_all | solution.py:221
  228.1 211.2 %all-gather.22.cloned.1.call-start = ((), (), s32[]{:S(2)}) async-start(), calls=%async_computation.27 | async-start | bytes 3686400 | tf_op jit(solution)/shard_map/all_gather | solution.py:153
  287.2 62.5 %all-to-all-start.3 = ((f32[1,256,2560]{1,0,2:T(1,128)}), f32[1,256,2560]{1,0,2:T(1,128)S(1)}, u32[]{:S(2)}, u32[]{:S(2)}) async-start(f32[1,256,2560]{1,0,2:T(1,128)} %copy.91), calls=%async_computation.3 | async-start | bytes 5242880 | tf_op jit(solution)/shard_map/all_to_all | solution.py:222
  290.9 159.9 %all-gather.24.cloned.1.call-start = ((), (), s32[]{:S(2)}) async-start(), calls=%async_computation.28 | async-start | bytes 3686400 | tf_op jit(solution)/shard_map/all_gather | solution.py:161
  291.5 347.0 %reduce-scatter.16.cloned.1.call-start = ((), (), s32[]{:S(2)}) async-start(), calls=%async_computation.29 | async-start | bytes 13107200 | tf_op jit(solution)/shard_map/reduce_scatter | solution.py:178
  461.3 252.9 %all-gather.30.cloned.1.call-start = ((), (), s32[]{:S(2)}) async-start(), calls=%async_computation.32 | async-start | bytes 11059200 | tf_op jit(solution)/shard_map/all_gather | solution.py:164
  462.1 352.4 %all-gather.26.cloned.1.call-start = ((), (), s32[]{:S(2)}) async-start(), calls=%async_computation.30 | async-start | bytes 6553600 | tf_op jit(solution)/shard_map/all_gather | solution.py:175
  642.8 232.3 %all-gather.28.cloned.1.call-start = ((), (), s32[]{:S(2)}) async-start(), calls=%async_computation.31 | async-start | bytes 11059200 | tf_op jit(solution)/shard_map/all_gather | solution.py:163
  643.4 332.0 %all-gather.34.cloned.1.call-start = ((), (), s32[]{:S(2)}) async-start(), calls=%async_computation.35 | async-start | bytes 6553600 | tf_op jit(solution)/shard_map/all_gather | solution.py:175
  684.6 351.4 %all-gather.32.cloned.1.call-start = ((), (), s32[]{:S(2)}) async-start(), calls=%async_computation.33 | async-start | bytes 11059200 | tf_op jit(solution)/shard_map/all_gather | solution.py:165
  685.2 591.2 %reduce-scatter.20.cloned.1.call-start = ((), (), s32[]{:S(2)}) async-start(), calls=%async_computation.36 | async-start | bytes 13107200 | tf_op jit(solution)/shard_map/reduce_scatter | solution.py:186
  1098.3 283.1 %all-gather.36.cloned.1.call-start = ((), (), s32[]{:S(2)}) async-start(), calls=%async_computation.37 | async-start | bytes 6553600 | tf_op jit(solution)/shard_map/all_gather | solution.py:175
  1517.4 36.2 %all-to-all-start.7 = ((bf16[4,256,640]{1,2,0:T(8,128)(2,1)}), bf16[4,256,640]{1,2,0:T(8,128)(2,1)}, u32[]{:S(2)}, u32[]{:S(2)}) async-start(bf16[4,256,640]{1,2,0:T(8,128)(2,1)} %copy.95), calls=%async_computation.10 | async-start | bytes 2621440 | tf_op jit(solution)/shard_map/all_to_all | solution.py:292
  1553.5 35.3 %all-to-all-start.6 = ((bf16[4,256,640]{1,2,0:T(8,128)(2,1)}), bf16[4,256,640]{1,2,0:T(8,128)(2,1)}, u32[]{:S(2)}, u32[]{:S(2)}) async-start(bf16[4,256,640]{1,2,0:T(8,128)(2,1)} %copy.93), calls=%async_computation.9 | async-start | bytes 2621440 | tf_op jit(solution)/shard_map/all_to_all | solution.py:285
  1557.8 209.0 %reduce-scatter.38.cloned.1.call-start = ((), (), s32[]{:S(2)}) async-start(), calls=%async_computation.46 | async-start | bytes 1474560 | tf_op jit(solution)/shard_map/reduce_scatter | solution.py:373
  1632.8 134.1 %reduce-scatter.36.cloned.1.call-start = ((), (), s32[]{:S(2)}) async-start(), calls=%async_computation.45 | async-start | bytes 1474560 | tf_op jit(solution)/shard_map/reduce_scatter | solution.py:370
  1636.2 239.4 %reduce-scatter.22.cloned.1.call-start = ((), (), s32[]{:S(2)}) async-start(), calls=%async_computation.38 | async-start | bytes 13107200 | tf_op jit(solution)/shard_map/reduce_scatter | solution.py:186
  1698.3 358.6 %reduce-scatter.18.cloned.1.call-start = ((), (), s32[]{:S(2)}) async-start(), calls=%async_computation.34 | async-start | bytes 13107200 | tf_op jit(solution)/shard_map/reduce_scatter | solution.py:178
  1715.7 439.0 %reduce-scatter.34.cloned.1.call-start = ((), (), s32[]{:S(2)}) async-start(), calls=%async_computation.44 | async-start | bytes 11059200 | tf_op jit(solution)/shard_map/reduce_scatter | solution.py:406
  1732.3 504.1 %reduce-scatter.30.cloned.1.call-start = ((), (), s32[]{:S(2)}) async-start(), calls=%async_computation.42 | async-start | bytes 11059200 | tf_op jit(solution)/shard_map/reduce_scatter | solution.py:400
  1748.9 569.4 %reduce-scatter.32.cloned.1.call-start = ((), (), s32[]{:S(2)}) async-start(), calls=%async_computation.43 | async-start | bytes 11059200 | tf_op jit(solution)/shard_map/reduce_scatter | solution.py:403
  1765.8 587.9 %reduce-scatter.40.cloned.1.call-start = ((), (), s32[]{:S(2)}) async-start(), calls=%async_computation.47 | async-start | bytes 184320
  1766.8 625.9 %all-reduce.69.cloned.1.call-start = ((), (), s32[]{:S(2)}) async-start(), calls=%async_computation.48 | async-start | bytes 655360 | tf_op jit(solution)/shard_map/psum | solution.py:360
  1767.5 675.4 %reduce-scatter.28.cloned.1.call-start = ((), (), s32[]{:S(2)}) async-start(), calls=%async_computation.41 | async-start | bytes 3686400 | tf_op jit(solution)/shard_map/reduce_scatter | solution.py:397
  1776.5 717.2 %reduce-scatter.26.cloned.1.call-start = ((), (), s32[]{:S(2)}) async-start(), calls=%async_computation.40 | async-start | bytes 3686400 | tf_op jit(solution)/shard_map/reduce_scatter | solution.py:379
  1785.4 758.9 %reduce-scatter.24.cloned.1.call-start = ((), (), s32[]{:S(2)}) async-start(), calls=%async_computation.39 | async-start | bytes 3686400 | tf_op jit(solution)/shard_map/reduce_scatter | solution.py:376
  2092.8 492.4 %all-to-all-start.4 = ((bf16[8,32,2560]{2,1,0:T(8,128)(2,1)}), bf16[8,32,2560]{2,1,0:T(8,128)(2,1)S(1)}, u32[]{:S(2)}, u32[]{:S(2)}) async-start(bf16[8,32,2560]{2,1,0:T(8,128)(2,1)} %get-tuple-element.130), calls=%async_computation.6 | async-start | bytes 2621440 | tf_op jit(solution)/shard_map/all_to_all | solution.py:343
  (100 other events, 9161.1 us)
Sparse Core Ops, SparseCore 0:
  9.9 42.9 all-gather.15
  62.6 98.4 all-gather.13
  163.1 22.9 all-gather.17
  187.8 24.5 all-gather.19
  230.6 34.1 all-gather.21
  293.3 34.2 all-gather.23
  461.4 177.0 reduce-scatter.15
  640.4 73.7 all-gather.29
  716.4 98.0 all-gather.25
  816.2 58.8 all-gather.27
  877.3 98.0 all-gather.33
  977.1 58.8 all-gather.31
  1098.4 177.9 reduce-scatter.19
  1282.3 99.1 all-gather.35
  1561.6 38.6 reduce-scatter.37
  1637.1 38.6 reduce-scatter.35
  1698.4 177.1 reduce-scatter.21
  1877.7 179.0 reduce-scatter.17
  2060.4 94.2 reduce-scatter.33
  2158.1 78.2 reduce-scatter.29
  2240.0 78.2 reduce-scatter.31
  2321.9 31.7 reduce-scatter.39
  2356.2 36.3 all-reduce.68
  2396.3 46.6 reduce-scatter.27
  2446.8 46.8 reduce-scatter.25
  2497.4 46.8 reduce-scatter.23
where the time goes:
time: 2610 us; the launch traced here: 2600 us
  waiting for transfers between devices  1710 us (66%)
  local copies, waits for them, and re-layouts  305 us (12%)
  matrix products  257 us (10%)
  blocking collectives  137 us (5%)
  other arithmetic  132 us (5%)
  starting transfers between devices  35 us (1%)
    reduce_scatter x2, waiting for transfers between devices, sum_branch(): lax.psum_scatter(term_fn(jnp.int32(0), lax.axis_size('tensor') * row_coun...  355 us
    all_gather x4, waiting for transfers between devices, gather_rows(): return lax.all_gather(values_in, 'tensor', axis=0, tiled=True)  320 us
    reduce_scatter x2, waiting for transfers between devices, sum_input(): lax.psum_scatter(term_fn(jnp.int32(0), lax.axis_size('tensor') * row_coun...  259 us
    slice x66, local copies, waits for them, and re-layouts, per_device(): lax.associative_scan(combine, (decay_next, grad_state), reverse=True)  101 us
    dot_general x6, matrix products, contract_cols(): lax.dot_general(left, right, (((1,), (1,)), ((), ())), preferred_element_...  85 us
    reduce_scatter x1, waiting for transfers between devices, per_device(): lax.psum_scatter(grad_w_up.astype(jnp.bfloat16), 'dp', scatter_dimension=...  79 us
    reduce_scatter x1, waiting for transfers between devices, per_device(): lax.psum_scatter(grad_w_gate.astype(jnp.bfloat16), 'dp', scatter_dimensio...  78.9 us
    dot_general x6, matrix products, contract_rows(): lax.dot_general(left, right, (((0,), (0,)), ((), ())), preferred_element_...  76 us
  transfers between devices with their start and end apart: 34, of which 26 were waited for; matrix products, arithmetic and copies ran while one was open for 18% of the time, Pallas kernels for 0%

commit v1 on v0

v1 whole, which is shorter than its diff:
```python
import functools

import jax
import jax.numpy as jnp
from jax import lax
from jax.experimental import pallas as pl
from jax.experimental.pallas import tpu as pltpu
from jax.sharding import PartitionSpec as P

norm_eps = 1e-06
scale_floor = 0.001
halo = 8
bf16 = jnp.bfloat16
f32 = jnp.float32
gelu_c = 0.7978845608028654
gelu_k = 0.044715


def gelu_both(x):
    sq = x * x
    th = jnp.tanh(gelu_c * x * (1.0 + gelu_k * sq))
    half = 0.5 * (1.0 + th)
    return x * half, half + 0.5 * x * (1.0 - th * th) * gelu_c * (1.0 + 3.0 * gelu_k * sq)


def inv_rms(x):
    return lax.rsqrt(jnp.mean(x * x, axis=-1, keepdims=True) + norm_eps)


def norm_back(x, gain, grad):
    r = inv_rms(x)
    v = gain * grad
    dx = r * v - x * (r * r * r) * jnp.mean(x * v, axis=-1, keepdims=True)
    return dx, jnp.sum(grad * x * r, axis=0)


def mm(a, b):
    return jnp.dot(a, b, preferred_element_type=f32)


def mm_nt(a, b):
    return lax.dot_general(a, b, (((1,), (1,)), ((), ())), preferred_element_type=f32)


def mm_tn(a, b):
    return lax.dot_general(a, b, (((0,), (0,)), ((), ())), preferred_element_type=f32)


roomy = pltpu.CompilerParams(vmem_limit_bytes=56 * 1024 * 1024)


def cost(microseconds):
    return pl.CostEstimate(flops=int(microseconds * 1.15e9), bytes_accessed=1024, transcendentals=0)


def tile_of(total, most):
    for tile in range(most - most % 128, 0, -128):
        if total % tile == 0:
            return tile
    return total


def _pick_kernel(order_ref, x_ref, o_ref):
    for i in range(o_ref.shape[0]):
        o_ref[i] = x_ref[order_ref[i]]


def pick_pieces(pieces, order):
    return pl.pallas_call(
        _pick_kernel,
        in_specs=[pl.BlockSpec(memory_space=pltpu.SMEM), pl.BlockSpec(memory_space=pltpu.VMEM)],
        out_specs=pl.BlockSpec(memory_space=pltpu.VMEM),
        out_shape=jax.ShapeDtypeStruct(pieces.shape, pieces.dtype),
        name="pick_pieces", cost_estimate=cost(2),
    )(order, pieces)


def _turn_kernel(from_ref, x_ref, o_ref):
    width = x_ref.shape[1]
    place = lax.broadcasted_iota(jnp.int32, (width, o_ref.shape[1]), 0)
    hot = jnp.where(place == from_ref[...], 1.0, 0.0).astype(bf16)
    o_ref[...] = mm(x_ref[...], hot).astype(bf16)


def turn_feats(x, from_feat):
    rows, width = x.shape
    tile = tile_of(width, 512)
    return pl.pallas_call(
        _turn_kernel,
        grid=(width // tile,),
        in_specs=[pl.BlockSpec((1, tile), lambda j: (0, j)), pl.BlockSpec((rows, width), lambda j: (0, 0))],
        out_specs=pl.BlockSpec((rows, tile), lambda j: (0, j)),
        out_shape=jax.ShapeDtypeStruct(x.shape, bf16),
        compiler_params=roomy,
        name="turn_feats", cost_estimate=cost(6),
    )(from_feat[None], x)


def unit(n):
    one = lax.broadcasted_iota(jnp.int32, (n, n), 0) == lax.broadcasted_iota(jnp.int32, (n, n), 1)
    return jnp.where(one, 1.0, 0.0).astype(bf16)


def _flip_kernel(x_ref, o_ref):
    o_ref[...] = mm_tn(x_ref[...], unit(x_ref.shape[0])).astype(bf16)


def flip_weight(x):
    rows, cols = x.shape
    tile = tile_of(rows, 640)
    return pl.pallas_call(
        _flip_kernel,
        grid=(rows // tile,),
        in_specs=[pl.BlockSpec((tile, cols), lambda j: (j, 0))],
        out_specs=pl.BlockSpec((cols, tile), lambda j: (0, j)),
        out_shape=jax.ShapeDtypeStruct((cols, rows), bf16),
        compiler_params=roomy,
        name="flip_weight", cost_estimate=cost(4),
    )(x)


def _join_kernel(own_ref, x_ref, y_ref, low_ref, high_ref, out_ref):
    extra, feats = own_ref.shape[0], own_ref.shape[1]
    half = feats // 2
    for e in range(extra):
        for q, ref in enumerate((own_ref, x_ref, y_ref)):
            out_ref[(4 * e + q) * feats : (4 * e + q + 1) * feats] = ref[e]
        at = (4 * e + 3) * feats
        out_ref[at : at + half] = low_ref[e]
        out_ref[at + half : at + feats] = high_ref[e]


def join_feats(own, from_x, from_y, low, high):
    extra, feats, cols = own.shape
    tile = tile_of(cols, 640)
    full = pl.BlockSpec((extra, feats, tile), lambda j: (0, 0, j))
    part = pl.BlockSpec((extra, feats // 2, tile), lambda j: (0, 0, j))
    rows = extra * 4 * feats
    return pl.pallas_call(
        _join_kernel,
        grid=(cols // tile,),
        in_specs=[full, full, full, part, part],
        out_specs=pl.BlockSpec((rows, tile), lambda j: (0, j)),
        out_shape=jax.ShapeDtypeStruct((rows, cols), bf16),
        compiler_params=roomy,
        name="join_feats", cost_estimate=cost(5.5),
    )(own, from_x, from_y, low, high)


def _join_lanes_kernel(own_ref, x_ref, y_ref, low_ref, high_ref, out_ref):
    extra, feats = own_ref.shape[0], own_ref.shape[2]
    half = feats // 2
    for e in range(extra):
        for q, ref in enumerate((own_ref, x_ref, y_ref)):
            out_ref[0, (4 * e + q) * feats : (4 * e + q + 1) * feats] = ref[e, 0]
        at = (4 * e + 3) * feats
        out_ref[0, at : at + half] = low_ref[e, 0]
        out_ref[0, at + half : at + feats] = high_ref[e, 0]


def join_lanes(own, from_x, from_y, low, high):
    extra, lanes, feats, chans = own.shape
    full = pl.BlockSpec((extra, 1, feats, chans), lambda k: (0, k, 0, 0))
    part = pl.BlockSpec((extra, 1, feats // 2, chans), lambda k: (0, k, 0, 0))
    rows = extra * 4 * feats
    return pl.pallas_call(
        _join_lanes_kernel,
        grid=(lanes,),
        in_specs=[full, full, full, part, part],
        out_specs=pl.BlockSpec((1, rows, chans), lambda k: (k, 0, 0)),
        out_shape=jax.ShapeDtypeStruct((lanes, rows, chans), bf16),
        compiler_params=roomy,
        name="join_lanes",
        cost_estimate=cost(5),
    )(own, from_x, from_y, low, high)


def chan_spec(rows, chans):
    if chans % 128 == 0:
        return pl.BlockSpec((rows, chans), lambda k: (0, k))
    return pl.BlockSpec((1, rows, chans), lambda k: (k, 0, 0))


def chan_in(x, chans):
    if chans % 128 == 0:
        return x
    return jnp.swapaxes(x.reshape(x.shape[0], -1, chans), 0, 1)


def chan_get(ref):
    return ref[...] if len(ref.shape) == 2 else ref[0]


def rows_into(a, weight):
    rows, width = a.shape
    lanes, half, chans = weight[0].shape
    flat = chans % 128 == 0

    def kernel(a_ref, own_ref, other_ref, out_ref):
        got = mm(a_ref[:, :half], own_ref[0]) + mm(a_ref[:, half:], other_ref[0])
        if flat:
            out_ref[...] = got
        else:
            out_ref[0] = got

    block = pl.BlockSpec((1, half, chans), lambda k: (k, 0, 0))
    out = pl.pallas_call(
        kernel,
        grid=(lanes,),
        in_specs=[pl.BlockSpec((rows, width), lambda k: (0, 0)), block, block],
        out_specs=chan_spec(rows, chans),
        out_shape=jax.ShapeDtypeStruct((rows, lanes * chans) if flat else (lanes, rows, chans), f32),
        compiler_params=roomy,
        name="rows_into",
        cost_estimate=cost(11),
    )(a, *weight)
    return out if flat else jnp.swapaxes(out, 0, 1).reshape(rows, lanes * chans)


def rows_back(terms):
    rows = terms[0][0].shape[0]
    lanes, half, chans = terms[0][1][0].shape
    pairs = len(terms)

    def kernel(*refs):
        out_ref = refs[-1]

        @pl.when(pl.program_id(0) == 0)
        def _():
            out_ref[...] = jnp.zeros_like(out_ref)

        for side in range(2):
            total = None
            for p in range(pairs):
                part = mm_nt(chan_get(refs[p]), refs[pairs + 2 * p + side][0])
                total = part if total is None else total + part
            cols = slice(side * half, (side + 1) * half)
            out_ref[:, cols] = out_ref[:, cols] + total

    block = pl.BlockSpec((1, half, chans), lambda k: (k, 0, 0))
    arrays = [chan_in(b, chans) for b, _ in terms]
    for _, weight in terms:
        arrays += list(weight)
    return pl.pallas_call(
        kernel,
        grid=(lanes,),
        in_specs=[chan_spec(rows, chans)] * pairs + [block] * (2 * pairs),
        out_specs=pl.BlockSpec((rows, 2 * half), lambda k: (0, 0)),
        out_shape=jax.ShapeDtypeStruct((rows, 2 * half), f32),
        compiler_params=roomy,
        name="rows_back",
        cost_estimate=cost(8 * pairs + 3),
    )(*arrays)


def lane_block(lane, k, lanes):
    return lax.rem(lane[0] - k + lanes, lanes)


def feed_pair(ns, cot_all, at, gate, up, down, lane, lanes):
    count = len(ns)
    rows, width = ns[0].shape
    half, hidden = gate[0].shape
    tile = tile_of(hidden, 640)

    def kernel(lane_ref, *refs):
        ns_refs, cot_refs = refs[:count], refs[count : 2 * count]
        weights = refs[2 * count : 2 * count + 6]
        hid_ref, gate_ref, up_ref, ns_all, cot_rows = refs[2 * count + 6 :]

        @pl.when(pl.program_id(0) == 0)
        def _():
            for i in range(count):
                ns_all[i * rows : (i + 1) * rows] = ns_refs[i][...]
                cot_rows[i * rows : (i + 1) * rows] = cot_refs[i][...]

        def times(a, i):
            return mm(a[:, :half], weights[i][...]) + mm(a[:, half:], weights[i + 1][...])

        act, slope = gelu_both(times(ns_all, 0))
        up_pre = times(ns_all, 2)
        hid_ref[...] = (act * up_pre).astype(bf16)
        grad = times(cot_rows, 4)
        gate_ref[...] = (grad * up_pre * slope).astype(bf16)
        up_ref[...] = (grad * act).astype(bf16)

    whole = pl.BlockSpec((rows, width), lambda j, lane: (0, 0))
    cots = [
        pl.BlockSpec((rows, width), functools.partial(lambda j, lane, k: (lane_block(lane, k, lanes), 0), k=at + i))
        for i in range(count)
    ]
    piece = pl.BlockSpec((half, tile), lambda j, lane: (0, j))
    out = pl.BlockSpec((count * rows, tile), lambda j, lane: (0, j))
    return pl.pallas_call(
        kernel,
        grid_spec=pltpu.PrefetchScalarGridSpec(
            num_scalar_prefetch=1,
            grid=(hidden // tile,),
            in_specs=[whole] * count + cots + [piece] * 6,
            out_specs=[out] * 3,
            scratch_shapes=[pltpu.VMEM((count * rows, width), bf16)] * 2,
        ),
        out_shape=[jax.ShapeDtypeStruct((count * rows, hidden), bf16)] * 3,
        compiler_params=roomy,
        name="feed_pair",
        cost_estimate=cost(27),
    )(lane, *ns, *([cot_all] * count), *gate, *up, *down)


def feed_back(terms, at, rows, adds, kind):
    half, hidden = terms[0][1][0].shape
    width = 2 * half
    tile = tile_of(half, 640)
    steps = half // tile
    pairs = len(terms)

    def kernel(*refs):
        out_ref = refs[-1]
        j = pl.program_id(0)
        for side in range(2):

            @pl.when((j < steps) if side == 0 else (j >= steps))
            def _():
                total = None
                for p in range(pairs):
                    part = mm_nt(refs[p][...], refs[pairs + 2 * p + side][...])
                    total = part if total is None else total + part
                for extra_ref in refs[3 * pairs : -1]:
                    total = total + extra_ref[...].astype(f32)
                out_ref[...] = total.astype(kind)

    specs = [pl.BlockSpec((rows, hidden), lambda j: (at, 0))] * pairs
    arrays = [b for b, _ in terms]
    for _, weight in terms:
        specs.append(pl.BlockSpec((tile, hidden), lambda j: (jnp.minimum(j, steps - 1), 0)))
        specs.append(pl.BlockSpec((tile, hidden), lambda j: (jnp.maximum(j - steps, 0), 0)))
        arrays += list(weight)
    specs += [pl.BlockSpec((rows, tile), lambda j: (0, j))] * len(adds)
    return pl.pallas_call(
        kernel,
        grid=(2 * steps,),
        in_specs=specs,
        out_specs=pl.BlockSpec((rows, tile), lambda j: (0, j)),
        out_shape=jax.ShapeDtypeStruct((rows, width), kind),
        compiler_params=roomy,
        name="feed_back",
        cost_estimate=cost(13),
    )(*arrays, *adds)


def feed_out(hidden, weight, lane, lanes):
    half, units = weight[0].shape
    width = 2 * half
    tile = tile_of(half, 640)
    steps = half // tile
    many = len(hidden)
    count = lanes // many
    rows = hidden[0].shape[0] // count

    def kernel(lane_ref, *refs):
        out_ref = refs[-1]
        j = pl.program_id(0)
        for side in range(2):

            @pl.when((j < steps) if side == 0 else (j >= steps))
            def _():
                for i in range(many):
                    got = mm_nt(refs[i][...], refs[many + side][...]).astype(bf16)
                    for c in range(count):
                        at = lane_block(lane_ref, i * count + c, lanes) * rows
                        out_ref[pl.ds(pl.multiple_of(at, rows), rows)] = got[c * rows : (c + 1) * rows]

    whole = pl.BlockSpec((count * rows, units), lambda j, lane: (0, 0))
    return pl.pallas_call(
        kernel,
        grid_spec=pltpu.PrefetchScalarGridSpec(
            num_scalar_prefetch=1,
            grid=(2 * steps,),
            in_specs=[whole] * many
            + [
                pl.BlockSpec((tile, units), lambda j, lane: (jnp.minimum(j, steps - 1), 0)),
                pl.BlockSpec((tile, units), lambda j, lane: (jnp.maximum(j - steps, 0), 0)),
            ],
            out_specs=pl.BlockSpec((lanes * rows, tile), lambda j, lane: (0, j)),
        ),
        out_shape=jax.ShapeDtypeStruct((lanes * rows, width), bf16),
        compiler_params=roomy,
        name="feed_out",
        cost_estimate=cost(18),
    )(lane, *hidden, *weight)


def weight_grad(lefts, rights, side, feats, lane, lanes, got=None, by_lane=False):
    specs, arrays = [], []
    for left in lefts:
        if isinstance(left, tuple):
            array, left_rows, k = left
            pick = functools.partial(lambda j, lane, k: (lane_block(lane, k, lanes), side), k=k)
        else:
            array, left_rows, pick = left, left.shape[0], lambda j, lane: (0, side)
        half = array.shape[1] // 2
        specs.append(pl.BlockSpec((left_rows, half), pick))
        arrays.append(array)
    count = len(lefts)
    right_rows, cols = rights[0].shape
    many = len(rights)
    tile = cols // lanes if by_lane else tile_of(cols, 640)
    extra = half // (4 * feats)
    part = feats // 2

    def kernel(lane_ref, *refs):
        left_refs, right_refs = refs[:count], refs[count : count + many]
        rest = refs[count + many :]
        if count > 1:
            all_ref, rest = rest[-1], rest[:-1]

            @pl.when(pl.program_id(0) == 0)
            def _():
                for i in range(count):
                    all_ref[i * left_rows : (i + 1) * left_rows] = left_refs[i][...]
        else:
            all_ref = left_refs[0]
        total = None
        for i in range(many):
            piece = mm_tn(all_ref[i * right_rows : (i + 1) * right_rows], chan_get(right_refs[i]))
            total = piece if total is None else total + piece
        if got is None:
            if by_lane:
                rest[0][0] = total.astype(bf16)
            else:
                rest[0][...] = total.astype(bf16)
            return
        total = (total + chan_get(rest[0]).astype(f32)).astype(bf16)
        cuts = (0, feats, 2 * feats, 3 * feats, 3 * feats + part, 4 * feats)
        for e in range(extra):
            base = 4 * feats * e
            for ref, a, b in zip(rest[1:], cuts[:-1], cuts[1:]):
                if by_lane:
                    ref[e, 0] = total[base + a : base + b]
                else:
                    ref[e] = total[base + a : base + b]

    flat = not by_lane or tile % 128 == 0
    if flat:
        right_spec = pl.BlockSpec((right_rows, tile), lambda j, lane: (0, j))
    else:
        right_spec = pl.BlockSpec((1, right_rows, tile), lambda j, lane: (j, 0, 0))
        rights = [chan_in(r, tile) for r in rights]
    if by_lane:
        sent, sent_shape = pl.BlockSpec((1, half, tile), lambda j, lane: (j, 0, 0)), (lanes, half, tile)
        block = lambda n: pl.BlockSpec((extra, 1, n, tile), lambda j, lane: (0, j, 0, 0))
        block_shape = lambda n: (extra, lanes, n, tile)
    else:
        sent, sent_shape = pl.BlockSpec((half, tile), lambda j, lane: (0, j)), (half, cols)
        block = lambda n: pl.BlockSpec((extra, n, tile), lambda j, lane: (0, 0, j))
        block_shape = lambda n: (extra, n, cols)
    sizes = (feats, feats, feats, part, part)
    specs += [right_spec] * many
    arrays += list(rights)
    if got is None:
        out_specs, out_shape = sent, jax.ShapeDtypeStruct(sent_shape, bf16)
    else:
        specs.append(sent)
        arrays.append(got)
        out_specs = [block(n) for n in sizes]
        out_shape = [jax.ShapeDtypeStruct(block_shape(n), bf16) for n in sizes]
    return pl.pallas_call(
        kernel,
        grid_spec=pltpu.PrefetchScalarGridSpec(
            num_scalar_prefetch=1,
            grid=(cols // tile,),
            in_specs=specs,
            out_specs=out_specs,
            scratch_shapes=[pltpu.VMEM((left_rows * count, half), bf16)] if count > 1 else [],
        ),
        out_shape=out_shape,
        compiler_params=roomy,
        name="weight_grad",
        cost_estimate=cost(10 if count > 1 else 7),
    )(lane, *arrays)


def scan_rows(a, b, reverse):
    rows = a.shape[0]
    place = lax.broadcasted_iota(jnp.int32, a.shape, 0)
    step = 1
    while step < rows:
        if reverse:
            inside = place < rows - step
            turn = rows - step
        else:
            inside = place >= step
            turn = step
        a_far = jnp.where(inside, pltpu.roll(a, turn, 0), 1.0)
        b_far = jnp.where(inside, pltpu.roll(b, turn, 0), 0.0)
        b = a * b_far + b
        a = a * a_far
        step *= 2
    return a, b


def gate_values(conv_low, rate_t, input_t, vec, first):
    q = jax.nn.sigmoid(mm_nt(conv_low, rate_t) + vec[5:6])
    p = jax.nn.sigmoid(mm_nt(conv_low, input_t) + vec[6:7])
    decay = jnp.where(first, 0.0, jnp.exp(-8.0 * q * vec[7:8]))
    room = 1.0 - decay * decay
    scale = jnp.sqrt(jnp.maximum(room, scale_floor))
    return q, p, decay, room, scale


def _mix_fwd_kernel(bx_ref, off_ref, vec_ref, rate_ref, input_ref, conv_ref, state_ref, prod_ref):
    rows = conv_ref.shape[0]
    off = off_ref[0:rows]
    vec = vec_ref[...]
    conv = jnp.broadcast_to(vec[4:5], state_ref.shape)
    for lag in range(4):
        conv = conv + jnp.where(off >= lag, bx_ref[halo - lag : halo - lag + rows], 0.0) * vec[lag : lag + 1]
    conv_low = conv.astype(bf16)
    conv_ref[...] = conv_low
    q, p, decay, room, scale = gate_values(conv_low, rate_ref[0], input_ref[0], vec, off == 0)
    driven = scale * p * conv_low.astype(f32)
    prod, state = scan_rows(decay, driven, False)
    state_ref[...] = state
    prod_ref[...] = prod


def mix_fwd(bx_ext, off_ext, vec, rate_t, input_t):
    heads, width, _ = rate_t.shape
    ext = bx_ext.shape[0]
    rows = ext - halo
    col = lambda h: (0, h)
    return pl.pallas_call(
        _mix_fwd_kernel,
        grid=(heads,),
        in_specs=[
            pl.BlockSpec((ext, width), col),
            pl.BlockSpec((ext, 1), lambda h: (0, 0)),
            pl.BlockSpec((16, width), col),
            pl.BlockSpec((1, width, width), lambda h: (h, 0, 0)),
            pl.BlockSpec((1, width, width), lambda h: (h, 0, 0)),
        ],
        out_specs=[pl.BlockSpec((rows, width), col)] * 3,
        out_shape=[
            jax.ShapeDtypeStruct((rows, heads * width), bf16),
            jax.ShapeDtypeStruct((rows, heads * width), f32),
            jax.ShapeDtypeStruct((rows, heads * width), f32),
        ],
        name="mix_fwd", cost_estimate=cost(12),
    )(bx_ext, off_ext, vec, rate_t, input_t)


def _mix_out_kernel(state_ref, prod_ref, enter_ref, by_ref, full_ref, mixed_ref):
    state = state_ref[...] + prod_ref[...] * enter_ref[0:1]
    full_ref[...] = state
    act, _ = gelu_both(by_ref[...])
    mixed_ref[...] = (state * act).astype(bf16)


def mix_out(state, prod, enter, by, width):
    rows, total = state.shape
    blk = pl.BlockSpec((rows, width), lambda h: (0, h))
    return pl.pallas_call(
        _mix_out_kernel,
        grid=(total // width,),
        in_specs=[blk, blk, pl.BlockSpec((8, width), lambda h: (0, h)), blk],
        out_specs=[blk, blk],
        out_shape=[jax.ShapeDtypeStruct((rows, total), f32), jax.ShapeDtypeStruct((rows, total), bf16)],
        name="mix_out", cost_estimate=cost(6),
    )(state, prod, enter, by)


def _mix_adj_kernel(gm_ref, by_ref, full_ref, conv_ref, off_ref, vec_ref, rate_ref, gy_ref, adj_ref, tail_ref, edge_ref):
    rows = conv_ref.shape[0]
    vec = vec_ref[...]
    off = off_ref[0:rows]
    q = jax.nn.sigmoid(mm_nt(conv_ref[...], rate_ref[0]) + vec[5:6])
    decay = jnp.where(off == 0, 0.0, jnp.exp(-8.0 * q * vec[7:8]))
    act, act_grad = gelu_both(by_ref[...])
    gm = gm_ref[...]
    gy_ref[...] = (gm * full_ref[...] * act_grad).astype(bf16)
    place = lax.broadcasted_iota(jnp.int32, decay.shape, 0)
    after = jnp.where(place == rows - 1, 1.0, pltpu.roll(decay, rows - 1, 0))
    tail, adj = scan_rows(after, gm * act, True)
    adj_ref[...] = adj
    tail_ref[...] = tail
    edge_ref[0:1] = decay[0:1] * adj[0:1]
    edge_ref[1:2] = decay[0:1] * tail[0:1]
    edge_ref[2:8] = jnp.zeros((6, decay.shape[1]), f32)


def mix_adj(gm, by, full, conv, off_ext, vec, rate_t):
    heads, width, _ = rate_t.shape
    rows, total = gm.shape
    blk = pl.BlockSpec((rows, width), lambda h: (0, h))
    return pl.pallas_call(
        _mix_adj_kernel,
        grid=(heads,),
        in_specs=[
            blk,
            blk,
            blk,
            blk,
            pl.BlockSpec((rows + halo, 1), lambda h: (0, 0)),
            pl.BlockSpec((16, width), lambda h: (0, h)),
            pl.BlockSpec((1, width, width), lambda h: (h, 0, 0)),
        ],
        out_specs=[blk, blk, blk, pl.BlockSpec((8, width), lambda h: (0, h))],
        out_shape=[
            jax.ShapeDtypeStruct((rows, total), bf16),
            jax.ShapeDtypeStruct((rows, total), f32),
            jax.ShapeDtypeStruct((rows, total), f32),
            jax.ShapeDtypeStruct((8, total), f32),
        ],
        name="mix_adj", cost_estimate=cost(13),
    )(gm, by, full, conv, off_ext, vec, rate_t)


def _mix_bwd_kernel(
    adj_ref, tail_ref, hand_ref, full_ref, enter_ref, conv_ref, off_ref, vec_ref, rate_ref, input_ref,
    gc_ref, drate_ref, dinput_ref, sums_ref,
):
    rows = conv_ref.shape[0]
    vec = vec_ref[...]
    off = off_ref[0:rows]
    conv_low = conv_ref[...]
    conv = conv_low.astype(f32)
    rate_t, input_t = rate_ref[0], input_ref[0]
    q, p, decay, room, scale = gate_values(conv_low, rate_t, input_t, vec, off == 0)
    adj = adj_ref[...] + tail_ref[...] * hand_ref[0:1]
    place = lax.broadcasted_iota(jnp.int32, adj.shape, 0)
    before = jnp.where(place == 0, enter_ref[0:1], pltpu.roll(full_ref[...], 1, 0))
    g_decay = adj * before - jnp.where(room > scale_floor, adj * p * conv * decay / scale, 0.0)
    g_log = g_decay * decay
    g_rate = (-8.0 * g_log * vec[7:8] * q * (1.0 - q)).astype(bf16)
    g_input = (adj * scale * conv * p * (1.0 - p)).astype(bf16)
    gc_ref[...] = adj * scale * p + mm(g_rate, rate_t) + mm(g_input, input_t)
    drate_ref[0] = mm_tn(g_rate, conv_low).astype(bf16)
    dinput_ref[0] = mm_tn(g_input, conv_low).astype(bf16)
    sums_ref[0:1] = jnp.sum(8.0 * g_log * q, axis=0, keepdims=True) * vec[8:9]
    sums_ref[1:2] = jnp.sum(g_rate.astype(f32), axis=0, keepdims=True)
    sums_ref[2:3] = jnp.sum(g_input.astype(f32), axis=0, keepdims=True)
    sums_ref[3:8] = jnp.zeros((5, adj.shape[1]), f32)


def mix_bwd(adj, tail, hand, full, enter, conv, off_ext, vec, rate_t, input_t):
    heads, width, _ = rate_t.shape
    rows, total = adj.shape
    col = lambda h: (0, h)
    blk = pl.BlockSpec((rows, width), col)
    row8 = pl.BlockSpec((8, width), col)
    square = pl.BlockSpec((1, width, width), lambda h: (h, 0, 0))
    return pl.pallas_call(
        _mix_bwd_kernel,
        grid=(heads,),
        in_specs=[
            blk, blk, row8, blk, row8, blk,
            pl.BlockSpec((rows + halo, 1), lambda h: (0, 0)),
            pl.BlockSpec((16, width), col),
            square, square,
        ],
        out_specs=[blk, square, square, row8],
        out_shape=[
            jax.ShapeDtypeStruct((rows, total), f32),
            jax.ShapeDtypeStruct((heads, width, width), bf16),
            jax.ShapeDtypeStruct((heads, width, width), bf16),
            jax.ShapeDtypeStruct((8, total), f32),
        ],
        name="mix_bwd", cost_estimate=cost(14),
    )(adj, tail, hand, full, enter, conv, off_ext, vec, rate_t, input_t)


def _conv_bwd_kernel(gc_ref, next_ref, bx_ref, off_ref, vec_ref, gx_ref, sums_ref, ext_ref):
    rows = gc_ref.shape[0]
    vec = vec_ref[...]
    gc = gc_ref[...]
    ext_ref[0:rows] = gc
    ext_ref[rows : rows + halo] = next_ref[...]
    off = off_ref[0:rows]
    gx = gc * vec[0:1]
    sums_ref[0:1] = jnp.sum(gc * bx_ref[halo : halo + rows], axis=0, keepdims=True)
    for lag in range(1, 4):
        gx = gx + jnp.where(off_ref[lag : lag + rows] >= lag, ext_ref[lag : lag + rows], 0.0) * vec[lag : lag + 1]
        term = jnp.where(off >= lag, gc * bx_ref[halo - lag : halo - lag + rows], 0.0)
        sums_ref[lag : lag + 1] = jnp.sum(term, axis=0, keepdims=True)
    sums_ref[4:5] = jnp.sum(gc, axis=0, keepdims=True)
    sums_ref[5:8] = jnp.zeros((3, gc.shape[1]), f32)
    gx_ref[...] = gx.astype(bf16)


def conv_bwd(gc, gc_next, bx_ext, off_ext, vec, width):
    rows, total = gc.shape
    col = lambda h: (0, h)
    return pl.pallas_call(
        _conv_bwd_kernel,
        grid=(total // width,),
        in_specs=[
            pl.BlockSpec((rows, width), col),
            pl.BlockSpec((halo, width), col),
            pl.BlockSpec((rows + halo, width), col),
            pl.BlockSpec((rows + halo, 1), lambda h: (0, 0)),
            pl.BlockSpec((16, width), col),
        ],
        out_specs=[pl.BlockSpec((rows, width), col), pl.BlockSpec((8, width), col)],
        out_shape=[jax.ShapeDtypeStruct((rows, total), bf16), jax.ShapeDtypeStruct((8, total), f32)],
        scratch_shapes=[pltpu.VMEM((rows + halo, width), f32)],
        name="conv_bwd", cost_estimate=cost(7),
    )(gc, gc_next, bx_ext, off_ext, vec)


def after(x, *deps):
    return lax.optimization_barrier((x, deps))[0]


def per_device(
    tokens, cotangent, lengths, seq_deal, mixer_gain, recur_weight, gelu_weight, kernel_taps, kernel_bias,
    decay_param, rate_bias, input_bias, rate_blocks, input_blocks, mixer_out, feed_gain, feed_gate, feed_up,
    feed_down,
):
    groups = lax.axis_size("dp")
    lanes = lax.axis_size("tensor")
    bits = groups.bit_length() - 1
    g = lax.axis_index("dp")
    t = lax.axis_index("tensor")
    lane = t[None].astype(jnp.int32)
    device = g * lanes + t
    rows, width = tokens.shape
    piece_rows = rows // groups
    feats = mixer_gain.shape[0]
    chans = recur_weight.shape[1]
    lru_total = chans * lanes
    head_width = rate_blocks.shape[1]
    wide = tile_of(lru_total, 640)

    def swap(x, bit):
        return lax.ppermute(x, "dp", [(i, i ^ (1 << bit)) for i in range(groups)])

    def up(x):
        return lax.ppermute(x, "tensor", [(i, (i + 1) % lanes) for i in range(lanes)])

    def shift(x, by):
        return lax.ppermute(x, "tensor", [(i, i + by) for i in range(lanes) if 0 <= i + by < lanes])

    def gather_outer(part, *deps):
        part = (after(part, *deps) if deps else part)[None]
        for bit in range(3, bits):
            part = jnp.concatenate([part, swap(part, bit)], axis=0)
        from_x, from_y = swap(part, 1), swap(part, 2)
        half = feats // 2
        low, high = swap(from_y[..., :half, :], 1), swap(from_x[..., half:, :], 2)
        return part, from_x, from_y, low, high

    def reduce_far(blocks):
        return swap(blocks[3], 1), swap(blocks[4], 2)

    def reduce_near(blocks, far):
        half = feats // 2
        to_x, to_y = blocks[1], blocks[2]
        y_low = to_y[..., :half, :].astype(f32) + far[0].astype(f32)
        to_y = jnp.concatenate([y_low.astype(bf16), to_y[..., half:, :]], axis=-2)
        x_high = to_x[..., half:, :].astype(f32) + far[1].astype(f32)
        to_x = jnp.concatenate([to_x[..., :half, :], x_high.astype(bf16)], axis=-2)
        return swap(to_x, 1), swap(to_y, 2)

    def reduce_end(blocks, near):
        total = blocks[0].astype(f32) + near[0].astype(f32) + near[1].astype(f32)
        for bit in reversed(range(3, bits)):
            keep = total.shape[0] // 2
            total = total[:keep] + swap(total[keep:].astype(bf16), bit).astype(f32)
        return total[0]

    feat_ids = jnp.arange(width, dtype=jnp.int32)
    block_ids, within = feat_ids // feats, feat_ids % feats
    rel_at = 2 * (block_ids % (groups // 2)) + block_ids // (groups // 2)
    from_in = (g ^ rel_at) * feats + within
    rel_of = g ^ block_ids
    from_out = ((rel_of & 1) * (groups // 2) + (rel_of >> 1)) * feats + within

    def vectors_out(x):
        lead = x.shape[0]
        y = jnp.moveaxis(x.reshape((lead,) + (2,) * bits + (feats,)), 1, bits)
        for bit in range(bits):
            y = jnp.where((g >> bit) & 1 == 1, jnp.flip(y, bits - bit), y)
        return y.reshape(lead, width)

    slots = jnp.arange(groups, dtype=jnp.int32)
    places = jnp.arange(seq_deal.shape[0], dtype=jnp.int32)
    own_ids = device * groups + slots
    place_of = jnp.sum(jnp.where(own_ids[:, None] == seq_deal[None, :], places[None, :], 0), axis=1)
    target = place_of // groups // lanes
    source = jnp.sum(jnp.where(own_ids[:, None] == places[None, :], seq_deal[None, :], 0), axis=1) // groups // lanes
    rel_group = slots ^ g
    send_order = jnp.sum(jnp.where(target[None, :] == rel_group[:, None], slots[None, :], 0), axis=1)
    back_order = jnp.sum(jnp.where(source[None, :] == rel_group[:, None], slots[None, :], 0), axis=1)

    def exchange(pieces, order):
        for bit in order:
            view = pieces.reshape((groups >> (bit + 1), 2, (1 << bit) * piece_rows, width))
            got = swap(view[:, 1], bit)
            pieces = jnp.stack([view[:, 0], got], axis=1)
        return pieces.reshape(groups, piece_rows, width)

    def deal(x, order):
        sent = pick_pieces(x.reshape(groups, piece_rows, width), send_order)
        return turn_feats(pick_pieces(exchange(sent, order), source ^ g).reshape(rows, width), from_in)

    def undeal(x, order):
        sent = pick_pieces(turn_feats(x, from_out).reshape(groups, piece_rows, width), back_order)
        return pick_pieces(exchange(sent, order), target ^ g).reshape(rows, width)

    x_first = [1, 2] + list(range(3, bits)) + [0]
    y_first = [2, 1] + list(range(3, bits)) + [0]

    row_place = t * rows + jnp.arange(rows + halo, dtype=jnp.int32)
    begins = jnp.zeros_like(row_place)
    start = jnp.int32(0)
    for s in range(lengths.shape[1]):
        begins = jnp.where(row_place >= start, start, begins)
        start = start + lengths[0, s]
    off_ext = jnp.where(row_place < lanes * rows, row_place - begins, -1)[:, None]

    chan_count = kernel_bias.shape[0]
    small = jnp.concatenate(
        [kernel_taps.reshape(-1), kernel_bias, rate_bias, input_bias, decay_param, mixer_gain, feed_gain]
    )
    small = jnp.pad(small, (0, -small.shape[0] % 128))[None, None]
    step = 1
    while step < lanes:
        got = lax.ppermute(small, "tensor", [(i, i ^ step) for i in range(lanes)])
        small = jnp.concatenate([small, got], axis=0)
        step *= 2
    small = small.reshape(1, lanes, -1)
    for bit in range(bits):
        small = jnp.concatenate([small, swap(small, bit)], axis=0)

    x_low = deal(tokens, x_first)
    x = x_low.astype(f32)
    cot_low = deal(cotangent, y_first)

    def over_lanes(w):
        return lax.all_gather(w, "tensor", axis=0)

    lanes_x = over_lanes(recur_weight)
    lanes_y = over_lanes(gelu_weight)
    blocks = jnp.stack([jnp.swapaxes(rate_blocks, 1, 2), jnp.swapaxes(input_blocks, 1, 2)])
    blocks = lax.all_gather(after(blocks, lanes_x), "dp", axis=2, tiled=True)
    rate_t, input_t = blocks[0], blocks[1]
    lanes_o = over_lanes(flip_weight(mixer_out))
    cot_all = lax.all_gather(after(cot_low, lanes_o), "tensor", axis=0, tiled=True)

    def with_other(own):
        return own, swap(own, 0)

    part_g = gather_outer(feed_gate)
    part_x = gather_outer(lanes_x)
    part_y = gather_outer(lanes_y, part_g[3:])
    wx = with_other(join_lanes(*part_x))
    part_o = gather_outer(lanes_o, part_x[3:], cot_low)
    wg = with_other(join_feats(*part_g))
    wy = with_other(join_lanes(*part_y))
    wo = with_other(join_lanes(*part_o))

    chan_ids = jnp.arange(lru_total, dtype=jnp.int32)
    chan_lane, chan_dp, chan_in = chan_ids // chans, chan_ids % chans // chan_count, chan_ids % chan_count
    from_chan = ((chan_dp ^ g) * lanes + (chan_lane ^ t)) * chan_count + chan_in
    from_gain = (g ^ rel_at ^ g) * feats + within
    small_cols = 8 * chan_count
    chan_part = small[:, :, :small_cols].reshape(groups, lanes, 8, chan_count)
    chan_part = jnp.moveaxis(chan_part, 2, 0).reshape(8, lru_total)
    gain_part = small[:, 0, small_cols : small_cols + 2 * feats].reshape(groups, 2, feats)
    gain_part = jnp.swapaxes(gain_part, 0, 1).reshape(2, width)
    chan_vec = turn_feats(jnp.pad(chan_part, ((0, 8), (0, 0))), from_chan).astype(f32)
    gains = turn_feats(jnp.pad(gain_part, ((0, 14), (0, 0))), from_gain).astype(f32)
    gain_first, gain_second = gains[0], gains[1]
    vec = jnp.concatenate(
        [
            chan_vec[:7],
            jax.nn.softplus(-chan_vec[7:8]),
            jax.nn.sigmoid(-chan_vec[7:8]),
            jnp.zeros((7, lru_total), f32),
        ],
        axis=0,
    )

    normed_low = (x * inv_rms(x) * gain_first[None]).astype(bf16)
    normed_ext = jnp.concatenate([up(normed_low[rows - halo :]), normed_low], axis=0)
    bx_ext = rows_into(normed_ext, wx)
    part_u = gather_outer(feed_up, part_y[3:], bx_ext)
    by = rows_into(normed_low, wy)
    conv_low, state_loc, prod_loc = mix_fwd(bx_ext, off_ext, vec, rate_t, input_t)
    part_d = gather_outer(flip_weight(feed_down), part_o[3:], state_loc)
    wu = with_other(join_feats(*part_u))
    wd = with_other(join_feats(*part_d))
    edge = jnp.concatenate([state_loc[rows - 1 :], prod_loc[rows - 1 :], jnp.zeros((6, lru_total), f32)], axis=0)

    def carry_in(edge, direction):
        total = jnp.zeros((1, lru_total), f32)
        factor = jnp.ones((1, lru_total), f32)
        for by_lanes in range(1, lanes):
            far = shift(edge, direction * by_lanes)
            total = total + factor * far[0:1]
            factor = factor * far[1:2]
        return jnp.broadcast_to(total, (8, lru_total))

    enter = carry_in(edge, 1)
    state, mixed = mix_out(state_loc, prod_loc, enter, by, wide)
    middle = x + rows_back([(mixed, wo)])
    ns_low = (middle * inv_rms(middle) * gain_second[None]).astype(bf16)
    ns_rows = [ns_low]
    for _ in range(lanes - 1):
        ns_rows.append(up(ns_rows[-1]))

    pair = 2
    hidden, g_gate, g_up = [], [], []
    total = None
    for at in range(0, lanes, pair):
        first = ns_rows[at] if total is None else after(ns_rows[at], total)
        h, gg, gu = feed_pair([first] + ns_rows[at + 1 : at + pair], cot_all, at, wg, wu, wd, lane, lanes)
        hidden.append(h)
        g_gate.append(gg)
        g_up.append(gu)
        if total is None:
            total = feed_back([(gg, wg), (gu, wu)], 1, rows, [], bf16)

    def other_half(lefts, rights, *deps, **kind):
        first = after(rights[0], *deps) if deps else rights[0]
        return weight_grad(lefts, [first] + rights[1:], 1, feats, lane, lanes, **kind)

    def own_half(lefts, rights, other, *deps, **kind):
        first = after(rights[0], *deps) if deps else rights[0]
        return weight_grad(lefts, [first] + rights[1:], 0, feats, lane, lanes, got=swap(other, 0), **kind)

    def second_part(k, total, *deps):
        terms = [(after(g_gate[k // pair], *deps) if deps else g_gate[k // pair], wg), (g_up[k // pair], wu)]
        return feed_back(terms, k % pair, rows, [] if total is None else [up(total)], f32 if k == 0 else bf16)

    cot_parts = [(cot_all, rows, k) for k in range(lanes)]
    for k in range(2, lanes - 2):
        total = second_part(k, total)
    total = second_part(lanes - 2, total)
    other_down = other_half(cot_parts, hidden, total)
    other_gate = other_half(ns_rows, g_gate, other_down)
    own_down = own_half(cot_parts, hidden, other_down, other_gate)
    far_down = reduce_far(own_down)
    own_gate = own_half(ns_rows, g_gate, other_gate, own_down)
    far_gate = reduce_far(own_gate)
    total = second_part(lanes - 1, total, own_gate, far_down)
    near_down = reduce_near(own_down, far_down)
    other_up = other_half(ns_rows, g_up, total)
    near_gate = reduce_near(own_gate, far_gate)
    own_up = own_half(ns_rows, g_up, other_up, far_gate)
    far_up = reduce_far([after(b, near_down) for b in own_up])
    g_second = second_part(0, total, own_up, near_down)
    near_up = reduce_near(own_up, far_up)

    g_mid_part, d_gain_second = norm_back(middle, gain_second[None], g_second)
    g_middle = cot_low.astype(f32) + g_mid_part
    g1 = g_middle.astype(bf16)

    def lane_sum(blocks):
        return lax.psum_scatter(blocks.astype(bf16), "tensor", scatter_dimension=0).astype(f32)

    by_lane = dict(by_lane=True)
    other_out = other_half([g1], [mixed], **by_lane)
    gm = rows_into(after(g1, other_out, near_gate), wo)
    own_out = own_half([g1], [mixed], other_out, gm, far_up, **by_lane)
    far_out = reduce_far(own_out)
    gy_low, adj_loc, tail, edge_back = mix_adj(after(gm, own_out), by, state, conv_low, off_ext, vec, rate_t)
    hand = carry_in(edge_back, -1)
    other_y = other_half([normed_low], [gy_low], near_up, **by_lane)
    near_out = reduce_near(own_out, far_out)
    feed_sum = feed_out([after(hidden[0], other_y, far_out)] + hidden[1:], wd, lane, lanes)
    feed_sum = lax.psum_scatter(feed_sum, "tensor", scatter_dimension=0, tiled=True)
    own_y = own_half([normed_low], [gy_low], other_y, **by_lane)
    far_y = reduce_far(own_y)
    g_conv, d_rate, d_input, sums_gate = mix_bwd(
        after(adj_loc, own_y), tail, hand, state, enter, conv_low, off_ext, vec, rate_t, input_t
    )
    gc_next = lax.ppermute(g_conv[:halo], "tensor", [(i, (i - 1) % lanes) for i in range(lanes)])
    gx_low, sums_conv = conv_bwd(g_conv, gc_next, bx_ext, off_ext, vec, wide)
    near_y = reduce_near(own_y, far_y)
    other_x = other_half([normed_low], [gx_low], near_out, **by_lane)
    g_first = rows_back([(after(gx_low, other_x), wx), (gy_low, wy)])
    own_x = own_half([normed_low], [gx_low], other_x, far_y, **by_lane)
    far_x = reduce_far(own_x)
    d_down = reduce_end(own_down, near_down)
    d_gate = reduce_end(own_gate, near_gate)
    d_up = reduce_end(own_up, near_up)
    d_out = lane_sum(reduce_end(own_out, near_out))
    near_x = reduce_near(own_x, far_x)
    d_y = lane_sum(reduce_end(own_y, near_y))
    d_x = lane_sum(reduce_end(own_x, near_x))
    g_tok_part, d_gain_first = norm_back(x, gain_first[None], g_first)
    tokens_grad = undeal((g_middle + g_tok_part).astype(bf16), y_first)
    block_out = undeal((middle + feed_sum.astype(f32)).astype(bf16), x_first)

    d_blocks = lax.psum_scatter(jnp.stack([d_rate, d_input]), "dp", scatter_dimension=2, tiled=True)
    d_blocks = jnp.swapaxes(lax.psum(d_blocks, "tensor"), 2, 3).astype(f32)
    d_gains = vectors_out(jnp.stack([d_gain_first, d_gain_second]))
    vectors = jnp.concatenate([sums_conv[:5], sums_gate[:3], d_gains, jnp.zeros((6, width), f32)], axis=0)
    for bit in range(bits):
        vectors = vectors + swap(vectors, bit)
    step = 1
    while step < lanes:
        vectors = vectors + lax.ppermute(vectors, "tensor", [(i, i ^ step) for i in range(lanes)])
        step *= 2
    chan_grad = lax.dynamic_slice_in_dim(vectors[:8], (t * groups + g) * chan_count, chan_count, axis=1)
    gain_grad = lax.dynamic_slice_in_dim(vectors[8:10], g * feats, feats, axis=1)

    return (
        block_out,
        tokens_grad,
        gain_grad[0],
        d_x,
        d_y,
        chan_grad[0:4],
        chan_grad[4],
        chan_grad[5],
        chan_grad[6],
        chan_grad[7],
        d_blocks[0],
        d_blocks[1],
        d_out.T,
        gain_grad[1],
        d_gate,
        d_up,
        d_down.T,
    )


def solution(mesh):
    rows = P(("dp", "tensor"), None)
    feat = P("dp")
    chan = P(("tensor", "dp"))
    taps = P(None, ("tensor", "dp"))
    into = P("dp", "tensor")
    back = P("tensor", "dp")
    blocks = P(None, None, "dp")
    in_specs = (
        rows, rows, P("dp", None), P(), feat, into, into, taps, chan, chan, chan, chan, blocks, blocks, back, feat,
        into, into, back,
    )
    out_specs = (
        rows, rows, feat, into, into, taps, chan, chan, chan, chan, blocks, blocks, back, feat, into, into, back,
    )
    return jax.shard_map(per_device, mesh=mesh, in_specs=in_specs, out_specs=out_specs, check_vma=False)
```

time: 2610 us -> 1200 us (0.46)
  waiting for transfers between devices: 1710 us -> 509 us
  Pallas kernels: 0 us -> 432 us
  matrix products: 257 us -> 0 us
  local copies, waits for them, and re-layouts: 305 us -> 54.2 us
  blocking collectives: 137 us -> 0 us
  starting transfers between devices: 35 us -> 100 us
  other arithmetic: 132 us -> 79 us
    reduce_scatter x12 -> x5, waiting for transfers between devices: 973 us -> 19.3 us  [the longest x3 11.6 us: lane_sum(): lax.psum_scatter(blocks.astype(bf16), 'tensor', scatter_dimension=0)]
    ppermute x0 -> x96, waiting for transfers between devices: none -> 488 us  [the longest x78 372 us: swap(): return lax.ppermute(x, 'dp', [(i, i ^ 1 << bit) for i in range(groups)])]
    all_gather x12 -> x5, waiting for transfers between devices: 461 us -> 0.04 us  [the longest x3 0.02 us: over_lanes(): return lax.all_gather(w, 'tensor', axis=0)]
    pallas_call x0 -> x51, Pallas kernels: none -> 432 us  [the longest x12 106 us: weight_grad(): pl.pallas_call(kernel, grid_spec=pltpu.PrefetchScalarGridSpec(num_scalar_...]
    dot_general x24 -> x0, matrix products: 257 us -> none  [the longest x6 85 us: contract_cols(): lax.dot_general(left, right, (((1,), (1,)), ((), ())), preferred_element_...]
    all_to_all x8 -> x0, waiting for transfers between devices: 202 us -> none  [the longest x1 50.8 us: per_device(): lax.all_to_all(input_part, 'tensor', split_axis=2, concat_axis=0, tiled=T...]
    slice x128 -> x45, local copies, waits for them, and re-layouts: 153 us -> 17.9 us  [the longest x12 6.03 us: gather_outer(): low, high = (swap(from_y[..., :half, :], 1), swap(from_x[..., half:, :], 2))]
    ppermute x0 -> x96, starting transfers between devices: none -> 99.9 us  [the longest x78 69.6 us: swap(): return lax.ppermute(x, 'dp', [(i, i ^ 1 << bit) for i in range(groups)])]
  transfers between devices with their start and end apart: 34 -> 107, of which waited for: 26 -> 50; matrix products, arithmetic and copies ran while one was open for 18% -> 9% of each run, Pallas kernels for 0% -> 30%
where the time goes in v1:
time: 1200 us; the launch traced here: 1190 us
  waiting for transfers between devices  509 us (42%)
  Pallas kernels  432 us (36%)
  starting transfers between devices  100 us (8%)
  other arithmetic  79 us (7%)
  local copies, waits for them, and re-layouts  54.2 us (5%)
  between operations  17.1 us (1%)
    ppermute x78, waiting for transfers between devices, swap(): return lax.ppermute(x, 'dp', [(i, i ^ 1 << bit) for i in range(groups)])  372 us
    pallas_call x12, Pallas kernels, weight_grad(): pl.pallas_call(kernel, grid_spec=pltpu.PrefetchScalarGridSpec(num_scalar_...  106 us
    ppermute x7, waiting for transfers between devices, up(): lax.ppermute(x, 'tensor', [(i, (i + 1) % lanes) for i in range(lanes)])  74.6 us
    ppermute x78, starting transfers between devices, swap(): return lax.ppermute(x, 'dp', [(i, i ^ 1 << bit) for i in range(groups)])  69.6 us
    pallas_call x4, Pallas kernels, feed_back(): pl.pallas_call(kernel, grid=(2 * steps,), in_specs=specs, out_specs=pl.Bl...  53.7 us
    pallas_call x2, Pallas kernels, feed_pair(): pl.pallas_call(kernel, grid_spec=pltpu.PrefetchScalarGridSpec(num_scalar_...  53.7 us
    pallas_call x6, Pallas kernels, turn_feats(): pl.pallas_call(_turn_kernel, grid=(width // tile,), in_specs=[pl.BlockSpe...  34 us
    pallas_call x3, Pallas kernels, rows_into(): pl.pallas_call(kernel, grid=(lanes,), in_specs=[pl.BlockSpec((rows, width...  28.4 us
  transfers between devices with their start and end apart: 107, of which 50 were waited for; matrix products, arithmetic and copies ran while one was open for 9% of the time, Pallas kernels for 30%

profile of v1, /device:TPU:0, one launch (start us, length us, event | category | flops | bytes accessed | tf_op | source)
XLA Modules:
  0.0 1191.7 jit_solution(5627873628625363243)
XLA Ops:
  88.7 21.3 %collective-permute-done.10.y_ref = bf16[1,4,320,640]{3,2,1,0:T(8,128)(2,1)S(1)} collective-permute-done((bf16[1,4,320,640]{3,2,1,0:T(8,128)(2,1)}, bf16[1,4,320,640]{3,2,1,0:T(8,128)(2,1)S(1)}, u32[]{:S(2)}, u32[]{:S(2)}) %collective-permute-start.10) | collective-permute-done | bytes 1638432 | tf_op jit(solution)/shard_map/ppermute | solution.py:735
  110.1 11.2 collective-permute-done.9.x_ref
  137.8 14.7 %collective-permute-done.11.low_ref = bf16[1,4,160,640]{3,2,1,0:T(8,128)(2,1)} collective-permute-done((bf16[1,4,160,640]{3,2,1,0:T(8,128)(2,1)S(1)}, bf16[1,4,160,640]{3,2,1,0:T(8,128)(2,1)}, u32[]{:S(2)}, u32[]{:S(2)}) %collective-permute-start.11) | collective-permute-done | bytes 819232 | tf_op jit(solution)/shard_map/ppermute | solution.py:735
  180.1 16.7 %collective-permute-done.22.y_ref = bf16[1,4,320,640]{3,2,1,0:T(8,128)(2,1)} collective-permute-done((bf16[1,4,320,640]{3,2,1,0:T(8,128)(2,1)}, bf16[1,4,320,640]{3,2,1,0:T(8,128)(2,1)}, u32[]{:S(2)}, u32[]{:S(2)}) %collective-permute-start.22) | collective-permute-done | bytes 1638432 | tf_op jit(solution)/shard_map/ppermute | solution.py:735
  238.8 13.1 %collective-permute-done.30.y_ref = bf16[1,4,320,640]{3,2,1,0:T(8,128)(2,1)S(1)} collective-permute-done((bf16[1,4,320,640]{3,2,1,0:T(8,128)(2,1)}, bf16[1,4,320,640]{3,2,1,0:T(8,128)(2,1)S(1)}, u32[]{:S(2)}, u32[]{:S(2)}) %collective-permute-start.30) | collective-permute-done | bytes 1638432 | tf_op jit(solution)/shard_map/ppermute | solution.py:735
  284.3 12.3 %mix_fwd.1 = (bf16[256,2560]{1,0:T(8,128)(2,1)}, f32[256,2560]{1,0:T(8,128)}, f32[256,2560]{1,0:T(8,128)}) custom-call(f32[264,2560]{1,0:T(8,128)} %rows_into.3.bx_ref, s32[264,1]{1,0:T(8,128)} %subtract_select_fusion.off_ref, f32[16,2560]{1,0:T(8,128)} %maximum_maximum_fusion.vec_ref, bf16[10,256,256]{2,1,0:T(8,128)(2,1)} %get-tuple-element.192.rate_ref, ...), custom_call_target="tpu_custom_call" | custom-call | flops 13799999488 | bytes 1024 | tf_op jit(solution)/shard_map/mix_fwd/pallas_call | solution.py:532
  328.0 16.3 %collective-permute-done.42.y_ref = bf16[1,320,1920]{2,1,0:T(8,128)(2,1)S(1)} collective-permute-done((bf16[1,320,1920]{2,1,0:T(8,128)(2,1)}, bf16[1,320,1920]{2,1,0:T(8,128)(2,1)S(1)}, u32[]{:S(2)}, u32[]{:S(2)}) %collective-permute-start.42) | collective-permute-done | bytes 1228832 | tf_op jit(solution)/shard_map/ppermute | solution.py:735
  347.3 23.3 %collective-permute-done.37.y_ref = bf16[1,320,1920]{2,1,0:T(8,128)(2,1)S(1)} collective-permute-done((bf16[1,320,1920]{2,1,0:T(8,128)(2,1)}, bf16[1,320,1920]{2,1,0:T(8,128)(2,1)S(1)}, u32[]{:S(2)}, u32[]{:S(2)}) %collective-permute-start.37) | collective-permute-done | bytes 1228832 | tf_op jit(solution)/shard_map/ppermute | solution.py:735
  415.1 33.0 %collective-permute-done.34.refs_1_ = bf16[256,2560]{1,0:T(8,128)(2,1)S(1)} collective-permute-done((bf16[256,2560]{1,0:T(8,128)(2,1)S(1)}, bf16[256,2560]{1,0:T(8,128)(2,1)S(1)}, u32[]{:S(2)}, u32[]{:S(2)}) %collective-permute-start.34) | collective-permute-done | bytes 1310752 | tf_op jit(solution)/shard_map/ppermute | solution.py:738
  448.0 32.3 %collective-permute-done.46.refs_0_.refs_2_ = bf16[256,2560]{1,0:T(8,128)(2,1)} collective-permute-done((bf16[256,2560]{1,0:T(8,128)(2,1)S(1)}, bf16[256,2560]{1,0:T(8,128)(2,1)}, u32[]{:S(2)}, u32[]{:S(2)}) %collective-permute-start.46) | collective-permute-done | bytes 1310752 | tf_op jit(solution)/shard_map/ppermute | solution.py:738
  480.4 26.8 %feed_pair.2 = (bf16[512,1920]{1,0:T(8,128)(2,1)}, bf16[512,1920]{1,0:T(8,128)(2,1)}, bf16[512,1920]{1,0:T(8,128)(2,1)}) custom-call(s32[1]{0:T(128)} %bitcast.42.lane_ref, bf16[256,2560]{1,0:T(8,128)(2,1)} %copy-done.19, bf16[256,2560]{1,0:T(8,128)(2,1)} %copy-done.74, bf16[1024,2560]{1,0:T(8,128)(2,1)} %all-gather.11.cloned.1.call-done.refs_2_.refs_3_.refs_0_.refs_1_, ...), custom_call_target="tpu_custom_call" | custom-call | flops 31050000384 | bytes 1024 | tf_op jit(solution)/shard_map/feed_pair/pallas_call | solution.py:294
  507.2 13.3 %feed_back.4 = bf16[256,2560]{1,0:T(8,128)(2,1)} custom-call(bf16[512,1920]{1,0:T(8,128)(2,1)} %get-tuple-element.132.refs_0_.refs_4_, bf16[512,1920]{1,0:T(8,128)(2,1)} %get-tuple-element.126.refs_1_.refs_4_, bf16[1280,1920]{1,0:T(8,128)(2,1)} %join_feats.3.refs_4_.refs_2_, bf16[1280,1920]{1,0:T(8,128)(2,1)} %collective-permute-done.35.refs_5_.refs_3_, ...), custom_call_target="tpu_custom_call" | custom-call | flops 14949999616 | bytes 1024 | tf_op jit(solution)/shard_map/feed_back/pallas_call | solution.py:339
  528.7 26.9 %feed_pair.3 = (bf16[512,1920]{1,0:T(8,128)(2,1)}, bf16[512,1920]{1,0:T(8,128)(2,1)}, bf16[512,1920]{1,0:T(8,128)(2,1)}) custom-call(s32[1]{0:T(128)} %bitcast.42.lane_ref, bf16[256,2560]{1,0:T(8,128)(2,1)} %collective-permute-done.46.refs_0_.refs_2_, bf16[256,2560]{1,0:T(8,128)(2,1)} %collective-permute-done.47.refs_1_.refs_3_, ...), custom_call_target="tpu_custom_call" | custom-call | flops 31050000384 | bytes 1024 | tf_op jit(solution)/shard_map/feed_pair/pallas_call | solution.py:294
  561.4 13.4 %feed_back.5 = bf16[256,2560]{1,0:T(8,128)(2,1)} custom-call(bf16[512,1920]{1,0:T(8,128)(2,1)} %get-tuple-element.125.refs_0_.refs_5_, bf16[512,1920]{1,0:T(8,128)(2,1)} %get-tuple-element.108.refs_1_.refs_5_, bf16[1280,1920]{1,0:T(8,128)(2,1)} %join_feats.3.refs_4_.refs_2_, bf16[1280,1920]{1,0:T(8,128)(2,1)} %collective-permute-done.35.refs_5_.refs_3_, ...), custom_call_target="tpu_custom_call" | custom-call | flops 14949999616 | bytes 1024 | tf_op jit(solution)/shard_map/feed_back/pallas_call | solution.py:339
  596.2 10.9 weight_grad.14
  612.4 10.8 weight_grad.15
  629.0 13.4 %feed_back.6 = bf16[256,2560]{1,0:T(8,128)(2,1)} custom-call(bf16[512,1920]{1,0:T(8,128)(2,1)} %get-tuple-element.125.refs_0_.refs_5_, bf16[512,1920]{1,0:T(8,128)(2,1)} %get-tuple-element.108.refs_1_.refs_5_, bf16[1280,1920]{1,0:T(8,128)(2,1)} %join_feats.3.refs_4_.refs_2_, bf16[1280,1920]{1,0:T(8,128)(2,1)} %collective-permute-done.35.refs_5_.refs_3_, ...), custom_call_target="tpu_custom_call" | custom-call | flops 14949999616 | bytes 1024 | tf_op jit(solution)/shard_map/feed_back/pallas_call | solution.py:339
  642.3 10.5 weight_grad.16
  658.4 11.0 collective-permute-done.51
  672.6 11.2 weight_grad.17
  683.8 13.2 %collective-permute-done.58 = bf16[1,320,1920]{2,1,0:T(8,128)(2,1)S(1)} collective-permute-done((bf16[1,320,1920]{2,1,0:T(8,128)(2,1)S(1)}, bf16[1,320,1920]{2,1,0:T(8,128)(2,1)S(1)}, u32[]{:S(2)}, u32[]{:S(2)}) %collective-permute-start.58) | collective-permute-done | bytes 1228832 | tf_op jit(solution)/shard_map/ppermute | solution.py:735
  698.4 13.7 %feed_back.7 = f32[256,2560]{1,0:T(8,128)} custom-call(bf16[512,1920]{1,0:T(8,128)(2,1)} %get-tuple-element.132.refs_0_.refs_4_, bf16[512,1920]{1,0:T(8,128)(2,1)} %get-tuple-element.126.refs_1_.refs_4_, bf16[1280,1920]{1,0:T(8,128)(2,1)} %join_feats.3.refs_4_.refs_2_, bf16[1280,1920]{1,0:T(8,128)(2,1)} %collective-permute-done.35.refs_5_.refs_3_, ...), custom_call_target="tpu_custom_call" | custom-call | flops 14949999616 | bytes 1024 | tf_op jit(solution)/shard_map/feed_back/pallas_call | solution.py:339
  730.8 25.1 %collective-permute-done.61 = bf16[1,320,1920]{2,1,0:T(8,128)(2,1)} collective-permute-done((bf16[1,320,1920]{2,1,0:T(8,128)(2,1)S(1)}, bf16[1,320,1920]{2,1,0:T(8,128)(2,1)}, u32[]{:S(2)}, u32[]{:S(2)}) %collective-permute-start.61) | collective-permute-done | bytes 1228832 | tf_op jit(solution)/shard_map/ppermute | solution.py:735
  780.3 13.1 %mix_adj.1 = (bf16[256,2560]{1,0:T(8,128)(2,1)}, f32[256,2560]{1,0:T(8,128)}, f32[256,2560]{1,0:T(8,128)}, f32[8,2560]{1,0:T(8,128)}) custom-call(f32[256,2560]{1,0:T(8,128)} %rows_into.5.gm_ref, f32[256,2560]{1,0:T(8,128)} %rows_into.4.by_ref, f32[256,2560]{1,0:T(8,128)} %get-tuple-element.143.full_ref, bf16[256,2560]{1,0:T(8,128)(2,1)} %get-tuple-element.144.conv_ref, ...), custom_call_target="tpu_custom_call" | custom-call | flops 14949999616 | bytes 1024 | tf_op jit(solution)/shard_map/mix_adj/pallas_call | solution.py:595
  808.5 17.9 %collective-permute-done.67 = bf16[1,4,160,640]{3,2,1,0:T(8,128)(2,1)S(1)} collective-permute-done((bf16[1,4,160,640]{3,2,1,0:T(8,128)(2,1)S(1)}, bf16[1,4,160,640]{3,2,1,0:T(8,128)(2,1)S(1)}, u32[]{:S(2)}, u32[]{:S(2)}) %collective-permute-start.67) | collective-permute-done | bytes 819232 | tf_op jit(solution)/shard_map/ppermute | solution.py:735
  829.8 34.4 %collective-permute-done.78 = bf16[1,4,320,640]{3,2,1,0:T(8,128)(2,1)S(1)} collective-permute-done((bf16[1,4,320,640]{3,2,1,0:T(8,128)(2,1)S(1)}, bf16[1,4,320,640]{3,2,1,0:T(8,128)(2,1)S(1)}, u32[]{:S(2)}, u32[]{:S(2)}) %collective-permute-start.78) | collective-permute-done | bytes 1638432 | tf_op jit(solution)/shard_map/ppermute | solution.py:735
  893.8 14.0 %mix_bwd.1 = (f32[256,2560]{1,0:T(8,128)}, bf16[10,256,256]{2,1,0:T(8,128)(2,1)}, bf16[10,256,256]{2,1,0:T(8,128)(2,1)}, f32[8,2560]{1,0:T(8,128)}) custom-call(f32[256,2560]{1,0:T(8,128)} %get-tuple-element.154.adj_ref, f32[256,2560]{1,0:T(8,128)} %get-tuple-element.155.tail_ref, f32[8,2560]{1,0:T(8,128)} %broadcast_in_dim.129.hand_ref, ...), custom_call_target="tpu_custom_call" | custom-call | flops 16099999744 | bytes 1024 | tf_op jit(solution)/shard_map/mix_bwd/pallas_call | solution.py:652
  917.1 18.8 %feed_out.1 = bf16[1024,2560]{1,0:T(8,128)(2,1)} custom-call(s32[1]{0:T(128)} %bitcast.42.lane_ref, bf16[512,1920]{1,0:T(8,128)(2,1)} %get-tuple-element.147.refs_4_.refs_0_, bf16[512,1920]{1,0:T(8,128)(2,1)} %get-tuple-element.110.refs_5_.refs_1_, bf16[1280,1920]{1,0:T(8,128)(2,1)} %join_feats.5.refs_8_.refs_2_, ...), custom_call_target="tpu_custom_call" | custom-call | flops 20700000256 | bytes 1024 | tf_op jit(solution)/shard_map/feed_out/pallas_call | solution.py:374
  951.8 14.8 %rows_back.3 = f32[256,2560]{1,0:T(8,128)} custom-call(bf16[256,2560]{1,0:T(8,128)(2,1)} %get-tuple-element.163.refs_1_.refs_0_, bf16[256,2560]{1,0:T(8,128)(2,1)} %get-tuple-element.146.refs_1_, bf16[4,1280,640]{2,1,0:T(8,128)(2,1)} %join_lanes.3.own_ref.refs_2_, bf16[4,1280,640]{2,1,0:T(8,128)(2,1)} %collective-permute-done.13.other_ref.refs_3_, ...), custom_call_target="tpu_custom_call" | custom-call | flops 21849999360 | bytes 1024 | tf_op jit(solution)/shard_map/rows_back/pallas_call | solution.py:244
  1024.3 17.0 %collective-permute-done.86 = f32[16,2560]{1,0:T(8,128)S(1)} collective-permute-done((f32[16,2560]{1,0:T(8,128)S(1)}, f32[16,2560]{1,0:T(8,128)S(1)}, u32[]{:S(2)}, u32[]{:S(2)}) %collective-permute-start.86) | collective-permute-done | bytes 163872 | tf_op jit(solution)/shard_map/ppermute | solution.py:1004
  1097.4 46.5 %collective-permute-done.69 = bf16[2,64,2560]{2,1,0:T(8,128)(2,1)S(1)} collective-permute-done((bf16[2,64,2560]{2,1,0:T(8,128)(2,1)S(1)}, bf16[2,64,2560]{2,1,0:T(8,128)(2,1)S(1)}, u32[]{:S(2)}, u32[]{:S(2)}) %collective-permute-start.69) | collective-permute-done | bytes 655392 | tf_op jit(solution)/shard_map/ppermute | solution.py:735
  1171.2 11.6 reduce-scatter.8.cloned.1.call-done
  (592 shorter events, 592.5 us)
Async XLA Ops:
  7.2 63.8 %all-gather.13.cloned.1.call-start = ((), (), s32[]{:S(2)}) async-start(), calls=%async_computation.13 | async-start | bytes 2048000 | tf_op jit(solution)/shard_map/all_gather | solution.py:840
  7.9 129.4 %all-gather.15.cloned.1.call-start = ((), (), s32[]{:S(2)}) async-start(), calls=%async_computation.14 | async-start | bytes 2048000 | tf_op jit(solution)/shard_map/all_gather | solution.py:840
  8.7 200.8 %all-gather.17.cloned.1.call-start = ((), (), s32[]{:S(2)}) async-start(), calls=%async_computation.15 | async-start | bytes 2048000 | tf_op jit(solution)/shard_map/all_gather | solution.py:840
  8.7 63.3 %collective-permute-start.17 = (bf16[1,320,1920]{2,1,0:T(8,128)(2,1)}, bf16[1,320,1920]{2,1,0:T(8,128)(2,1)}, u32[]{:S(2)}, u32[]{:S(2)}) collective-permute-start(bf16[1,320,1920]{2,1,0:T(8,128)(2,1)} %bitcast.188), channel_id=1, source_target_pairs={{0,16},{4,20},{8,24},{12,28},{16,0},{20,4},{24,8},{28,12},{1,17},{... | collective-permute-start | bytes 3686408 | tf_op jit(solution)/shard_map/ppermute | solution.py:735
  11.8 63.1 %collective-permute-start.19 = (bf16[1,320,1920]{2,1,0:T(8,128)(2,1)}, bf16[1,320,1920]{2,1,0:T(8,128)(2,1)}, u32[]{:S(2)}, u32[]{:S(2)}) collective-permute-start(bf16[1,320,1920]{2,1,0:T(8,128)(2,1)} %bitcast.189), channel_id=1, source_target_pairs={{0,8},{4,12},{8,0},{12,4},{16,24},{20,28},{24,16},{28,20},{1,9},{5... | collective-permute-start | bytes 3686408 | tf_op jit(solution)/shard_map/ppermute | solution.py:735
  17.6 239.4 %all-gather.9.cloned.1.call-start = ((), (), s32[]{:S(2)}) async-start(), calls=%async_computation.5 | async-start | bytes 2949120 | tf_op jit(solution)/shard_map/all_gather | solution.py:845
  32.2 448.1 %all-gather.11.cloned.1.call-start = ((), (), s32[]{:S(2)}) async-start(), calls=%async_computation.6 | async-start | bytes 6553600 | tf_op jit(solution)/shard_map/all_gather | solution.py:848
  72.0 52.0 %collective-permute-start.1 = (bf16[1,128,2560]{2,1,0:T(8,128)(2,1)S(1)}, bf16[1,128,2560]{2,1,0:T(8,128)(2,1)S(1)}, u32[]{:S(2)}, u32[]{:S(2)}) collective-permute-start(bf16[1,128,2560]{2,1,0:T(8,128)(2,1)S(1)} %get-tuple-element.214), channel_id=1, source_target_pairs={{0,16},{4,20},{8,24},{12,28},{16,0},{20,4},{24,8},{28,12},{1,17},{... | collective-permute-start | bytes 1966088 | tf_op jit(solution)/shard_map/ppermute | solution.py:735
  74.9 59.5 %collective-permute-start.18 = (bf16[1,160,1920]{2,1,0:T(8,128)(2,1)S(1)}, bf16[1,160,1920]{2,1,0:T(8,128)(2,1)S(1)}, u32[]{:S(2)}, u32[]{:S(2)}) collective-permute-start(bf16[1,160,1920]{2,1,0:T(8,128)(2,1)S(1)} %slice.408), channel_id=1, source_target_pairs={{0,8},{4,12},{8,0},{12,4},{16,24},{20,28},{24,16},{28,20},{1,9},{5... | collective-permute-start | bytes 1843208 | tf_op jit(solution)/shard_map/ppermute | solution.py:735
  86.2 51.1 %collective-permute-start.20 = (bf16[1,160,1920]{2,1,0:T(8,128)(2,1)S(1)}, bf16[1,160,1920]{2,1,0:T(8,128)(2,1)}, u32[]{:S(2)}, u32[]{:S(2)}) collective-permute-start(bf16[1,160,1920]{2,1,0:T(8,128)(2,1)S(1)} %slice.409), channel_id=1, source_target_pairs={{0,16},{4,20},{8,24},{12,28},{16,0},{20,4},{24,8},{28,12},{1,17},{... | collective-permute-start | bytes 1843208 | tf_op jit(solution)/shard_map/ppermute | solution.py:735
  110.0 62.9 %collective-permute-start.28 = (bf16[4,32,2560]{2,1,0:T(8,128)(2,1)}, bf16[4,32,2560]{2,1,0:T(8,128)(2,1)}, u32[]{:S(2)}, u32[]{:S(2)}) collective-permute-start(bf16[4,32,2560]{2,1,0:T(8,128)(2,1)} %get-tuple-element.206), channel_id=1, source_target_pairs={{0,4},{4,0},{8,12},{12,8},{16,20},{20,16},{24,28},{28,24},{1,5},{5... | collective-permute-start | bytes 1966088 | tf_op jit(solution)/shard_map/ppermute | solution.py:735
  137.3 59.5 %collective-permute-start.22 = (bf16[1,4,320,640]{3,2,1,0:T(8,128)(2,1)}, bf16[1,4,320,640]{3,2,1,0:T(8,128)(2,1)}, u32[]{:S(2)}, u32[]{:S(2)}) collective-permute-start(bf16[1,4,320,640]{3,2,1,0:T(8,128)(2,1)} %bitcast.180), channel_id=1, source_target_pairs={{0,16},{4,20},{8,24},{12,28},{16,0},{20,4},{24,8},{28,12},{1,17},{... | collective-permute-start | bytes 4915208 | tf_op jit(solution)/shard_map/ppermute | solution.py:735
  167.7 107.2 %collective-permute-start.13 = (bf16[4,1280,640]{2,1,0:T(8,128)(2,1)}, bf16[4,1280,640]{2,1,0:T(8,128)(2,1)}, u32[]{:S(2)}, u32[]{:S(2)}) collective-permute-start(bf16[4,1280,640]{2,1,0:T(8,128)(2,1)} %join_lanes.3.own_ref.refs_2_), channel_id=1, source_target_pairs={{0,4},{4,0},{8,12},{12,8},{16,20},{20,16},{24,28},{28,24},{1,5},{5... | collective-permute-start | bytes 19660808 | tf_op jit(solution)/shard_map/ppermute | solution.py:735
  227.2 86.9 %collective-permute-start.25 = (bf16[4,1280,640]{2,1,0:T(8,128)(2,1)}, bf16[4,1280,640]{2,1,0:T(8,128)(2,1)}, u32[]{:S(2)}, u32[]{:S(2)}) collective-permute-start(bf16[4,1280,640]{2,1,0:T(8,128)(2,1)} %join_lanes.4.own_ref.refs_4_), channel_id=1, source_target_pairs={{0,4},{4,0},{8,12},{12,8},{16,20},{20,16},{24,28},{28,24},{1,5},{5... | collective-permute-start | bytes 19660808 | tf_op jit(solution)/shard_map/ppermute | solution.py:735
  274.9 127.0 %collective-permute-start.33 = (bf16[4,1280,640]{2,1,0:T(8,128)(2,1)}, bf16[4,1280,640]{2,1,0:T(8,128)(2,1)}, u32[]{:S(2)}, u32[]{:S(2)}) collective-permute-start(bf16[4,1280,640]{2,1,0:T(8,128)(2,1)} %join_lanes.5.refs_1_.own_ref), channel_id=1, source_target_pairs={{0,4},{4,0},{8,12},{12,8},{16,20},{20,16},{24,28},{28,24},{1,5},{5... | collective-permute-start | bytes 19660808 | tf_op jit(solution)/shard_map/ppermute | solution.py:735
  314.1 708.3 %reduce-scatter.14.cloned.1.call-start = ((), (), s32[]{:S(2)}) async-start(), calls=%async_computation.12 | async-start | bytes 2048000 | tf_op jit(solution)/shard_map/reduce_scatter | solution.py:960
  316.2 54.5 %collective-permute-start.37 = (bf16[1,320,1920]{2,1,0:T(8,128)(2,1)}, bf16[1,320,1920]{2,1,0:T(8,128)(2,1)S(1)}, u32[]{:S(2)}, u32[]{:S(2)}) collective-permute-start(bf16[1,320,1920]{2,1,0:T(8,128)(2,1)} %bitcast.191), channel_id=1, source_target_pairs={{0,16},{4,20},{8,24},{12,28},{16,0},{20,4},{24,8},{28,12},{1,17},{... | collective-permute-start | bytes 3686408 | tf_op jit(solution)/shard_map/ppermute | solution.py:735
  317.7 54.5 %collective-permute-start.36 = (bf16[1,320,1920]{2,1,0:T(8,128)(2,1)}, bf16[1,320,1920]{2,1,0:T(8,128)(2,1)S(1)}, u32[]{:S(2)}, u32[]{:S(2)}) collective-permute-start(bf16[1,320,1920]{2,1,0:T(8,128)(2,1)} %bitcast.192), channel_id=1, source_target_pairs={{0,8},{4,12},{8,0},{12,4},{16,24},{20,28},{24,16},{28,20},{1,9},{5... | collective-permute-start | bytes 3686408 | tf_op jit(solution)/shard_map/ppermute | solution.py:735
  384.4 95.9 %collective-permute-start.35 = (bf16[1280,1920]{1,0:T(8,128)(2,1)}, bf16[1280,1920]{1,0:T(8,128)(2,1)}, u32[]{:S(2)}, u32[]{:S(2)}) collective-permute-start(bf16[1280,1920]{1,0:T(8,128)(2,1)} %join_feats.3.refs_4_.refs_2_), channel_id=1, source_target_pairs={{0,4},{4,0},{8,12},{12,8},{16,20},{20,16},{24,28},{28,24},{1,5},{5... | collective-permute-start | bytes 14745608 | tf_op jit(solution)/shard_map/ppermute | solution.py:735
  389.9 90.4 %collective-permute-start.45 = (bf16[1280,1920]{1,0:T(8,128)(2,1)}, bf16[1280,1920]{1,0:T(8,128)(2,1)}, u32[]{:S(2)}, u32[]{:S(2)}) collective-permute-start(bf16[1280,1920]{1,0:T(8,128)(2,1)} %join_feats.5.refs_8_.refs_2_), channel_id=1, source_target_pairs={{0,4},{4,0},{8,12},{12,8},{16,20},{20,16},{24,28},{28,24},{1,5},{5... | collective-permute-start | bytes 14745608 | tf_op jit(solution)/shard_map/ppermute | solution.py:735
  401.9 78.5 %collective-permute-start.40 = (bf16[1280,1920]{1,0:T(8,128)(2,1)}, bf16[1280,1920]{1,0:T(8,128)(2,1)}, u32[]{:S(2)}, u32[]{:S(2)}) collective-permute-start(bf16[1280,1920]{1,0:T(8,128)(2,1)} %join_feats.4.refs_6_.refs_4_), channel_id=1, source_target_pairs={{0,4},{4,0},{8,12},{12,8},{16,20},{20,16},{24,28},{28,24},{1,5},{5... | collective-permute-start | bytes 14745608 | tf_op jit(solution)/shard_map/ppermute | solution.py:735
  805.7 80.0 %collective-permute-start.72 = (bf16[4,1280,640]{2,1,0:T(8,128)(2,1)}, bf16[4,1280,640]{2,1,0:T(8,128)(2,1)}, u32[]{:S(2)}, u32[]{:S(2)}) collective-permute-start(bf16[4,1280,640]{2,1,0:T(8,128)(2,1)} %weight_grad.20), channel_id=1, source_target_pairs={{0,4},{4,0},{8,12},{12,8},{16,20},{20,16},{24,28},{28,24},{1,5},{5... | collective-permute-start | bytes 19660808 | tf_op jit(solution)/shard_map/ppermute | solution.py:735
  867.7 180.9 %reduce-scatter.12.cloned.1.call-start = ((), (), s32[]{:S(2)}) async-start(), calls=%async_computation.10 | async-start | bytes 2949120 | tf_op jit(solution)/shard_map/reduce_scatter | solution.py:996
  911.2 150.8 %reduce-scatter.6.cloned.1.call-start = ((), (), s32[]{:S(2)}) async-start(), calls=%async_computation.7 | async-start | bytes 6553600 | tf_op jit(solution)/shard_map/reduce_scatter | solution.py:972
  936.0 227.5 %all-reduce.4.cloned.1.call-start = ((), (), s32[]{:S(2)}) async-start(), calls=%async_computation.11 | async-start | bytes 655360 | tf_op jit(solution)/shard_map/psum | solution.py:997
  936.1 56.2 %collective-permute-start.88 = (bf16[1,4,160,640]{3,2,1,0:T(8,128)(2,1)}, bf16[1,4,160,640]{3,2,1,0:T(8,128)(2,1)}, u32[]{:S(2)}, u32[]{:S(2)}) collective-permute-start(bf16[1,4,160,640]{3,2,1,0:T(8,128)(2,1)} %get-tuple-element.153), channel_id=1, source_target_pairs={{0,16},{4,20},{8,24},{12,28},{16,0},{20,4},{24,8},{28,12},{1,17},{... | collective-permute-start | bytes 2457608 | tf_op jit(solution)/shard_map/ppermute | solution.py:735
  937.5 59.2 %collective-permute-start.87 = (bf16[1,4,160,640]{3,2,1,0:T(8,128)(2,1)}, bf16[1,4,160,640]{3,2,1,0:T(8,128)(2,1)}, u32[]{:S(2)}, u32[]{:S(2)}) collective-permute-start(bf16[1,4,160,640]{3,2,1,0:T(8,128)(2,1)} %get-tuple-element.152), channel_id=1, source_target_pairs={{0,8},{4,12},{8,0},{12,4},{16,24},{20,28},{24,16},{28,20},{1,9},{5... | collective-permute-start | bytes 2457608 | tf_op jit(solution)/shard_map/ppermute | solution.py:735
  951.8 112.9 %collective-permute-start.89 = (bf16[4,1280,640]{2,1,0:T(8,128)(2,1)}, bf16[4,1280,640]{2,1,0:T(8,128)(2,1)}, u32[]{:S(2)}, u32[]{:S(2)}) collective-permute-start(bf16[4,1280,640]{2,1,0:T(8,128)(2,1)} %weight_grad.22), channel_id=1, source_target_pairs={{0,4},{4,0},{8,12},{12,8},{16,20},{20,16},{24,28},{28,24},{1,5},{5... | collective-permute-start | bytes 19660808 | tf_op jit(solution)/shard_map/ppermute | solution.py:735
  995.0 53.7 %collective-permute-start.94 = (bf16[1,4,320,640]{3,2,1,0:T(8,128)(2,1)}, bf16[1,4,320,640]{3,2,1,0:T(8,128)(2,1)S(1)}, u32[]{:S(2)}, u32[]{:S(2)}) collective-permute-start(bf16[1,4,320,640]{3,2,1,0:T(8,128)(2,1)} %pad_maximum_fusion.5), channel_id=1, source_target_pairs={{0,8},{4,12},{8,0},{12,4},{16,24},{20,28},{24,16},{28,20},{1,9},{5... | collective-permute-start | bytes 4915208 | tf_op jit(solution)/shard_map/ppermute | solution.py:735
  1048.6 116.8 %reduce-scatter.10.cloned.1.call-start = ((), (), s32[]{:S(2)}) async-start(), calls=%async_computation.9 | async-start | bytes 2048000 | tf_op jit(solution)/shard_map/reduce_scatter | solution.py:960
  1054.3 128.5 %reduce-scatter.8.cloned.1.call-start = ((), (), s32[]{:S(2)}) async-start(), calls=%async_computation.8 | async-start | bytes 2048000 | tf_op jit(solution)/shard_map/reduce_scatter | solution.py:960
  1097.3 52.0 %collective-permute-start.81 = (bf16[4,32,2560]{2,1,0:T(8,128)(2,1)S(1)}, bf16[4,32,2560]{2,1,0:T(8,128)(2,1)S(1)}, u32[]{:S(2)}, u32[]{:S(2)}) collective-permute-start(bf16[4,32,2560]{2,1,0:T(8,128)(2,1)S(1)} %get-tuple-element.194), channel_id=1, source_target_pairs={{0,4},{4,0},{8,12},{12,8},{16,20},{20,16},{24,28},{28,24},{1,5},{5... | collective-permute-start | bytes 1966088 | tf_op jit(solution)/shard_map/ppermute | solution.py:735
  (164 other events, 2891.9 us)
Sparse Core Ops, SparseCore 0:
  9.6 41.1 all-gather.12
  52.3 36.9 all-gather.14
  91.5 37.0 all-gather.16
  130.9 47.5 all-gather.8
  314.2 95.3 all-gather.10
  867.8 36.5 reduce-scatter.13
  911.3 47.3 reduce-scatter.11
  961.1 100.9 reduce-scatter.5
  1064.5 36.6 all-reduce.3
  1103.5 36.0 reduce-scatter.9
  1145.9 36.7 reduce-scatter.7

commit v2 on v1

--- a/solution.py
+++ b/solution.py
@@ -740,6 +740,18 @@
     def shift(x, by):
         return lax.ppermute(x, "tensor", [(i, i + by) for i in range(lanes) if 0 <= i + by < lanes])
 
+    def gather_near(part, *deps):
+        part = (after(part, *deps) if deps else part)[None]
+        for bit in range(3, bits):
+            part = jnp.concatenate([part, swap(part, bit)], axis=0)
+        return part, swap(part, 1), swap(part, 2)
+
+    def gather_far(near, *deps):
+        part, from_x, from_y = near
+        half = feats // 2
+        low, high = after((from_y[..., :half, :], from_x[..., half:, :]), *deps)
+        return part, from_x, from_y, swap(low, 1), swap(high, 2)
+
     def gather_outer(part, *deps):
         part = (after(part, *deps) if deps else part)[None]
         for bit in range(3, bits):
@@ -884,12 +896,10 @@
     normed_low = (x * inv_rms(x) * gain_first[None]).astype(bf16)
     normed_ext = jnp.concatenate([up(normed_low[rows - halo :]), normed_low], axis=0)
     bx_ext = rows_into(normed_ext, wx)
-    part_u = gather_outer(feed_up, part_y[3:], bx_ext)
+    near_u = gather_near(feed_up, part_y[3:], bx_ext)
     by = rows_into(normed_low, wy)
     conv_low, state_loc, prod_loc = mix_fwd(bx_ext, off_ext, vec, rate_t, input_t)
-    part_d = gather_outer(flip_weight(feed_down), part_o[3:], state_loc)
-    wu = with_other(join_feats(*part_u))
-    wd = with_other(join_feats(*part_d))
+    near_d = gather_near(flip_weight(feed_down), part_o[3:], state_loc)
     edge = jnp.concatenate([state_loc[rows - 1 :], prod_loc[rows - 1 :], jnp.zeros((6, lru_total), f32)], axis=0)
 
     def carry_in(edge, direction):
@@ -905,9 +915,16 @@
     state, mixed = mix_out(state_loc, prod_loc, enter, by, wide)
     middle = x + rows_back([(mixed, wo)])
     ns_low = (middle * inv_rms(middle) * gain_second[None]).astype(bf16)
+    part_u = gather_far(near_u, ns_low)
+    part_d = gather_far(near_d, ns_low)
     ns_rows = [ns_low]
     for _ in range(lanes - 1):
         ns_rows.append(up(ns_rows[-1]))
+
+    part_u = (after(part_u[0], ns_rows[1]),) + tuple(part_u[1:])
+    part_d = (after(part_d[0], ns_rows[1]),) + tuple(part_d[1:])
+    wu = with_other(join_feats(*part_u))
+    wd = with_other(join_feats(*part_d))
 
     pair = 2
     hidden, g_gate, g_up = [], [], []

time: 1200 us -> 1180 us (0.983)
  waiting for transfers between devices: 509 us -> 476 us
    ppermute x7, waiting for transfers between devices: 74.6 us -> 53.5 us  [up(): lax.ppermute(x, 'tensor', [(i, (i + 1) % lanes) for i in range(lanes)])]
    ppermute x78, waiting for transfers between devices: 372 us -> 360 us  [swap(): return lax.ppermute(x, 'dp', [(i, i ^ 1 << bit) for i in range(groups)])]
  transfers between devices with their start and end apart: 107 -> 107, of which waited for: 50 -> 50; matrix products, arithmetic and copies ran while one was open for 9% -> 10% of each run, Pallas kernels for 30% -> 31%
where the time goes in v2:
time: 1180 us; the launch traced here: 1160 us
  waiting for transfers between devices  476 us (40%)
  Pallas kernels  432 us (37%)
  starting transfers between devices  98 us (8%)
  other arithmetic  77.7 us (7%)
  local copies, waits for them, and re-layouts  60.8 us (5%)
  between operations  17.1 us (1%)
    ppermute x78, waiting for transfers between devices, swap(): return lax.ppermute(x, 'dp', [(i, i ^ 1 << bit) for i in range(groups)])  360 us
    pallas_call x12, Pallas kernels, weight_grad(): pl.pallas_call(kernel, grid_spec=pltpu.PrefetchScalarGridSpec(num_scalar_...  106 us
    ppermute x78, starting transfers between devices, swap(): return lax.ppermute(x, 'dp', [(i, i ^ 1 << bit) for i in range(groups)])  69.6 us
    pallas_call x4, Pallas kernels, feed_back(): pl.pallas_call(kernel, grid=(2 * steps,), in_specs=specs, out_specs=pl.Bl...  53.7 us
    pallas_call x2, Pallas kernels, feed_pair(): pl.pallas_call(kernel, grid_spec=pltpu.PrefetchScalarGridSpec(num_scalar_...  53.6 us
    ppermute x7, waiting for transfers between devices, up(): lax.ppermute(x, 'tensor', [(i, (i + 1) % lanes) for i in range(lanes)])  53.5 us
    pallas_call x6, Pallas kernels, turn_feats(): pl.pallas_call(_turn_kernel, grid=(width // tile,), in_specs=[pl.BlockSpe...  34 us
    pallas_call x3, Pallas kernels, rows_into(): pl.pallas_call(kernel, grid=(lanes,), in_specs=[pl.BlockSpec((rows, width...  28.6 us
  transfers between devices with their start and end apart: 107, of which 50 were waited for; matrix products, arithmetic and copies ran while one was open for 10% of the time, Pallas kernels for 31%

profile of v2, /device:TPU:0, one launch (start us, length us, event | category | flops | bytes accessed | tf_op | source)
XLA Modules:
  0.0 1161.4 jit_solution(15208457352607633285)
XLA Ops:
  87.5 22.5 %collective-permute-done.10.y_ref = bf16[1,4,320,640]{3,2,1,0:T(8,128)(2,1)S(1)} collective-permute-done((bf16[1,4,320,640]{3,2,1,0:T(8,128)(2,1)}, bf16[1,4,320,640]{3,2,1,0:T(8,128)(2,1)S(1)}, u32[]{:S(2)}, u32[]{:S(2)}) %collective-permute-start.10) | collective-permute-done | bytes 1638432 | tf_op jit(solution)/shard_map/ppermute | solution.py:735
  110.0 11.2 collective-permute-done.9.x_ref
  137.8 14.7 %collective-permute-done.11.low_ref = bf16[1,4,160,640]{3,2,1,0:T(8,128)(2,1)} collective-permute-done((bf16[1,4,160,640]{3,2,1,0:T(8,128)(2,1)S(1)}, bf16[1,4,160,640]{3,2,1,0:T(8,128)(2,1)}, u32[]{:S(2)}, u32[]{:S(2)}) %collective-permute-start.11) | collective-permute-done | bytes 819232 | tf_op jit(solution)/shard_map/ppermute | solution.py:735
  179.5 17.3 %collective-permute-done.22.y_ref = bf16[1,4,320,640]{3,2,1,0:T(8,128)(2,1)} collective-permute-done((bf16[1,4,320,640]{3,2,1,0:T(8,128)(2,1)}, bf16[1,4,320,640]{3,2,1,0:T(8,128)(2,1)}, u32[]{:S(2)}, u32[]{:S(2)}) %collective-permute-start.22) | collective-permute-done | bytes 1638432 | tf_op jit(solution)/shard_map/ppermute | solution.py:735
  229.7 21.7 %collective-permute-done.30.y_ref = bf16[1,4,320,640]{3,2,1,0:T(8,128)(2,1)} collective-permute-done((bf16[1,4,320,640]{3,2,1,0:T(8,128)(2,1)}, bf16[1,4,320,640]{3,2,1,0:T(8,128)(2,1)}, u32[]{:S(2)}, u32[]{:S(2)}) %collective-permute-start.30) | collective-permute-done | bytes 1638432 | tf_op jit(solution)/shard_map/ppermute | solution.py:735
  298.5 12.3 %mix_fwd.1 = (bf16[256,2560]{1,0:T(8,128)(2,1)}, f32[256,2560]{1,0:T(8,128)}, f32[256,2560]{1,0:T(8,128)}) custom-call(f32[264,2560]{1,0:T(8,128)} %rows_into.3.bx_ref, s32[264,1]{1,0:T(8,128)} %subtract_select_fusion.off_ref, f32[16,2560]{1,0:T(8,128)} %maximum_maximum_fusion.vec_ref, bf16[10,256,256]{2,1,0:T(8,128)(2,1)} %get-tuple-element.204.rate_ref, ...), custom_call_target="tpu_custom_call" | custom-call | flops 13799999488 | bytes 1024 | tf_op jit(solution)/shard_map/mix_fwd/pallas_call | solution.py:532
  364.2 13.3 %collective-permute-done.37.y_ref = bf16[1,320,1920]{2,1,0:T(8,128)(2,1)S(1)} collective-permute-done((bf16[1,320,1920]{2,1,0:T(8,128)(2,1)}, bf16[1,320,1920]{2,1,0:T(8,128)(2,1)S(1)}, u32[]{:S(2)}, u32[]{:S(2)}) %collective-permute-start.37) | collective-permute-done | bytes 1228832 | tf_op jit(solution)/shard_map/ppermute | solution.py:735
  396.1 13.5 %collective-permute-done.34.refs_1_ = bf16[256,2560]{1,0:T(8,128)(2,1)S(1)} collective-permute-done((bf16[256,2560]{1,0:T(8,128)(2,1)S(1)}, bf16[256,2560]{1,0:T(8,128)(2,1)S(1)}, u32[]{:S(2)}, u32[]{:S(2)}) %collective-permute-start.34) | collective-permute-done | bytes 1310752 | tf_op jit(solution)/shard_map/ppermute | solution.py:738
  426.2 30.4 %collective-permute-done.46.refs_0_.refs_2_ = bf16[256,2560]{1,0:T(8,128)(2,1)S(1)} collective-permute-done((bf16[256,2560]{1,0:T(8,128)(2,1)S(1)}, bf16[256,2560]{1,0:T(8,128)(2,1)S(1)}, u32[]{:S(2)}, u32[]{:S(2)}) %collective-permute-start.46) | collective-permute-done | bytes 1310752 | tf_op jit(solution)/shard_map/ppermute | solution.py:738
  457.3 26.8 %feed_pair.2 = (bf16[512,1920]{1,0:T(8,128)(2,1)}, bf16[512,1920]{1,0:T(8,128)(2,1)}, bf16[512,1920]{1,0:T(8,128)(2,1)}) custom-call(s32[1]{0:T(128)} %bitcast.42.lane_ref, bf16[256,2560]{1,0:T(8,128)(2,1)} %copy-done.19, bf16[256,2560]{1,0:T(8,128)(2,1)} %copy-done.69, bf16[1024,2560]{1,0:T(8,128)(2,1)} %all-gather.11.cloned.1.call-done.refs_2_.refs_3_.refs_0_.refs_1_, ...), custom_call_target="tpu_custom_call" | custom-call | flops 31050000384 | bytes 1024 | tf_op jit(solution)/shard_map/feed_pair/pallas_call | solution.py:294
  484.1 13.3 %feed_back.4 = bf16[256,2560]{1,0:T(8,128)(2,1)} custom-call(bf16[512,1920]{1,0:T(8,128)(2,1)} %get-tuple-element.144.refs_0_.refs_4_, bf16[512,1920]{1,0:T(8,128)(2,1)} %get-tuple-element.138.refs_1_.refs_4_, bf16[1280,1920]{1,0:T(8,128)(2,1)} %join_feats.3.refs_4_.refs_2_, bf16[1280,1920]{1,0:T(8,128)(2,1)} %collective-permute-done.35.refs_5_.refs_3_, ...), custom_call_target="tpu_custom_call" | custom-call | flops 14949999616 | bytes 1024 | tf_op jit(solution)/shard_map/feed_back/pallas_call | solution.py:339
  501.1 26.8 %feed_pair.3 = (bf16[512,1920]{1,0:T(8,128)(2,1)}, bf16[512,1920]{1,0:T(8,128)(2,1)}, bf16[512,1920]{1,0:T(8,128)(2,1)}) custom-call(s32[1]{0:T(128)} %bitcast.42.lane_ref, bf16[256,2560]{1,0:T(8,128)(2,1)} %copy-done.70, bf16[256,2560]{1,0:T(8,128)(2,1)} %copy-done.71, bf16[1024,2560]{1,0:T(8,128)(2,1)} %all-gather.11.cloned.1.call-done.refs_2_.refs_3_.refs_0_.refs_1_, ...), custom_call_target="tpu_custom_call" | custom-call | flops 31050000384 | bytes 1024 | tf_op jit(solution)/shard_map/feed_pair/pallas_call | solution.py:294
  530.9 13.4 %feed_back.5 = bf16[256,2560]{1,0:T(8,128)(2,1)} custom-call(bf16[512,1920]{1,0:T(8,128)(2,1)} %get-tuple-element.137.refs_0_.refs_5_, bf16[512,1920]{1,0:T(8,128)(2,1)} %get-tuple-element.120.refs_1_.refs_5_, bf16[1280,1920]{1,0:T(8,128)(2,1)} %join_feats.3.refs_4_.refs_2_, bf16[1280,1920]{1,0:T(8,128)(2,1)} %collective-permute-done.35.refs_5_.refs_3_, ...), custom_call_target="tpu_custom_call" | custom-call | flops 14949999616 | bytes 1024 | tf_op jit(solution)/shard_map/feed_back/pallas_call | solution.py:339
  544.2 10.4 weight_grad.12
  566.2 10.9 weight_grad.14
  582.5 10.8 weight_grad.15
  598.5 13.4 %feed_back.6 = bf16[256,2560]{1,0:T(8,128)(2,1)} custom-call(bf16[512,1920]{1,0:T(8,128)(2,1)} %get-tuple-element.137.refs_0_.refs_5_, bf16[512,1920]{1,0:T(8,128)(2,1)} %get-tuple-element.120.refs_1_.refs_5_, bf16[1280,1920]{1,0:T(8,128)(2,1)} %join_feats.3.refs_4_.refs_2_, bf16[1280,1920]{1,0:T(8,128)(2,1)} %collective-permute-done.35.refs_5_.refs_3_, ...), custom_call_target="tpu_custom_call" | custom-call | flops 14949999616 | bytes 1024 | tf_op jit(solution)/shard_map/feed_back/pallas_call | solution.py:339
  611.9 10.5 weight_grad.16
  628.0 11.0 collective-permute-done.51
  642.2 11.2 weight_grad.17
  653.4 13.2 %collective-permute-done.58 = bf16[1,320,1920]{2,1,0:T(8,128)(2,1)S(1)} collective-permute-done((bf16[1,320,1920]{2,1,0:T(8,128)(2,1)S(1)}, bf16[1,320,1920]{2,1,0:T(8,128)(2,1)S(1)}, u32[]{:S(2)}, u32[]{:S(2)}) %collective-permute-start.58) | collective-permute-done | bytes 1228832 | tf_op jit(solution)/shard_map/ppermute | solution.py:735
  668.0 13.7 %feed_back.7 = f32[256,2560]{1,0:T(8,128)} custom-call(bf16[512,1920]{1,0:T(8,128)(2,1)} %get-tuple-element.144.refs_0_.refs_4_, bf16[512,1920]{1,0:T(8,128)(2,1)} %get-tuple-element.138.refs_1_.refs_4_, bf16[1280,1920]{1,0:T(8,128)(2,1)} %join_feats.3.refs_4_.refs_2_, bf16[1280,1920]{1,0:T(8,128)(2,1)} %collective-permute-done.35.refs_5_.refs_3_, ...), custom_call_target="tpu_custom_call" | custom-call | flops 14949999616 | bytes 1024 | tf_op jit(solution)/shard_map/feed_back/pallas_call | solution.py:339
  700.3 25.1 %collective-permute-done.61 = bf16[1,320,1920]{2,1,0:T(8,128)(2,1)} collective-permute-done((bf16[1,320,1920]{2,1,0:T(8,128)(2,1)S(1)}, bf16[1,320,1920]{2,1,0:T(8,128)(2,1)}, u32[]{:S(2)}, u32[]{:S(2)}) %collective-permute-start.61) | collective-permute-done | bytes 1228832 | tf_op jit(solution)/shard_map/ppermute | solution.py:735
  749.8 13.1 %mix_adj.1 = (bf16[256,2560]{1,0:T(8,128)(2,1)}, f32[256,2560]{1,0:T(8,128)}, f32[256,2560]{1,0:T(8,128)}, f32[8,2560]{1,0:T(8,128)}) custom-call(f32[256,2560]{1,0:T(8,128)} %rows_into.5.gm_ref, f32[256,2560]{1,0:T(8,128)} %rows_into.4.by_ref, f32[256,2560]{1,0:T(8,128)} %get-tuple-element.155.full_ref, bf16[256,2560]{1,0:T(8,128)(2,1)} %get-tuple-element.156.conv_ref, ...), custom_call_target="tpu_custom_call" | custom-call | flops 14949999616 | bytes 1024 | tf_op jit(solution)/shard_map/mix_adj/pallas_call | solution.py:595
  778.0 18.0 %collective-permute-done.67 = bf16[1,4,160,640]{3,2,1,0:T(8,128)(2,1)S(1)} collective-permute-done((bf16[1,4,160,640]{3,2,1,0:T(8,128)(2,1)S(1)}, bf16[1,4,160,640]{3,2,1,0:T(8,128)(2,1)S(1)}, u32[]{:S(2)}, u32[]{:S(2)}) %collective-permute-start.67) | collective-permute-done | bytes 819232 | tf_op jit(solution)/shard_map/ppermute | solution.py:735
  799.3 34.5 %collective-permute-done.78 = bf16[1,4,320,640]{3,2,1,0:T(8,128)(2,1)S(1)} collective-permute-done((bf16[1,4,320,640]{3,2,1,0:T(8,128)(2,1)S(1)}, bf16[1,4,320,640]{3,2,1,0:T(8,128)(2,1)S(1)}, u32[]{:S(2)}, u32[]{:S(2)}) %collective-permute-start.78) | collective-permute-done | bytes 1638432 | tf_op jit(solution)/shard_map/ppermute | solution.py:735
  863.2 14.0 %mix_bwd.1 = (f32[256,2560]{1,0:T(8,128)}, bf16[10,256,256]{2,1,0:T(8,128)(2,1)}, bf16[10,256,256]{2,1,0:T(8,128)(2,1)}, f32[8,2560]{1,0:T(8,128)}) custom-call(f32[256,2560]{1,0:T(8,128)} %get-tuple-element.166.adj_ref, f32[256,2560]{1,0:T(8,128)} %get-tuple-element.167.tail_ref, f32[8,2560]{1,0:T(8,128)} %broadcast_in_dim.129.hand_ref, ...), custom_call_target="tpu_custom_call" | custom-call | flops 16099999744 | bytes 1024 | tf_op jit(solution)/shard_map/mix_bwd/pallas_call | solution.py:652
  886.5 18.9 %feed_out.1 = bf16[1024,2560]{1,0:T(8,128)(2,1)} custom-call(s32[1]{0:T(128)} %bitcast.42.lane_ref, bf16[512,1920]{1,0:T(8,128)(2,1)} %get-tuple-element.159.refs_4_.refs_0_, bf16[512,1920]{1,0:T(8,128)(2,1)} %get-tuple-element.122.refs_5_.refs_1_, bf16[1280,1920]{1,0:T(8,128)(2,1)} %join_feats.5.refs_8_.refs_2_, ...), custom_call_target="tpu_custom_call" | custom-call | flops 20700000256 | bytes 1024 | tf_op jit(solution)/shard_map/feed_out/pallas_call | solution.py:374
  921.4 14.8 %rows_back.3 = f32[256,2560]{1,0:T(8,128)} custom-call(bf16[256,2560]{1,0:T(8,128)(2,1)} %get-tuple-element.175.refs_1_.refs_0_, bf16[256,2560]{1,0:T(8,128)(2,1)} %get-tuple-element.158.refs_1_, bf16[4,1280,640]{2,1,0:T(8,128)(2,1)} %join_lanes.3.own_ref.refs_2_, bf16[4,1280,640]{2,1,0:T(8,128)(2,1)} %collective-permute-done.13.other_ref.refs_3_, ...), custom_call_target="tpu_custom_call" | custom-call | flops 21849999360 | bytes 1024 | tf_op jit(solution)/shard_map/rows_back/pallas_call | solution.py:244
  993.9 17.1 %collective-permute-done.86 = f32[16,2560]{1,0:T(8,128)S(1)} collective-permute-done((f32[16,2560]{1,0:T(8,128)S(1)}, f32[16,2560]{1,0:T(8,128)S(1)}, u32[]{:S(2)}, u32[]{:S(2)}) %collective-permute-start.86) | collective-permute-done | bytes 163872 | tf_op jit(solution)/shard_map/ppermute | solution.py:1021
  1067.0 46.6 %collective-permute-done.69 = bf16[2,64,2560]{2,1,0:T(8,128)(2,1)S(1)} collective-permute-done((bf16[2,64,2560]{2,1,0:T(8,128)(2,1)S(1)}, bf16[2,64,2560]{2,1,0:T(8,128)(2,1)S(1)}, u32[]{:S(2)}, u32[]{:S(2)}) %collective-permute-start.69) | collective-permute-done | bytes 655392 | tf_op jit(solution)/shard_map/ppermute | solution.py:735
  1141.0 11.4 reduce-scatter.8.cloned.1.call-done
  (592 shorter events, 588.8 us)
Async XLA Ops:
  7.2 63.8 %all-gather.13.cloned.1.call-start = ((), (), s32[]{:S(2)}) async-start(), calls=%async_computation.13 | async-start | bytes 2048000 | tf_op jit(solution)/shard_map/all_gather | solution.py:852
  7.9 129.4 %all-gather.15.cloned.1.call-start = ((), (), s32[]{:S(2)}) async-start(), calls=%async_computation.14 | async-start | bytes 2048000 | tf_op jit(solution)/shard_map/all_gather | solution.py:852
  8.7 191.9 %all-gather.17.cloned.1.call-start = ((), (), s32[]{:S(2)}) async-start(), calls=%async_computation.15 | async-start | bytes 2048000 | tf_op jit(solution)/shard_map/all_gather | solution.py:852
  8.7 63.3 %collective-permute-start.17 = (bf16[1,320,1920]{2,1,0:T(8,128)(2,1)}, bf16[1,320,1920]{2,1,0:T(8,128)(2,1)}, u32[]{:S(2)}, u32[]{:S(2)}) collective-permute-start(bf16[1,320,1920]{2,1,0:T(8,128)(2,1)} %bitcast.189), channel_id=1, source_target_pairs={{0,16},{4,20},{8,24},{12,28},{16,0},{20,4},{24,8},{28,12},{1,17},{... | collective-permute-start | bytes 3686408 | tf_op jit(solution)/shard_map/ppermute | solution.py:735
  11.8 63.1 %collective-permute-start.19 = (bf16[1,320,1920]{2,1,0:T(8,128)(2,1)}, bf16[1,320,1920]{2,1,0:T(8,128)(2,1)}, u32[]{:S(2)}, u32[]{:S(2)}) collective-permute-start(bf16[1,320,1920]{2,1,0:T(8,128)(2,1)} %bitcast.190), channel_id=1, source_target_pairs={{0,8},{4,12},{8,0},{12,4},{16,24},{20,28},{24,16},{28,20},{1,9},{5... | collective-permute-start | bytes 3686408 | tf_op jit(solution)/shard_map/ppermute | solution.py:735
  17.6 267.3 %all-gather.9.cloned.1.call-start = ((), (), s32[]{:S(2)}) async-start(), calls=%async_computation.5 | async-start | bytes 2949120 | tf_op jit(solution)/shard_map/all_gather | solution.py:857
  32.3 425.0 %all-gather.11.cloned.1.call-start = ((), (), s32[]{:S(2)}) async-start(), calls=%async_computation.6 | async-start | bytes 6553600 | tf_op jit(solution)/shard_map/all_gather | solution.py:860
  72.0 52.0 %collective-permute-start.1 = (bf16[1,128,2560]{2,1,0:T(8,128)(2,1)S(1)}, bf16[1,128,2560]{2,1,0:T(8,128)(2,1)S(1)}, u32[]{:S(2)}, u32[]{:S(2)}) collective-permute-start(bf16[1,128,2560]{2,1,0:T(8,128)(2,1)S(1)} %get-tuple-element.226), channel_id=1, source_target_pairs={{0,16},{4,20},{8,24},{12,28},{16,0},{20,4},{24,8},{28,12},{1,17},{... | collective-permute-start | bytes 1966088 | tf_op jit(solution)/shard_map/ppermute | solution.py:735
  74.9 59.5 %collective-permute-start.18 = (bf16[1,160,1920]{2,1,0:T(8,128)(2,1)S(1)}, bf16[1,160,1920]{2,1,0:T(8,128)(2,1)S(1)}, u32[]{:S(2)}, u32[]{:S(2)}) collective-permute-start(bf16[1,160,1920]{2,1,0:T(8,128)(2,1)S(1)} %slice.408), channel_id=1, source_target_pairs={{0,8},{4,12},{8,0},{12,4},{16,24},{20,28},{24,16},{28,20},{1,9},{5... | collective-permute-start | bytes 1843208 | tf_op jit(solution)/shard_map/ppermute | solution.py:735
  86.1 51.2 %collective-permute-start.20 = (bf16[1,160,1920]{2,1,0:T(8,128)(2,1)S(1)}, bf16[1,160,1920]{2,1,0:T(8,128)(2,1)}, u32[]{:S(2)}, u32[]{:S(2)}) collective-permute-start(bf16[1,160,1920]{2,1,0:T(8,128)(2,1)S(1)} %slice.409), channel_id=1, source_target_pairs={{0,16},{4,20},{8,24},{12,28},{16,0},{20,4},{24,8},{28,12},{1,17},{... | collective-permute-start | bytes 1843208 | tf_op jit(solution)/shard_map/ppermute | solution.py:735
  110.0 58.3 %collective-permute-start.28 = (bf16[4,32,2560]{2,1,0:T(8,128)(2,1)}, bf16[4,32,2560]{2,1,0:T(8,128)(2,1)}, u32[]{:S(2)}, u32[]{:S(2)}) collective-permute-start(bf16[4,32,2560]{2,1,0:T(8,128)(2,1)} %get-tuple-element.218), channel_id=1, source_target_pairs={{0,4},{4,0},{8,12},{12,8},{16,20},{20,16},{24,28},{28,24},{1,5},{5... | collective-permute-start | bytes 1966088 | tf_op jit(solution)/shard_map/ppermute | solution.py:735
  135.2 66.7 %collective-permute-start.2 = (bf16[4,32,2560]{2,1,0:T(8,128)(2,1)}, bf16[4,32,2560]{2,1,0:T(8,128)(2,1)}, u32[]{:S(2)}, u32[]{:S(2)}) collective-permute-start(bf16[4,32,2560]{2,1,0:T(8,128)(2,1)} %get-tuple-element.224), channel_id=1, source_target_pairs={{0,4},{4,0},{8,12},{12,8},{16,20},{20,16},{24,28},{28,24},{1,5},{5... | collective-permute-start | bytes 1966088 | tf_op jit(solution)/shard_map/ppermute | solution.py:735
  137.3 59.5 %collective-permute-start.22 = (bf16[1,4,320,640]{3,2,1,0:T(8,128)(2,1)}, bf16[1,4,320,640]{3,2,1,0:T(8,128)(2,1)}, u32[]{:S(2)}, u32[]{:S(2)}) collective-permute-start(bf16[1,4,320,640]{3,2,1,0:T(8,128)(2,1)} %bitcast.181), channel_id=1, source_target_pairs={{0,16},{4,20},{8,24},{12,28},{16,0},{20,4},{24,8},{28,12},{1,17},{... | collective-permute-start | bytes 4915208 | tf_op jit(solution)/shard_map/ppermute | solution.py:735
  168.2 120.1 %collective-permute-start.13 = (bf16[4,1280,640]{2,1,0:T(8,128)(2,1)}, bf16[4,1280,640]{2,1,0:T(8,128)(2,1)}, u32[]{:S(2)}, u32[]{:S(2)}) collective-permute-start(bf16[4,1280,640]{2,1,0:T(8,128)(2,1)} %join_lanes.3.own_ref.refs_2_), channel_id=1, source_target_pairs={{0,4},{4,0},{8,12},{12,8},{16,20},{20,16},{24,28},{28,24},{1,5},{5... | collective-permute-start | bytes 19660808 | tf_op jit(solution)/shard_map/ppermute | solution.py:735
  201.9 52.2 %collective-permute-start.29 = (bf16[1,4,320,640]{3,2,1,0:T(8,128)(2,1)}, bf16[1,4,320,640]{3,2,1,0:T(8,128)(2,1)}, u32[]{:S(2)}, u32[]{:S(2)}) collective-permute-start(bf16[1,4,320,640]{3,2,1,0:T(8,128)(2,1)} %bitcast.179), channel_id=1, source_target_pairs={{0,8},{4,12},{8,0},{12,4},{16,24},{20,28},{24,16},{28,20},{1,9},{5... | collective-permute-start | bytes 4915208 | tf_op jit(solution)/shard_map/ppermute | solution.py:735
  227.2 93.6 %collective-permute-start.25 = (bf16[4,1280,640]{2,1,0:T(8,128)(2,1)}, bf16[4,1280,640]{2,1,0:T(8,128)(2,1)}, u32[]{:S(2)}, u32[]{:S(2)}) collective-permute-start(bf16[4,1280,640]{2,1,0:T(8,128)(2,1)} %join_lanes.4.own_ref.refs_4_), channel_id=1, source_target_pairs={{0,4},{4,0},{8,12},{12,8},{16,20},{20,16},{24,28},{28,24},{1,5},{5... | collective-permute-start | bytes 19660808 | tf_op jit(solution)/shard_map/ppermute | solution.py:735
  277.4 63.1 %collective-permute-start.33 = (bf16[4,1280,640]{2,1,0:T(8,128)(2,1)}, bf16[4,1280,640]{2,1,0:T(8,128)(2,1)}, u32[]{:S(2)}, u32[]{:S(2)}) collective-permute-start(bf16[4,1280,640]{2,1,0:T(8,128)(2,1)} %join_lanes.5.refs_1_.own_ref), channel_id=1, source_target_pairs={{0,4},{4,0},{8,12},{12,8},{16,20},{20,16},{24,28},{28,24},{1,5},{5... | collective-permute-start | bytes 19660808 | tf_op jit(solution)/shard_map/ppermute | solution.py:735
  284.9 707.1 %reduce-scatter.14.cloned.1.call-start = ((), (), s32[]{:S(2)}) async-start(), calls=%async_computation.12 | async-start | bytes 2048000 | tf_op jit(solution)/shard_map/reduce_scatter | solution.py:977
  332.7 54.5 %collective-permute-start.36 = (bf16[1,320,1920]{2,1,0:T(8,128)(2,1)}, bf16[1,320,1920]{2,1,0:T(8,128)(2,1)}, u32[]{:S(2)}, u32[]{:S(2)}) collective-permute-start(bf16[1,320,1920]{2,1,0:T(8,128)(2,1)} %bitcast.43.own_ref), channel_id=1, source_target_pairs={{0,8},{4,12},{8,0},{12,4},{16,24},{20,28},{24,16},{28,20},{1,9},{5... | collective-permute-start | bytes 3686408 | tf_op jit(solution)/shard_map/ppermute | solution.py:735
  353.7 55.9 %collective-permute-start.34 = (bf16[256,2560]{1,0:T(8,128)(2,1)S(1)}, bf16[256,2560]{1,0:T(8,128)(2,1)S(1)}, u32[]{:S(2)}, u32[]{:S(2)}) collective-permute-start(bf16[256,2560]{1,0:T(8,128)(2,1)S(1)} %multiply_convert_fusion.refs_0_), channel_id=1, source_target_pairs={{0,1},{1,2},{2,3},{3,0},{4,5},{5,6},{6,7},{7,4},{8,9},{9,10},{10,1... | collective-permute-start | bytes 3932168 | tf_op jit(solution)/shard_map/ppermute | solution.py:738
  775.2 79.9 %collective-permute-start.72 = (bf16[4,1280,640]{2,1,0:T(8,128)(2,1)}, bf16[4,1280,640]{2,1,0:T(8,128)(2,1)}, u32[]{:S(2)}, u32[]{:S(2)}) collective-permute-start(bf16[4,1280,640]{2,1,0:T(8,128)(2,1)} %weight_grad.20), channel_id=1, source_target_pairs={{0,4},{4,0},{8,12},{12,8},{16,20},{20,16},{24,28},{28,24},{1,5},{5... | collective-permute-start | bytes 19660808 | tf_op jit(solution)/shard_map/ppermute | solution.py:735
  837.2 180.8 %reduce-scatter.12.cloned.1.call-start = ((), (), s32[]{:S(2)}) async-start(), calls=%async_computation.10 | async-start | bytes 2949120 | tf_op jit(solution)/shard_map/reduce_scatter | solution.py:1013
  880.7 151.0 %reduce-scatter.6.cloned.1.call-start = ((), (), s32[]{:S(2)}) async-start(), calls=%async_computation.7 | async-start | bytes 6553600 | tf_op jit(solution)/shard_map/reduce_scatter | solution.py:989
  905.4 227.9 %all-reduce.4.cloned.1.call-start = ((), (), s32[]{:S(2)}) async-start(), calls=%async_computation.11 | async-start | bytes 655360 | tf_op jit(solution)/shard_map/psum | solution.py:1014
  905.5 56.3 %collective-permute-start.88 = (bf16[1,4,160,640]{3,2,1,0:T(8,128)(2,1)}, bf16[1,4,160,640]{3,2,1,0:T(8,128)(2,1)}, u32[]{:S(2)}, u32[]{:S(2)}) collective-permute-start(bf16[1,4,160,640]{3,2,1,0:T(8,128)(2,1)} %get-tuple-element.165), channel_id=1, source_target_pairs={{0,16},{4,20},{8,24},{12,28},{16,0},{20,4},{24,8},{28,12},{1,17},{... | collective-permute-start | bytes 2457608 | tf_op jit(solution)/shard_map/ppermute | solution.py:735
  906.9 59.3 %collective-permute-start.87 = (bf16[1,4,160,640]{3,2,1,0:T(8,128)(2,1)}, bf16[1,4,160,640]{3,2,1,0:T(8,128)(2,1)}, u32[]{:S(2)}, u32[]{:S(2)}) collective-permute-start(bf16[1,4,160,640]{3,2,1,0:T(8,128)(2,1)} %get-tuple-element.164), channel_id=1, source_target_pairs={{0,8},{4,12},{8,0},{12,4},{16,24},{20,28},{24,16},{28,20},{1,9},{5... | collective-permute-start | bytes 2457608 | tf_op jit(solution)/shard_map/ppermute | solution.py:735
  921.4 112.9 %collective-permute-start.89 = (bf16[4,1280,640]{2,1,0:T(8,128)(2,1)}, bf16[4,1280,640]{2,1,0:T(8,128)(2,1)}, u32[]{:S(2)}, u32[]{:S(2)}) collective-permute-start(bf16[4,1280,640]{2,1,0:T(8,128)(2,1)} %weight_grad.22), channel_id=1, source_target_pairs={{0,4},{4,0},{8,12},{12,8},{16,20},{20,16},{24,28},{28,24},{1,5},{5... | collective-permute-start | bytes 19660808 | tf_op jit(solution)/shard_map/ppermute | solution.py:735
  964.4 53.6 %collective-permute-start.94 = (bf16[1,4,320,640]{3,2,1,0:T(8,128)(2,1)}, bf16[1,4,320,640]{3,2,1,0:T(8,128)(2,1)S(1)}, u32[]{:S(2)}, u32[]{:S(2)}) collective-permute-start(bf16[1,4,320,640]{3,2,1,0:T(8,128)(2,1)} %pad_maximum_fusion.5), channel_id=1, source_target_pairs={{0,8},{4,12},{8,0},{12,4},{16,24},{20,28},{24,16},{28,20},{1,9},{5... | collective-permute-start | bytes 4915208 | tf_op jit(solution)/shard_map/ppermute | solution.py:735
  1018.0 117.3 %reduce-scatter.10.cloned.1.call-start = ((), (), s32[]{:S(2)}) async-start(), calls=%async_computation.9 | async-start | bytes 2048000 | tf_op jit(solution)/shard_map/reduce_scatter | solution.py:977
  1023.7 128.8 %reduce-scatter.8.cloned.1.call-start = ((), (), s32[]{:S(2)}) async-start(), calls=%async_computation.8 | async-start | bytes 2048000 | tf_op jit(solution)/shard_map/reduce_scatter | solution.py:977
  1062.6 51.1 %collective-permute-start.91 = (bf16[1,4,320,640]{3,2,1,0:T(8,128)(2,1)S(1)}, bf16[1,4,320,640]{3,2,1,0:T(8,128)(2,1)S(1)}, u32[]{:S(2)}, u32[]{:S(2)}) collective-permute-start(bf16[1,4,320,640]{3,2,1,0:T(8,128)(2,1)S(1)} %pad_maximum_fusion.3), channel_id=1, source_target_pairs={{0,8},{4,12},{8,0},{12,4},{16,24},{20,28},{24,16},{28,20},{1,9},{5... | collective-permute-start | bytes 4915208 | tf_op jit(solution)/shard_map/ppermute | solution.py:735
  1066.9 52.2 %collective-permute-start.81 = (bf16[4,32,2560]{2,1,0:T(8,128)(2,1)S(1)}, bf16[4,32,2560]{2,1,0:T(8,128)(2,1)S(1)}, u32[]{:S(2)}, u32[]{:S(2)}) collective-permute-start(bf16[4,32,2560]{2,1,0:T(8,128)(2,1)S(1)} %get-tuple-element.206), channel_id=1, source_target_pairs={{0,4},{4,0},{8,12},{12,8},{16,20},{20,16},{24,28},{28,24},{1,5},{5... | collective-permute-start | bytes 1966088 | tf_op jit(solution)/shard_map/ppermute | solution.py:735
  (164 other events, 2789.3 us)
Sparse Core Ops, SparseCore 0:
  9.6 41.0 all-gather.12
  52.3 37.0 all-gather.14
  91.0 37.0 all-gather.16
  130.3 45.7 all-gather.8
  285.0 124.0 all-gather.10
  837.3 36.5 reduce-scatter.13
  880.8 47.5 reduce-scatter.11
  930.8 100.8 reduce-scatter.5
  1034.1 36.6 all-reduce.3
  1073.0 36.0 reduce-scatter.9
  1115.7 36.7 reduce-scatter.7

commit v3 on v2

--- a/solution.py
+++ b/solution.py
@@ -982,7 +982,14 @@
     own_out = own_half([g1], [mixed], other_out, gm, far_up, **by_lane)
     far_out = reduce_far(own_out)
     gy_low, adj_loc, tail, edge_back = mix_adj(after(gm, own_out), by, state, conv_low, off_ext, vec, rate_t)
-    hand = carry_in(edge_back, -1)
+    hand_got = shift(edge_back, -1)
+    span = 1
+    while span < lanes - 1:
+        hand_far = shift(hand_got, -span)
+        rows01 = [hand_got[0:1] + hand_got[1:2] * hand_far[0:1], hand_got[1:2] * hand_far[1:2]]
+        hand_got = jnp.concatenate(rows01 + [jnp.zeros((6, lru_total), f32)], axis=0)
+        span *= 2
+    hand = jnp.broadcast_to(hand_got[0:1], (8, lru_total))
     other_y = other_half([normed_low], [gy_low], near_up, **by_lane)
     near_out = reduce_near(own_out, far_out)
     feed_sum = feed_out([after(hidden[0], other_y, far_out)] + hidden[1:], wd, lane, lanes)

time: 1180 us -> 1170 us (level)
  no operation moved by 1% of the time
where the time goes in v3:
time: 1170 us; the launch traced here: 1160 us
  waiting for transfers between devices  471 us (40%)
  Pallas kernels  432 us (37%)
  starting transfers between devices  98.1 us (8%)
  other arithmetic  77.7 us (7%)
  local copies, waits for them, and re-layouts  61.4 us (5%)
  between operations  17.1 us (1%)
    ppermute x78, waiting for transfers between devices, swap(): return lax.ppermute(x, 'dp', [(i, i ^ 1 << bit) for i in range(groups)])  351 us
    pallas_call x12, Pallas kernels, weight_grad(): pl.pallas_call(kernel, grid_spec=pltpu.PrefetchScalarGridSpec(num_scalar_...  106 us
    ppermute x78, starting transfers between devices, swap(): return lax.ppermute(x, 'dp', [(i, i ^ 1 << bit) for i in range(groups)])  68.8 us
    pallas_call x4, Pallas kernels, feed_back(): pl.pallas_call(kernel, grid=(2 * steps,), in_specs=specs, out_specs=pl.Bl...  53.8 us
    ppermute x7, waiting for transfers between devices, up(): lax.ppermute(x, 'tensor', [(i, (i + 1) % lanes) for i in range(lanes)])  53.8 us
    pallas_call x2, Pallas kernels, feed_pair(): pl.pallas_call(kernel, grid_spec=pltpu.PrefetchScalarGridSpec(num_scalar_...  53.6 us
    pallas_call x6, Pallas kernels, turn_feats(): pl.pallas_call(_turn_kernel, grid=(width // tile,), in_specs=[pl.BlockSpe...  34 us
    pallas_call x3, Pallas kernels, rows_into(): pl.pallas_call(kernel, grid=(lanes,), in_specs=[pl.BlockSpec((rows, width...  28.5 us
  transfers between devices with their start and end apart: 107, of which 50 were waited for; matrix products, arithmetic and copies ran while one was open for 10% of the time, Pallas kernels for 31%

profile of v3, /device:TPU:0, one launch (start us, length us, event | category | flops | bytes accessed | tf_op | source)
XLA Modules:
  0.0 1157.2 jit_solution(13956583362263688756)
XLA Ops:
  87.5 22.4 %collective-permute-done.10.y_ref = bf16[1,4,320,640]{3,2,1,0:T(8,128)(2,1)S(1)} collective-permute-done((bf16[1,4,320,640]{3,2,1,0:T(8,128)(2,1)}, bf16[1,4,320,640]{3,2,1,0:T(8,128)(2,1)S(1)}, u32[]{:S(2)}, u32[]{:S(2)}) %collective-permute-start.10) | collective-permute-done | bytes 1638432 | tf_op jit(solution)/shard_map/ppermute | solution.py:735
  110.0 11.2 collective-permute-done.9.x_ref
  137.8 14.7 %collective-permute-done.11.low_ref = bf16[1,4,160,640]{3,2,1,0:T(8,128)(2,1)} collective-permute-done((bf16[1,4,160,640]{3,2,1,0:T(8,128)(2,1)S(1)}, bf16[1,4,160,640]{3,2,1,0:T(8,128)(2,1)}, u32[]{:S(2)}, u32[]{:S(2)}) %collective-permute-start.11) | collective-permute-done | bytes 819232 | tf_op jit(solution)/shard_map/ppermute | solution.py:735
  179.5 17.3 %collective-permute-done.22.y_ref = bf16[1,4,320,640]{3,2,1,0:T(8,128)(2,1)} collective-permute-done((bf16[1,4,320,640]{3,2,1,0:T(8,128)(2,1)}, bf16[1,4,320,640]{3,2,1,0:T(8,128)(2,1)}, u32[]{:S(2)}, u32[]{:S(2)}) %collective-permute-start.22) | collective-permute-done | bytes 1638432 | tf_op jit(solution)/shard_map/ppermute | solution.py:735
  229.7 21.6 %collective-permute-done.30.y_ref = bf16[1,4,320,640]{3,2,1,0:T(8,128)(2,1)} collective-permute-done((bf16[1,4,320,640]{3,2,1,0:T(8,128)(2,1)}, bf16[1,4,320,640]{3,2,1,0:T(8,128)(2,1)}, u32[]{:S(2)}, u32[]{:S(2)}) %collective-permute-start.30) | collective-permute-done | bytes 1638432 | tf_op jit(solution)/shard_map/ppermute | solution.py:735
  298.5 12.3 %mix_fwd.1 = (bf16[256,2560]{1,0:T(8,128)(2,1)}, f32[256,2560]{1,0:T(8,128)}, f32[256,2560]{1,0:T(8,128)}) custom-call(f32[264,2560]{1,0:T(8,128)} %rows_into.3.bx_ref, s32[264,1]{1,0:T(8,128)} %subtract_select_fusion.off_ref, f32[16,2560]{1,0:T(8,128)} %maximum_maximum_fusion.vec_ref, bf16[10,256,256]{2,1,0:T(8,128)(2,1)} %get-tuple-element.204.rate_ref, ...), custom_call_target="tpu_custom_call" | custom-call | flops 13799999488 | bytes 1024 | tf_op jit(solution)/shard_map/mix_fwd/pallas_call | solution.py:532
  364.0 13.3 %collective-permute-done.37.y_ref = bf16[1,320,1920]{2,1,0:T(8,128)(2,1)S(1)} collective-permute-done((bf16[1,320,1920]{2,1,0:T(8,128)(2,1)}, bf16[1,320,1920]{2,1,0:T(8,128)(2,1)S(1)}, u32[]{:S(2)}, u32[]{:S(2)}) %collective-permute-start.37) | collective-permute-done | bytes 1228832 | tf_op jit(solution)/shard_map/ppermute | solution.py:735
  396.0 13.6 %collective-permute-done.34.refs_1_ = bf16[256,2560]{1,0:T(8,128)(2,1)S(1)} collective-permute-done((bf16[256,2560]{1,0:T(8,128)(2,1)S(1)}, bf16[256,2560]{1,0:T(8,128)(2,1)S(1)}, u32[]{:S(2)}, u32[]{:S(2)}) %collective-permute-start.34) | collective-permute-done | bytes 1310752 | tf_op jit(solution)/shard_map/ppermute | solution.py:738
  426.2 30.4 %collective-permute-done.46.refs_0_.refs_2_ = bf16[256,2560]{1,0:T(8,128)(2,1)S(1)} collective-permute-done((bf16[256,2560]{1,0:T(8,128)(2,1)S(1)}, bf16[256,2560]{1,0:T(8,128)(2,1)S(1)}, u32[]{:S(2)}, u32[]{:S(2)}) %collective-permute-start.46) | collective-permute-done | bytes 1310752 | tf_op jit(solution)/shard_map/ppermute | solution.py:738
  457.4 26.8 %feed_pair.2 = (bf16[512,1920]{1,0:T(8,128)(2,1)}, bf16[512,1920]{1,0:T(8,128)(2,1)}, bf16[512,1920]{1,0:T(8,128)(2,1)}) custom-call(s32[1]{0:T(128)} %bitcast.42.lane_ref, bf16[256,2560]{1,0:T(8,128)(2,1)} %copy-done.21, bf16[256,2560]{1,0:T(8,128)(2,1)} %copy-done.69, bf16[1024,2560]{1,0:T(8,128)(2,1)} %all-gather.11.cloned.1.call-done.refs_2_.refs_3_.refs_0_.refs_1_, ...), custom_call_target="tpu_custom_call" | custom-call | flops 31050000384 | bytes 1024 | tf_op jit(solution)/shard_map/feed_pair/pallas_call | solution.py:294
  484.1 13.3 %feed_back.4 = bf16[256,2560]{1,0:T(8,128)(2,1)} custom-call(bf16[512,1920]{1,0:T(8,128)(2,1)} %get-tuple-element.144.refs_0_.refs_4_, bf16[512,1920]{1,0:T(8,128)(2,1)} %get-tuple-element.138.refs_1_.refs_4_, bf16[1280,1920]{1,0:T(8,128)(2,1)} %join_feats.3.refs_4_.refs_2_, bf16[1280,1920]{1,0:T(8,128)(2,1)} %collective-permute-done.35.refs_5_.refs_3_, ...), custom_call_target="tpu_custom_call" | custom-call | flops 14949999616 | bytes 1024 | tf_op jit(solution)/shard_map/feed_back/pallas_call | solution.py:339
  501.1 26.8 %feed_pair.3 = (bf16[512,1920]{1,0:T(8,128)(2,1)}, bf16[512,1920]{1,0:T(8,128)(2,1)}, bf16[512,1920]{1,0:T(8,128)(2,1)}) custom-call(s32[1]{0:T(128)} %bitcast.42.lane_ref, bf16[256,2560]{1,0:T(8,128)(2,1)} %copy-done.70, bf16[256,2560]{1,0:T(8,128)(2,1)} %copy-done.71, bf16[1024,2560]{1,0:T(8,128)(2,1)} %all-gather.11.cloned.1.call-done.refs_2_.refs_3_.refs_0_.refs_1_, ...), custom_call_target="tpu_custom_call" | custom-call | flops 31050000384 | bytes 1024 | tf_op jit(solution)/shard_map/feed_pair/pallas_call | solution.py:294
  531.0 13.4 %feed_back.5 = bf16[256,2560]{1,0:T(8,128)(2,1)} custom-call(bf16[512,1920]{1,0:T(8,128)(2,1)} %get-tuple-element.137.refs_0_.refs_5_, bf16[512,1920]{1,0:T(8,128)(2,1)} %get-tuple-element.120.refs_1_.refs_5_, bf16[1280,1920]{1,0:T(8,128)(2,1)} %join_feats.3.refs_4_.refs_2_, bf16[1280,1920]{1,0:T(8,128)(2,1)} %collective-permute-done.35.refs_5_.refs_3_, ...), custom_call_target="tpu_custom_call" | custom-call | flops 14949999616 | bytes 1024 | tf_op jit(solution)/shard_map/feed_back/pallas_call | solution.py:339
  544.3 10.4 weight_grad.12
  566.2 10.8 weight_grad.14
  582.5 10.8 weight_grad.15
  598.5 13.3 %feed_back.6 = bf16[256,2560]{1,0:T(8,128)(2,1)} custom-call(bf16[512,1920]{1,0:T(8,128)(2,1)} %get-tuple-element.137.refs_0_.refs_5_, bf16[512,1920]{1,0:T(8,128)(2,1)} %get-tuple-element.120.refs_1_.refs_5_, bf16[1280,1920]{1,0:T(8,128)(2,1)} %join_feats.3.refs_4_.refs_2_, bf16[1280,1920]{1,0:T(8,128)(2,1)} %collective-permute-done.35.refs_5_.refs_3_, ...), custom_call_target="tpu_custom_call" | custom-call | flops 14949999616 | bytes 1024 | tf_op jit(solution)/shard_map/feed_back/pallas_call | solution.py:339
  611.9 10.5 weight_grad.16
  627.9 11.0 collective-permute-done.51
  642.1 11.2 weight_grad.17
  653.3 13.2 %collective-permute-done.58 = bf16[1,320,1920]{2,1,0:T(8,128)(2,1)S(1)} collective-permute-done((bf16[1,320,1920]{2,1,0:T(8,128)(2,1)S(1)}, bf16[1,320,1920]{2,1,0:T(8,128)(2,1)S(1)}, u32[]{:S(2)}, u32[]{:S(2)}) %collective-permute-start.58) | collective-permute-done | bytes 1228832 | tf_op jit(solution)/shard_map/ppermute | solution.py:735
  667.9 13.8 %feed_back.7 = f32[256,2560]{1,0:T(8,128)} custom-call(bf16[512,1920]{1,0:T(8,128)(2,1)} %get-tuple-element.144.refs_0_.refs_4_, bf16[512,1920]{1,0:T(8,128)(2,1)} %get-tuple-element.138.refs_1_.refs_4_, bf16[1280,1920]{1,0:T(8,128)(2,1)} %join_feats.3.refs_4_.refs_2_, bf16[1280,1920]{1,0:T(8,128)(2,1)} %collective-permute-done.35.refs_5_.refs_3_, ...), custom_call_target="tpu_custom_call" | custom-call | flops 14949999616 | bytes 1024 | tf_op jit(solution)/shard_map/feed_back/pallas_call | solution.py:339
  700.3 25.1 %collective-permute-done.61 = bf16[1,320,1920]{2,1,0:T(8,128)(2,1)} collective-permute-done((bf16[1,320,1920]{2,1,0:T(8,128)(2,1)S(1)}, bf16[1,320,1920]{2,1,0:T(8,128)(2,1)}, u32[]{:S(2)}, u32[]{:S(2)}) %collective-permute-start.61) | collective-permute-done | bytes 1228832 | tf_op jit(solution)/shard_map/ppermute | solution.py:735
  749.8 13.2 %mix_adj.1 = (bf16[256,2560]{1,0:T(8,128)(2,1)}, f32[256,2560]{1,0:T(8,128)}, f32[256,2560]{1,0:T(8,128)}, f32[8,2560]{1,0:T(8,128)}) custom-call(f32[256,2560]{1,0:T(8,128)} %rows_into.5.gm_ref, f32[256,2560]{1,0:T(8,128)} %rows_into.4.by_ref, f32[256,2560]{1,0:T(8,128)} %get-tuple-element.155.full_ref, bf16[256,2560]{1,0:T(8,128)(2,1)} %get-tuple-element.156.conv_ref, ...), custom_call_target="tpu_custom_call" | custom-call | flops 14949999616 | bytes 1024 | tf_op jit(solution)/shard_map/mix_adj/pallas_call | solution.py:595
  777.9 18.0 %collective-permute-done.67 = bf16[1,4,160,640]{3,2,1,0:T(8,128)(2,1)S(1)} collective-permute-done((bf16[1,4,160,640]{3,2,1,0:T(8,128)(2,1)S(1)}, bf16[1,4,160,640]{3,2,1,0:T(8,128)(2,1)S(1)}, u32[]{:S(2)}, u32[]{:S(2)}) %collective-permute-start.67) | collective-permute-done | bytes 819232 | tf_op jit(solution)/shard_map/ppermute | solution.py:735
  806.8 26.9 %collective-permute-done.78 = bf16[1,4,320,640]{3,2,1,0:T(8,128)(2,1)S(1)} collective-permute-done((bf16[1,4,320,640]{3,2,1,0:T(8,128)(2,1)S(1)}, bf16[1,4,320,640]{3,2,1,0:T(8,128)(2,1)S(1)}, u32[]{:S(2)}, u32[]{:S(2)}) %collective-permute-start.78) | collective-permute-done | bytes 1638432 | tf_op jit(solution)/shard_map/ppermute | solution.py:735
  857.8 14.0 %mix_bwd.1 = (f32[256,2560]{1,0:T(8,128)}, bf16[10,256,256]{2,1,0:T(8,128)(2,1)}, bf16[10,256,256]{2,1,0:T(8,128)(2,1)}, f32[8,2560]{1,0:T(8,128)}) custom-call(f32[256,2560]{1,0:T(8,128)} %get-tuple-element.166.adj_ref, f32[256,2560]{1,0:T(8,128)} %get-tuple-element.167.tail_ref, f32[8,2560]{1,0:T(8,128)} %broadcast_in_dim.129.hand_ref, ...), custom_call_target="tpu_custom_call" | custom-call | flops 16099999744 | bytes 1024 | tf_op jit(solution)/shard_map/mix_bwd/pallas_call | solution.py:652
  880.9 19.0 %feed_out.1 = bf16[1024,2560]{1,0:T(8,128)(2,1)} custom-call(s32[1]{0:T(128)} %bitcast.42.lane_ref, bf16[512,1920]{1,0:T(8,128)(2,1)} %get-tuple-element.159.refs_4_.refs_0_, bf16[512,1920]{1,0:T(8,128)(2,1)} %get-tuple-element.122.refs_5_.refs_1_, bf16[1280,1920]{1,0:T(8,128)(2,1)} %join_feats.5.refs_8_.refs_2_, ...), custom_call_target="tpu_custom_call" | custom-call | flops 20700000256 | bytes 1024 | tf_op jit(solution)/shard_map/feed_out/pallas_call | solution.py:374
  916.5 14.8 %rows_back.3 = f32[256,2560]{1,0:T(8,128)} custom-call(bf16[256,2560]{1,0:T(8,128)(2,1)} %get-tuple-element.175.refs_1_.refs_0_, bf16[256,2560]{1,0:T(8,128)(2,1)} %get-tuple-element.158.refs_1_, bf16[4,1280,640]{2,1,0:T(8,128)(2,1)} %join_lanes.3.own_ref.refs_2_, bf16[4,1280,640]{2,1,0:T(8,128)(2,1)} %collective-permute-done.13.other_ref.refs_3_, ...), custom_call_target="tpu_custom_call" | custom-call | flops 21849999360 | bytes 1024 | tf_op jit(solution)/shard_map/rows_back/pallas_call | solution.py:244
  989.3 17.5 %collective-permute-done.86 = f32[16,2560]{1,0:T(8,128)S(1)} collective-permute-done((f32[16,2560]{1,0:T(8,128)S(1)}, f32[16,2560]{1,0:T(8,128)S(1)}, u32[]{:S(2)}, u32[]{:S(2)}) %collective-permute-start.86) | collective-permute-done | bytes 163872 | tf_op jit(solution)/shard_map/ppermute | solution.py:1028
  1062.9 46.5 %collective-permute-done.69 = bf16[2,64,2560]{2,1,0:T(8,128)(2,1)S(1)} collective-permute-done((bf16[2,64,2560]{2,1,0:T(8,128)(2,1)S(1)}, bf16[2,64,2560]{2,1,0:T(8,128)(2,1)S(1)}, u32[]{:S(2)}, u32[]{:S(2)}) %collective-permute-start.69) | collective-permute-done | bytes 655392 | tf_op jit(solution)/shard_map/ppermute | solution.py:735
  1136.7 11.6 %reduce-scatter.8.cloned.1.call-done = bf16[1,320,640]{2,1,0:T(8,128)(2,1)} async-done(((bf16[4,320,640]{2,1,0:T(8,128)(2,1)}), bf16[1,320,640]{2,1,0:T(8,128)(2,1)}) %reduce-scatter.8.cloned.1.call-update) | async-done | bytes 409616 | tf_op jit(solution)/shard_map/reduce_scatter | solution.py:977
  (594 shorter events, 591.6 us)
Async XLA Ops:
  7.2 63.8 %all-gather.13.cloned.1.call-start = ((), (), s32[]{:S(2)}) async-start(), calls=%async_computation.13 | async-start | bytes 2048000 | tf_op jit(solution)/shard_map/all_gather | solution.py:852
  7.9 129.4 %all-gather.15.cloned.1.call-start = ((), (), s32[]{:S(2)}) async-start(), calls=%async_computation.14 | async-start | bytes 2048000 | tf_op jit(solution)/shard_map/all_gather | solution.py:852
  8.7 191.9 %all-gather.17.cloned.1.call-start = ((), (), s32[]{:S(2)}) async-start(), calls=%async_computation.15 | async-start | bytes 2048000 | tf_op jit(solution)/shard_map/all_gather | solution.py:852
  8.7 63.3 %collective-permute-start.17 = (bf16[1,320,1920]{2,1,0:T(8,128)(2,1)}, bf16[1,320,1920]{2,1,0:T(8,128)(2,1)}, u32[]{:S(2)}, u32[]{:S(2)}) collective-permute-start(bf16[1,320,1920]{2,1,0:T(8,128)(2,1)} %bitcast.189), channel_id=1, source_target_pairs={{0,16},{4,20},{8,24},{12,28},{16,0},{20,4},{24,8},{28,12},{1,17},{... | collective-permute-start | bytes 3686408 | tf_op jit(solution)/shard_map/ppermute | solution.py:735
  11.8 63.1 %collective-permute-start.19 = (bf16[1,320,1920]{2,1,0:T(8,128)(2,1)}, bf16[1,320,1920]{2,1,0:T(8,128)(2,1)}, u32[]{:S(2)}, u32[]{:S(2)}) collective-permute-start(bf16[1,320,1920]{2,1,0:T(8,128)(2,1)} %bitcast.190), channel_id=1, source_target_pairs={{0,8},{4,12},{8,0},{12,4},{16,24},{20,28},{24,16},{28,20},{1,9},{5... | collective-permute-start | bytes 3686408 | tf_op jit(solution)/shard_map/ppermute | solution.py:735
  17.6 267.3 %all-gather.9.cloned.1.call-start = ((), (), s32[]{:S(2)}) async-start(), calls=%async_computation.5 | async-start | bytes 2949120 | tf_op jit(solution)/shard_map/all_gather | solution.py:857
  32.3 425.0 %all-gather.11.cloned.1.call-start = ((), (), s32[]{:S(2)}) async-start(), calls=%async_computation.6 | async-start | bytes 6553600 | tf_op jit(solution)/shard_map/all_gather | solution.py:860
  72.0 52.0 %collective-permute-start.1 = (bf16[1,128,2560]{2,1,0:T(8,128)(2,1)S(1)}, bf16[1,128,2560]{2,1,0:T(8,128)(2,1)S(1)}, u32[]{:S(2)}, u32[]{:S(2)}) collective-permute-start(bf16[1,128,2560]{2,1,0:T(8,128)(2,1)S(1)} %get-tuple-element.226), channel_id=1, source_target_pairs={{0,16},{4,20},{8,24},{12,28},{16,0},{20,4},{24,8},{28,12},{1,17},{... | collective-permute-start | bytes 1966088 | tf_op jit(solution)/shard_map/ppermute | solution.py:735
  74.9 59.5 %collective-permute-start.18 = (bf16[1,160,1920]{2,1,0:T(8,128)(2,1)S(1)}, bf16[1,160,1920]{2,1,0:T(8,128)(2,1)S(1)}, u32[]{:S(2)}, u32[]{:S(2)}) collective-permute-start(bf16[1,160,1920]{2,1,0:T(8,128)(2,1)S(1)} %slice.409), channel_id=1, source_target_pairs={{0,8},{4,12},{8,0},{12,4},{16,24},{20,28},{24,16},{28,20},{1,9},{5... | collective-permute-start | bytes 1843208 | tf_op jit(solution)/shard_map/ppermute | solution.py:735
  86.1 51.2 %collective-permute-start.20 = (bf16[1,160,1920]{2,1,0:T(8,128)(2,1)S(1)}, bf16[1,160,1920]{2,1,0:T(8,128)(2,1)}, u32[]{:S(2)}, u32[]{:S(2)}) collective-permute-start(bf16[1,160,1920]{2,1,0:T(8,128)(2,1)S(1)} %slice.410), channel_id=1, source_target_pairs={{0,16},{4,20},{8,24},{12,28},{16,0},{20,4},{24,8},{28,12},{1,17},{... | collective-permute-start | bytes 1843208 | tf_op jit(solution)/shard_map/ppermute | solution.py:735
  110.0 58.3 %collective-permute-start.28 = (bf16[4,32,2560]{2,1,0:T(8,128)(2,1)}, bf16[4,32,2560]{2,1,0:T(8,128)(2,1)}, u32[]{:S(2)}, u32[]{:S(2)}) collective-permute-start(bf16[4,32,2560]{2,1,0:T(8,128)(2,1)} %get-tuple-element.218), channel_id=1, source_target_pairs={{0,4},{4,0},{8,12},{12,8},{16,20},{20,16},{24,28},{28,24},{1,5},{5... | collective-permute-start | bytes 1966088 | tf_op jit(solution)/shard_map/ppermute | solution.py:735
  135.2 66.7 %collective-permute-start.2 = (bf16[4,32,2560]{2,1,0:T(8,128)(2,1)}, bf16[4,32,2560]{2,1,0:T(8,128)(2,1)}, u32[]{:S(2)}, u32[]{:S(2)}) collective-permute-start(bf16[4,32,2560]{2,1,0:T(8,128)(2,1)} %get-tuple-element.224), channel_id=1, source_target_pairs={{0,4},{4,0},{8,12},{12,8},{16,20},{20,16},{24,28},{28,24},{1,5},{5... | collective-permute-start | bytes 1966088 | tf_op jit(solution)/shard_map/ppermute | solution.py:735
  137.3 59.5 %collective-permute-start.22 = (bf16[1,4,320,640]{3,2,1,0:T(8,128)(2,1)}, bf16[1,4,320,640]{3,2,1,0:T(8,128)(2,1)}, u32[]{:S(2)}, u32[]{:S(2)}) collective-permute-start(bf16[1,4,320,640]{3,2,1,0:T(8,128)(2,1)} %bitcast.181), channel_id=1, source_target_pairs={{0,16},{4,20},{8,24},{12,28},{16,0},{20,4},{24,8},{28,12},{1,17},{... | collective-permute-start | bytes 4915208 | tf_op jit(solution)/shard_map/ppermute | solution.py:735
  168.2 120.1 %collective-permute-start.13 = (bf16[4,1280,640]{2,1,0:T(8,128)(2,1)}, bf16[4,1280,640]{2,1,0:T(8,128)(2,1)}, u32[]{:S(2)}, u32[]{:S(2)}) collective-permute-start(bf16[4,1280,640]{2,1,0:T(8,128)(2,1)} %join_lanes.3.own_ref.refs_2_), channel_id=1, source_target_pairs={{0,4},{4,0},{8,12},{12,8},{16,20},{20,16},{24,28},{28,24},{1,5},{5... | collective-permute-start | bytes 19660808 | tf_op jit(solution)/shard_map/ppermute | solution.py:735
  201.9 52.2 %collective-permute-start.29 = (bf16[1,4,320,640]{3,2,1,0:T(8,128)(2,1)}, bf16[1,4,320,640]{3,2,1,0:T(8,128)(2,1)}, u32[]{:S(2)}, u32[]{:S(2)}) collective-permute-start(bf16[1,4,320,640]{3,2,1,0:T(8,128)(2,1)} %bitcast.179), channel_id=1, source_target_pairs={{0,8},{4,12},{8,0},{12,4},{16,24},{20,28},{24,16},{28,20},{1,9},{5... | collective-permute-start | bytes 4915208 | tf_op jit(solution)/shard_map/ppermute | solution.py:735
  227.3 93.5 %collective-permute-start.25 = (bf16[4,1280,640]{2,1,0:T(8,128)(2,1)}, bf16[4,1280,640]{2,1,0:T(8,128)(2,1)}, u32[]{:S(2)}, u32[]{:S(2)}) collective-permute-start(bf16[4,1280,640]{2,1,0:T(8,128)(2,1)} %join_lanes.4.own_ref.refs_4_), channel_id=1, source_target_pairs={{0,4},{4,0},{8,12},{12,8},{16,20},{20,16},{24,28},{28,24},{1,5},{5... | collective-permute-start | bytes 19660808 | tf_op jit(solution)/shard_map/ppermute | solution.py:735
  277.4 63.0 %collective-permute-start.33 = (bf16[4,1280,640]{2,1,0:T(8,128)(2,1)}, bf16[4,1280,640]{2,1,0:T(8,128)(2,1)}, u32[]{:S(2)}, u32[]{:S(2)}) collective-permute-start(bf16[4,1280,640]{2,1,0:T(8,128)(2,1)} %join_lanes.5.refs_1_.own_ref), channel_id=1, source_target_pairs={{0,4},{4,0},{8,12},{12,8},{16,20},{20,16},{24,28},{28,24},{1,5},{5... | collective-permute-start | bytes 19660808 | tf_op jit(solution)/shard_map/ppermute | solution.py:735
  284.9 702.5 %reduce-scatter.14.cloned.1.call-start = ((), (), s32[]{:S(2)}) async-start(), calls=%async_computation.12 | async-start | bytes 2048000 | tf_op jit(solution)/shard_map/reduce_scatter | solution.py:977
  332.6 54.5 %collective-permute-start.36 = (bf16[1,320,1920]{2,1,0:T(8,128)(2,1)}, bf16[1,320,1920]{2,1,0:T(8,128)(2,1)}, u32[]{:S(2)}, u32[]{:S(2)}) collective-permute-start(bf16[1,320,1920]{2,1,0:T(8,128)(2,1)} %bitcast.43.own_ref), channel_id=1, source_target_pairs={{0,8},{4,12},{8,0},{12,4},{16,24},{20,28},{24,16},{28,20},{1,9},{5... | collective-permute-start | bytes 3686408 | tf_op jit(solution)/shard_map/ppermute | solution.py:735
  353.6 55.9 %collective-permute-start.34 = (bf16[256,2560]{1,0:T(8,128)(2,1)S(1)}, bf16[256,2560]{1,0:T(8,128)(2,1)S(1)}, u32[]{:S(2)}, u32[]{:S(2)}) collective-permute-start(bf16[256,2560]{1,0:T(8,128)(2,1)S(1)} %multiply_convert_fusion.refs_0_), channel_id=1, source_target_pairs={{0,1},{1,2},{2,3},{3,0},{4,5},{5,6},{6,7},{7,4},{8,9},{9,10},{10,1... | collective-permute-start | bytes 3932168 | tf_op jit(solution)/shard_map/ppermute | solution.py:738
  775.2 74.5 %collective-permute-start.72 = (bf16[4,1280,640]{2,1,0:T(8,128)(2,1)}, bf16[4,1280,640]{2,1,0:T(8,128)(2,1)}, u32[]{:S(2)}, u32[]{:S(2)}) collective-permute-start(bf16[4,1280,640]{2,1,0:T(8,128)(2,1)} %weight_grad.20), channel_id=1, source_target_pairs={{0,4},{4,0},{8,12},{12,8},{16,20},{20,16},{24,28},{28,24},{1,5},{5... | collective-permute-start | bytes 19660808 | tf_op jit(solution)/shard_map/ppermute | solution.py:735
  837.1 176.1 %reduce-scatter.12.cloned.1.call-start = ((), (), s32[]{:S(2)}) async-start(), calls=%async_computation.10 | async-start | bytes 2949120 | tf_op jit(solution)/shard_map/reduce_scatter | solution.py:1020
  875.2 152.4 %reduce-scatter.6.cloned.1.call-start = ((), (), s32[]{:S(2)}) async-start(), calls=%async_computation.7 | async-start | bytes 6553600 | tf_op jit(solution)/shard_map/reduce_scatter | solution.py:996
  900.0 229.1 %all-reduce.4.cloned.1.call-start = ((), (), s32[]{:S(2)}) async-start(), calls=%async_computation.11 | async-start | bytes 655360 | tf_op jit(solution)/shard_map/psum | solution.py:1021
  900.0 57.1 %collective-permute-start.88 = (bf16[1,4,160,640]{3,2,1,0:T(8,128)(2,1)}, bf16[1,4,160,640]{3,2,1,0:T(8,128)(2,1)}, u32[]{:S(2)}, u32[]{:S(2)}) collective-permute-start(bf16[1,4,160,640]{3,2,1,0:T(8,128)(2,1)} %get-tuple-element.165), channel_id=1, source_target_pairs={{0,16},{4,20},{8,24},{12,28},{16,0},{20,4},{24,8},{28,12},{1,17},{... | collective-permute-start | bytes 2457608 | tf_op jit(solution)/shard_map/ppermute | solution.py:735
  901.4 58.7 %collective-permute-start.87 = (bf16[1,4,160,640]{3,2,1,0:T(8,128)(2,1)}, bf16[1,4,160,640]{3,2,1,0:T(8,128)(2,1)}, u32[]{:S(2)}, u32[]{:S(2)}) collective-permute-start(bf16[1,4,160,640]{3,2,1,0:T(8,128)(2,1)} %get-tuple-element.164), channel_id=1, source_target_pairs={{0,8},{4,12},{8,0},{12,4},{16,24},{20,28},{24,16},{28,20},{1,9},{5... | collective-permute-start | bytes 2457608 | tf_op jit(solution)/shard_map/ppermute | solution.py:735
  916.5 113.7 %collective-permute-start.89 = (bf16[4,1280,640]{2,1,0:T(8,128)(2,1)}, bf16[4,1280,640]{2,1,0:T(8,128)(2,1)}, u32[]{:S(2)}, u32[]{:S(2)}) collective-permute-start(bf16[4,1280,640]{2,1,0:T(8,128)(2,1)} %weight_grad.22), channel_id=1, source_target_pairs={{0,4},{4,0},{8,12},{12,8},{16,20},{20,16},{24,28},{28,24},{1,5},{5... | collective-permute-start | bytes 19660808 | tf_op jit(solution)/shard_map/ppermute | solution.py:735
  959.9 53.4 %collective-permute-start.94 = (bf16[1,4,320,640]{3,2,1,0:T(8,128)(2,1)}, bf16[1,4,320,640]{3,2,1,0:T(8,128)(2,1)S(1)}, u32[]{:S(2)}, u32[]{:S(2)}) collective-permute-start(bf16[1,4,320,640]{3,2,1,0:T(8,128)(2,1)} %pad_maximum_fusion.5), channel_id=1, source_target_pairs={{0,8},{4,12},{8,0},{12,4},{16,24},{20,28},{24,16},{28,20},{1,9},{5... | collective-permute-start | bytes 4915208 | tf_op jit(solution)/shard_map/ppermute | solution.py:735
  963.2 51.2 %collective-permute-start.95 = (bf16[1,4,320,640]{3,2,1,0:T(8,128)(2,1)}, bf16[1,4,320,640]{3,2,1,0:T(8,128)(2,1)}, u32[]{:S(2)}, u32[]{:S(2)}) collective-permute-start(bf16[1,4,320,640]{3,2,1,0:T(8,128)(2,1)} %pad_maximum_fusion.6), channel_id=1, source_target_pairs={{0,16},{4,20},{8,24},{12,28},{16,0},{20,4},{24,8},{28,12},{1,17},{... | collective-permute-start | bytes 4915208 | tf_op jit(solution)/shard_map/ppermute | solution.py:735
  1013.2 117.7 %reduce-scatter.10.cloned.1.call-start = ((), (), s32[]{:S(2)}) async-start(), calls=%async_computation.9 | async-start | bytes 2048000 | tf_op jit(solution)/shard_map/reduce_scatter | solution.py:977
  1018.9 129.4 %reduce-scatter.8.cloned.1.call-start = ((), (), s32[]{:S(2)}) async-start(), calls=%async_computation.8 | async-start | bytes 2048000 | tf_op jit(solution)/shard_map/reduce_scatter | solution.py:977
  1062.8 52.0 %collective-permute-start.81 = (bf16[4,32,2560]{2,1,0:T(8,128)(2,1)S(1)}, bf16[4,32,2560]{2,1,0:T(8,128)(2,1)S(1)}, u32[]{:S(2)}, u32[]{:S(2)}) collective-permute-start(bf16[4,32,2560]{2,1,0:T(8,128)(2,1)S(1)} %get-tuple-element.206), channel_id=1, source_target_pairs={{0,4},{4,0},{8,12},{12,8},{16,20},{20,16},{24,28},{28,24},{1,5},{5... | collective-permute-start | bytes 1966088 | tf_op jit(solution)/shard_map/ppermute | solution.py:735
  (164 other events, 2801.2 us)
Sparse Core Ops, SparseCore 0:
  9.6 41.0 all-gather.12
  52.3 37.0 all-gather.14
  91.0 36.9 all-gather.16
  130.3 45.6 all-gather.8
  285.0 124.0 all-gather.10
  837.2 33.6 reduce-scatter.13
  875.3 49.1 reduce-scatter.11
  926.9 100.6 reduce-scatter.5
  1030.0 36.6 all-reduce.3
  1069.0 36.0 reduce-scatter.9
  1111.4 36.7 reduce-scatter.7
